TPU v7x, 32 devices: a whole 2x2x4 slice. The times are simulated.
32 devices in a mesh: dp: 8 (over z, x), mp: 4 (over y, core).
Axes of the slice: x: 2, y: 2, z: 4, core: 2. Of those that a mesh axis runs over, the one named last changes fastest.
Arguments:
- inputs: bfloat16 [41472, 512], P(('dp', 'mp')), may hold values from -6 to 6
- counts: int32 [128], P('dp'), may hold values from 100 to 324, as said below
- input_norm_gain: float32 [512], replicated, may hold values from 0.5 to 1.5
- shift_in: float32 [512], replicated, may hold values from -1.75 to 1.75
- w_value: float32 [512, 1536], P('dp', 'mp'), may hold values from -0.25 to 0.25
- w_gate: float32 [512, 1536], P('dp', 'mp'), may hold values from -0.25 to 0.25
- bias_value: float32 [1536], P('mp'), may hold values from -1.75 to 1.75
- bias_gate: float32 [1536], P('mp'), may hold values from -1.75 to 1.75
- gate_gain: float32 [1536], P('mp'), may hold values from 0.5 to 1.5
- gate_shift: float32 [1536], P('mp'), may hold values from -1.75 to 1.75
- spatial: float32 [324, 324], replicated, may hold values from -0.3125 to 0.3125
- spatial_bias: float32 [324], replicated, may hold values from 0.5 to 1.5
- w_out: float32 [1536, 512], P('mp', 'dp'), may hold values from -0.3125 to 0.3125
- out_bias: float32 [512], replicated, may hold values from -1.75 to 1.75
- cotangent: bfloat16 [41472, 512], P(('dp', 'mp')), may hold values from -6 to 6
Outputs:
- result: bfloat16 [41472, 512], P(('dp', 'mp'))
- input_grad: float32 [41472, 512], P(('dp', 'mp'))
- grad_gain_in: float32 [512], replicated
- grad_shift_in: float32 [512], replicated
- grad_w_value: float32 [512, 1536], P('dp', 'mp')
- grad_w_gate: float32 [512, 1536], P('dp', 'mp')
- grad_bias_value: float32 [1536], P('mp')
- grad_bias_gate: float32 [1536], P('mp')
- grad_gate_gain: float32 [1536], P('mp')
- grad_gate_shift: float32 [1536], P('mp')
- grad_spatial: float32 [324, 324], replicated
- grad_spatial_bias: float32 [324], replicated
- grad_w_out: float32 [1536, 512], P('mp', 'dp')
- grad_out_bias: float32 [512], replicated
Inputs may be any that keep to these rules, and one draw needn't show every extreme that they name: `counts`: each entry is 100, 196 or 324; rows of an image beyond its count are padding slots. Each aligned group of 16 images holds at least one image of 324 patches.
All inputs are finite; a program needn't handle non-finite values.
Results may differ from a plain program's by a relative error of at most 0.0098.
Values may be sent and summed in bfloat16 or wider, within the bound.
No kernel may reach another device: no remote copies, remote signals or barrier semaphores. Data moves between devices by JAX's collectives and lax.ppermute only.
A program may use at most 192 MiB of HBM per device.

v0:
```python
import jax
import jax.numpy as jnp
from jax import lax
from jax.sharding import PartitionSpec as P

GATE = 1536
MAXP = 324


EPS = 1e-05


def cut_along(array, dim, size):
    before, after = (array.shape[:dim], array.shape[dim + 1 :])
    return jnp.moveaxis(array.reshape(*before, size, -1, *after), dim, 0)


def sent_and_summed(array, axis, dim):
    size = lax.axis_size(axis)
    tiles = lax.all_to_all(cut_along(array, dim, size), axis, 0, 0, tiled=True)
    return jnp.sum(tiles.astype(jnp.float32), axis=0)


def in_one_piece(arrays, axis, dim, along):
    ends, at = ([], 0)
    for a in arrays[:-1]:
        at += a.shape[along]
        ends.append(at)
    both = jnp.concatenate(arrays, axis=along)
    return tuple(jnp.split(sent_and_summed(both, axis, dim), ends, axis=along))


def gelu_exact(values):
    return jax.nn.gelu(values, approximate=False)


def body(
    inputs,
    counts,
    input_norm_gain,
    shift_in,
    w_value,
    w_gate,
    bias_value,
    bias_gate,
    gate_gain,
    gate_shift,
    spatial,
    spatial_bias,
    w_out,
    out_bias,
    cotangent,
):
    image_count = counts.shape[0]
    chan_width = w_value.shape[1]
    input_f = inputs.astype(jnp.float32)
    centre = input_f - jnp.mean(input_f, -1, keepdims=True)
    inverse = lax.rsqrt(jnp.mean(centre * centre, -1, keepdims=True) + EPS)
    input_hat = centre * inverse
    normed = (input_hat * input_norm_gain + shift_in).astype(jnp.bfloat16)
    value_w, gate_w, out_w = (
        lax.all_gather(w_value.astype(jnp.bfloat16), "dp", axis=0, tiled=True),
        lax.all_gather(w_gate.astype(jnp.bfloat16), "dp", axis=0, tiled=True),
        lax.all_gather(w_out.astype(jnp.bfloat16), "dp", axis=1, tiled=True),
    )
    joined_w = jnp.concatenate([value_w, gate_w], 1)
    gathered = lax.all_gather(normed, "mp", axis=0, tiled=True)
    hidden_pre = jnp.dot(gathered, joined_w, preferred_element_type=jnp.float32) + jnp.concatenate(
        [bias_value, bias_gate]
    )
    value_act, value_pull = jax.vjp(gelu_exact, hidden_pre[:, :chan_width])
    gate_act, gate_pull = jax.vjp(gelu_exact, hidden_pre[:, chan_width:])
    gate_sum_total = lax.psum(jnp.sum(gate_act, -1, keepdims=True), "mp")
    gate_cen = gate_act - gate_sum_total / GATE
    square_total = lax.psum(jnp.sum(gate_cen * gate_cen, -1, keepdims=True), "mp")
    gate_var = square_total / GATE
    gate_inv = lax.rsqrt(gate_var + EPS)
    gate_hat = gate_cen * gate_inv
    positions = jnp.arange(MAXP, dtype=jnp.int32)
    live_mask = (positions[None, :] < counts[:, None])[:, :, None]
    live_low = live_mask.astype(jnp.bfloat16)
    live_float = live_mask.astype(jnp.float32)
    gate_rows = (gate_hat * gate_gain + gate_shift).astype(jnp.bfloat16).reshape(
        image_count, MAXP, chan_width
    ) * live_low
    spatial_low = spatial.astype(jnp.bfloat16)
    mixed_rows = jnp.einsum(
        "rc,bcf->brf", spatial_low, gate_rows, preferred_element_type=jnp.float32
    )
    shifted_output = ((mixed_rows + spatial_bias[None, :, None]) * live_float).reshape(
        image_count * MAXP, chan_width
    )
    product = (value_act * shifted_output).astype(jnp.bfloat16)
    slab_rows = product
    branch_sum = lax.psum_scatter(
        jnp.dot(slab_rows, out_w, preferred_element_type=jnp.float32).astype(jnp.bfloat16),
        "mp",
        scatter_dimension=0,
        tiled=True,
    ).astype(jnp.float32)
    result = (input_f + branch_sum + out_bias).astype(jnp.bfloat16)
    tangent_f = cotangent.astype(jnp.float32)
    tangent_all = lax.all_gather(cotangent, "mp", axis=0, tiled=True)
    grad_w_out = lax.dot_general(
        product, tangent_all, (((0,), (0,)), ((), ())), preferred_element_type=jnp.float32
    )
    d_product = lax.dot_general(
        tangent_all, out_w, (((1,), (1,)), ((), ())), preferred_element_type=jnp.float32
    )
    d_shift = (d_product * value_act).astype(jnp.bfloat16).reshape(
        image_count, MAXP, chan_width
    ) * live_low
    d_value = d_product * shifted_output
    grad_spatial = jnp.einsum("brf,bcf->rc", d_shift, gate_rows, preferred_element_type=jnp.float32)
    grad_spatial_bias = jnp.sum(d_shift.astype(jnp.float32), (0, 2))
    d_gate_rows = (
        jnp.einsum("rc,brf->bcf", spatial_low, d_shift, preferred_element_type=jnp.float32)
        * live_float
    )
    d_gate_rows = d_gate_rows.reshape(image_count * MAXP, chan_width)
    grad_gate_gain = jnp.sum(d_gate_rows * gate_hat, 0)
    grad_gate_shift = jnp.sum(d_gate_rows, 0)
    d_hat = d_gate_rows * gate_gain
    hat_total, cross_product_sum = (
        lax.psum(jnp.sum(d_hat, -1, keepdims=True).astype(jnp.bfloat16), "mp").astype(jnp.float32),
        lax.psum(jnp.sum(d_hat * gate_hat, -1, keepdims=True).astype(jnp.bfloat16), "mp").astype(
            jnp.float32
        ),
    )
    d_gate = gate_inv * (d_hat - hat_total / GATE - gate_hat * cross_product_sum / GATE)
    d_pre_value = value_pull(d_value)[0].astype(jnp.bfloat16)
    d_pre_gate = gate_pull(d_gate)[0].astype(jnp.bfloat16)
    d_joined = jnp.concatenate([d_pre_value, d_pre_gate], 1)
    grad_bias_value = jnp.sum(d_pre_value.astype(jnp.float32), 0)
    grad_bias_gate = jnp.sum(d_pre_gate.astype(jnp.float32), 0)
    rows_back = lax.all_gather(normed, "mp", axis=0, tiled=True)
    grad_joined = lax.dot_general(
        rows_back, d_joined, (((0,), (0,)), ((), ())), preferred_element_type=jnp.float32
    )
    slab_rows = d_joined
    normed_gradient = lax.psum_scatter(
        lax.dot_general(
            slab_rows, joined_w, (((1,), (1,)), ((), ())), preferred_element_type=jnp.float32
        ).astype(jnp.bfloat16),
        "mp",
        scatter_dimension=0,
        tiled=True,
    ).astype(jnp.float32)
    grad_gain_part = jnp.sum(normed_gradient * input_hat, 0)
    grad_shift_part = jnp.sum(normed_gradient, 0)
    input_hat_gradient = normed_gradient * input_norm_gain
    input_grad = tangent_f + inverse * (
        input_hat_gradient
        - jnp.mean(input_hat_gradient, -1, keepdims=True)
        - input_hat * jnp.mean(input_hat_gradient * input_hat, -1, keepdims=True)
    )
    grad_w_value, grad_w_gate, grad_w_out = (
        *in_one_piece(
            (
                grad_joined[:, :chan_width].astype(jnp.bfloat16),
                grad_joined[:, chan_width:].astype(jnp.bfloat16),
            ),
            "dp",
            0,
            1,
        ),
        sent_and_summed(grad_w_out.astype(jnp.bfloat16), "dp", 1),
    )
    grad_bias_value, grad_bias_gate, grad_gate_gain, grad_gate_shift = lax.psum(
        (grad_bias_value, grad_bias_gate, grad_gate_gain, grad_gate_shift), "dp"
    )
    grad_spatial, grad_spatial_bias, grad_gain_in, grad_shift_in, grad_out_bias = lax.psum(
        (grad_spatial, grad_spatial_bias, grad_gain_part, grad_shift_part, jnp.sum(tangent_f, 0)),
        ("dp", "mp"),
    )
    return (
        result,
        input_grad,
        grad_gain_in,
        grad_shift_in,
        grad_w_value,
        grad_w_gate,
        grad_bias_value,
        grad_bias_gate,
        grad_gate_gain,
        grad_gate_shift,
        grad_spatial,
        grad_spatial_bias,
        grad_w_out,
        grad_out_bias,
    )


def solution(mesh):
    placed = (
        P(("dp", "mp"), None),
        P("dp"),
        P(),
        P(),
        P("dp", "mp"),
        P("dp", "mp"),
        P("mp"),
        P("mp"),
        P("mp"),
        P("mp"),
        P(),
        P(),
        P("mp", "dp"),
        P(),
        P(("dp", "mp"), None),
    )
    return jax.shard_map(
        body,
        mesh=mesh,
        in_specs=placed,
        out_specs=(
            P(("dp", "mp"), None),
            P(("dp", "mp"), None),
            P(),
            P(),
            P("dp", "mp"),
            P("dp", "mp"),
            P("mp"),
            P("mp"),
            P("mp"),
            P("mp"),
            P(),
            P(),
            P("mp", "dp"),
            P(),
        ),
        check_vma=False,
    )
```

profile of v0, /device:TPU:0, one launch (start us, length us, event | category | flops | bytes accessed | tf_op | source)
XLA Modules:
  0.0 537.9 jit_solution(6720295963130620473)
XLA Ops:
  7.3 1.7 convert_reduce_fusion.4
  9.0 1.9 fusion.32
  11.0 0.6 copy-done.8
  11.5 2.9 fusion.29
  14.6 0.7 all-gather.5.cloned.1.call-update
  15.3 33.0 %all_gather.17 = bf16[512,384]{1,0:T(8,128)(2,1)S(1)} all-gather(bf16[64,384]{1,0:T(8,128)(2,1)S(1)} %convert_element_type.128), channel_id=1, replica_groups=mesh['dp'=8,'mp'=4] {'dp'}, dimensions={0}, use_global_device_ids=true | all-gather | bytes 442368 | tf_op jit(solution)/shard_map/all_gather | solution.py:62
  48.4 31.3 %all_gather.18 = bf16[512,384]{1,0:T(8,128)(2,1)S(1)} all-gather(bf16[64,384]{1,0:T(8,128)(2,1)S(1)} %convert_element_type.129), channel_id=1, replica_groups=mesh['dp'=8,'mp'=4] {'dp'}, dimensions={0}, use_global_device_ids=true | all-gather | bytes 442368 | tf_op jit(solution)/shard_map/all_gather | solution.py:63
  79.9 31.0 %all_gather.19 = bf16[384,512]{0,1:T(8,128)(2,1)S(1)} all-gather(bf16[384,64]{0,1:T(8,128)(2,1)S(1)} %convert_element_type.135), channel_id=1, replica_groups=mesh['dp'=8,'mp'=4] {'dp'}, dimensions={1}, use_global_device_ids=true | all-gather | bytes 442368 | tf_op jit(solution)/shard_map/all_gather | solution.py:64
  111.0 6.2 %convolution_add_fusion = f32[5184,768]{1,0:T(8,128)S(1)} fusion(bf16[5184,512]{1,0:T(8,128)(2,1)} %all-gather.3.cloned.1.call-done, bf16[512,768]{1,0:T(8,128)(2,1)S(1)} %constant_dynamic-update-slice_fusion, f32[768]{0:T(1024)S(1)} %pad_maximum_fusion.5), kind=kOutput, calls=%fused_computation.2 | convolution fusion | flops 4080844800 | bytes 22023168 | tf_op jit(solution)/shard_map/dot_general | solution.py:68
  117.3 19.7 %fusion.49 = (f32[5184]{0:T(1024)S(1)}, f32[5184,384]{1,0:T(8,128)}, f32[5184,384]{1,0:T(8,128)}) fusion(f32[5184,768]{1,0:T(8,128)S(1)} %convolution_add_fusion), kind=kLoop, calls=%fused_computation.111 | loop fusion | flops 129387456 | bytes 23908608 | tf_op jit(solution)/shard_map/reduce_sum | solution.py:73
  137.0 10.3 %psum.91 = f32[5184,1]{0,1:T(1,128)S(1)} all-reduce(f32[5184,1]{0,1:T(1,128)S(1)} %broadcast_in_dim.4), channel_id=1, replica_groups=mesh['dp'=8,'mp'=4] {'mp'}, use_global_device_ids=true, to_apply=%region_3.0 | all-reduce | flops 5184 | bytes 41472 | tf_op jit(solution)/shard_map/psum | solution.py:73
  147.3 4.8 multiply_reduce_fusion.3
  152.2 11.2 %psum.92 = f32[5184,1]{0,1:T(1,128)S(1)} all-reduce(f32[5184,1]{0,1:T(1,128)S(1)} %broadcast_in_dim.5), channel_id=1, replica_groups=mesh['dp'=8,'mp'=4] {'mp'}, use_global_device_ids=true, to_apply=%region_5.0 | all-reduce | flops 5184 | bytes 41472 | tf_op jit(solution)/shard_map/psum | solution.py:75
  163.5 8.8 %broadcast_multiply_fusion = (bf16[5184,384]{1,0:T(8,128)(2,1)}, bf16[5184,384]{1,0:T(8,128)(2,1)}) fusion(bf16[5184]{0:T(1024)(128)(2,1)S(1)} %reshape.163, f32[384]{0:T(512)S(1)} %copy-done.18, f32[384]{0:T(512)S(1)} %copy-done.13, f32[5184]{0:T(1024)S(1)} %rsqrt_reduce_fusion, f32[5184,384]{1,0:T(8,128)} %get-tuple-element.43, ...), kind=kLoop, calls=%fused_computation.85 | loop fusion | flops 11943936 | bytes 15980160 | tf_op jit(solution)/shard_map/mul | solution.py:83
  172.3 4.9 reshape.156
  177.2 6.5 %multiply_bitcast_fusion = f32[16,324,384]{2,1,0:T(8,128)} fusion(f32[16,324]{1,0:T(8,128)S(1)} %get-tuple-element.52, f32[324]{0:T(512)S(1)} %copy-done.21, bf16[16,324,384]{2,1,0:T(8,128)(2,1)} %reshape.156, bf16[16,324]{1,0:T(8,128)(2,1)S(1)} %get-tuple-element.51, f32[324,324]{1,0:T(8,128)S(1)} %copy-done.20), kind=kOutput, calls=%fused_computation.6 | convolution fusion | flops 1296022016 | bytes 12396240 | tf_op jit(solution)/shard_map/rc,bcf->brf/dot_general | solution.py:87
  183.8 6.9 %reshape.157 = f32[5184,384]{1,0:T(8,128)} reshape(f32[16,324,384]{2,1,0:T(8,128)} %multiply_bitcast_fusion) | data formatting | bytes 15925248 | tf_op jit(solution)/shard_map/reshape | solution.py:90
  190.7 24.7 %convert_reduce_fusion.2 = (f32[384]{0:T(512)S(1)}, bf16[5184,384]{1,0:T(8,128)(2,1)}, f32[5184,384]{1,0:T(8,128)S(1)}, f32[5184,384]{1,0:T(8,128)}) fusion(f32[5184,384]{1,0:T(8,128)} %reshape.157, f32[5184,768]{1,0:T(8,128)} %copy-done, bf16[5184,512]{1,0:T(8,128)(2,1)} %all-gather.5.cloned.1.call-done, bf16[384,512]{0,1:T(8,128)(2,1)S(1)} %all_gather.19), kind=kOutput, calls=%fused_computation.13 | convolution fusion | flops 2187730432 | bytes 41534976 | tf_op jit(solution)/shard_map/dot_general | solution.py:107
  215.4 11.8 %convert_reduce_fusion = (f32[5184]{0:T(1024)S(1)}, bf16[5184,384]{1,0:T(8,128)(2,1)}, bf16[5184,384]{1,0:T(8,128)(2,1)}, bf16[5184,384]{1,0:T(8,128)(2,1)}) fusion(bf16[5184]{0:T(1024)(128)(2,1)S(1)} %reshape.163, f32[5184,384]{1,0:T(8,128)} %get-tuple-element.53, f32[5184,384]{1,0:T(8,128)S(1)} %get-tuple-element.36, f32[5184,768]{1,0:T(8,128)} %copy-done, ...), kind=kLoop, calls=%fused_computation.10 | loop fusion | flops 17910720 | bytes 43825536 | tf_op jit(solution)/shard_map/reduce_sum | solution.py:115
  227.1 4.8 reshape.158
  231.9 5.3 multiply_reduce_fusion.4
  237.3 4.0 multiply_reduce_fusion
  241.3 7.2 %reshape.159 = f32[5184,384]{1,0:T(8,128)} reshape(f32[16,324,384]{2,1,0:T(8,128)} %get-tuple-element.41) | data formatting | bytes 15925248 | tf_op jit(solution)/shard_map/reshape | solution.py:120
  248.5 8.8 %multiply_reduce_fusion.1 = (f32[384]{0:T(512)S(1)}, bf16[5184]{0:T(1024)(128)(2,1)S(1)}) fusion(f32[5184,384]{1,0:T(8,128)} %reshape.159, f32[5184,384]{1,0:T(8,128)} %get-tuple-element.43, f32[5184]{0:T(1024)S(1)} %rsqrt_reduce_fusion, f32[5184]{0:T(1024)S(1)} %multiply_reduce_fusion.6, f32[384]{0:T(512)S(1)} %copy-done.13), kind=kLoop, calls=%fused_computation.11 | loop fusion | flops 13929024 | bytes 15980160 | tf_op jit(solution)/shard_map/reduce_sum | solution.py:121
  257.3 0.1 convert_element_type.143
  257.4 11.0 %all-reduce.2 = (bf16[5184]{0:T(1024)(128)(2,1)S(1)}, bf16[5184,1]{0,1:T(2,128)(2,1)S(1)}) all-reduce(bf16[5184]{0:T(1024)(128)(2,1)S(1)} %get-tuple-element.15, bf16[5184,1]{0,1:T(2,128)(2,1)S(1)} %convert_element_type.143), channel_id=1, replica_groups=mesh['dp'=8,'mp'=4] {'mp'}, use_global_device_ids=true, to_apply=%region_10.0 | all-reduce | flops 10368 | bytes 41472 | tf_op jit(solution)/shard_map/psum | solution.py:126
  268.5 12.8 %convert_reduce_fusion.1 = (f32[384]{0:T(512)S(1)}, bf16[5184,384]{1,0:T(8,128)(2,1)S(1)}) fusion(f32[5184,384]{1,0:T(8,128)} %get-tuple-element.44, f32[5184]{0:T(1024)S(1)} %mul.251, f32[5184,384]{1,0:T(8,128)} %get-tuple-element.43, f32[5184]{0:T(1024)S(1)} %multiply_reduce_fusion.6, f32[5184]{0:T(1024)S(1)} %multiply_reduce_fusion.5, ...), kind=kLoop, calls=%fused_computation.12 | loop fusion | flops 47775360 | bytes 35917824 | tf_op jit(solution)/shard_map/reduce_sum | solution.py:135
  281.4 2.0 copy-done.4
  283.4 6.3 %convolution_convert_fusion = bf16[5184,512]{1,0:T(8,128)(2,1)} fusion(bf16[512,768]{1,0:T(8,128)(2,1)S(1)} %constant_dynamic-update-slice_fusion, bf16[5184,384]{1,0:T(8,128)(2,1)S(1)} %get-tuple-element.33, bf16[5184,384]{1,0:T(8,128)(2,1)S(1)} %copy-done.22), kind=kOutput, calls=%fused_computation.3 | convolution fusion | flops 4095442944 | bytes 14057472 | tf_op jit(solution)/shard_map/dot_general | solution.py:142
  289.7 6.9 %convolution_convert_fusion.1 = bf16[5184,512]{1,0:T(8,128)(2,1)} fusion(bf16[5184,384]{1,0:T(8,128)(2,1)} %get-tuple-element.45, bf16[384,512]{0,1:T(8,128)(2,1)S(1)} %all_gather.19), kind=kOutput, calls=%fused_computation.4 | convolution fusion | flops 2041085952 | bytes 9682944 | tf_op jit(solution)/shard_map/dot_general | solution.py:96
  296.6 7.6 %convolution_convert_fusion.2 = bf16[384,512]{1,0:T(8,128)(2,1)S(1)} fusion(bf16[5184,384]{1,0:T(8,128)(2,1)} %get-tuple-element.45, bf16[5184,512]{1,0:T(8,128)(2,1)} %all-gather.5.cloned.1.call-done), kind=kOutput, calls=%fused_computation.89 | convolution fusion | flops 2038628352 | bytes 9682944 | tf_op jit(solution)/shard_map/dot_general | solution.py:104
  304.2 0.9 copy.33
  305.1 5.6 %all-to-all-start.1 = ((bf16[8,384,64]{1,2,0:T(8,128)(2,1)}), bf16[8,384,64]{1,2,0:T(8,128)(2,1)S(1)}, u32[]{:S(2)}, u32[]{:S(2)}) async-start(bf16[8,384,64]{1,2,0:T(8,128)(2,1)} %bitcast.7), calls=%async_computation.3 | async-start | bytes 786432 | tf_op jit(solution)/shard_map/all_to_all | solution.py:20
  310.8 10.2 %fusion.39 = bf16[512,768]{1,0:T(8,128)(2,1)} fusion(bf16[5184,512]{1,0:T(8,128)(2,1)} %all-gather.3.cloned.1.call-done, bf16[5184,384]{1,0:T(8,128)(2,1)} %copy-done.4, bf16[5184,384]{1,0:T(8,128)(2,1)} %get-tuple-element.35), kind=kOutput, calls=%fused_computation.88 | convolution fusion | flops 4093181952 | bytes 14057472 | tf_op jit(solution)/shard_map/dot_general | solution.py:137
  321.0 0.7 all-to-all-done.1
  321.6 5.3 all-to-all-start
  327.1 4.9 mul.270
  332.0 4.9 mul.272
  337.0 6.6 %convolution_bitcast_fusion = f32[324,324]{1,0:T(8,128)} fusion(bf16[16,324,384]{2,1,0:T(8,128)(2,1)} %mul.270, bf16[16,324,384]{2,1,0:T(8,128)(2,1)} %mul.272), kind=kOutput, calls=%fused_computation.90 | convolution fusion | flops 1289945088 | bytes 8382528 | tf_op jit(solution)/shard_map/brf,bcf->rc/dot_general | solution.py:114
  343.5 22.6 %all-reduce.1 = (f32[384]{0:T(512)}, f32[384]{0:T(512)}, f32[384]{0:T(512)}, f32[384]{0:T(512)}) all-reduce(f32[384]{0:T(512)S(1)} %get-tuple-element.34, f32[384]{0:T(512)S(1)} %get-tuple-element.32, f32[384]{0:T(512)S(1)} %get-tuple-element.14, f32[384]{0:T(512)S(1)} %get-tuple-element.54), channel_id=1, replica_groups=mesh['dp'=8,'mp'=4] {'dp'}, use_global_device_ids=true, to_apply=%region_20.0 | all-reduce | flops 1536 | bytes 12288 | tf_op jit(solution)/shard_map/psum | solution.py:169
  366.1 1.7 convert_reduce_fusion.7
  367.9 0.7 fusion.52
  368.6 2.8 fusion.36
  371.5 24.5 %reduce-scatter.3.cloned.1.call-done = bf16[1296,512]{1,0:T(8,128)(2,1)} async-done(((bf16[5184,512]{1,0:T(8,128)(2,1)}), bf16[1296,512]{1,0:T(8,128)(2,1)}) %reduce-scatter.3.cloned.1.call-update) | async-done | bytes 1327120 | tf_op jit(solution)/shard_map/reduce_scatter | solution.py:95
  396.0 4.2 convert_reduce_fusion.5
  400.2 39.5 %all-reduce = (f32[512]{0:T(512)}, f32[512]{0:T(512)}, f32[324]{0:T(512)}, f32[512]{0:T(512)}) all-reduce(f32[512]{0:T(512)S(1)} %get-tuple-element.16, f32[512]{0:T(512)S(1)} %get-tuple-element.19, f32[324]{0:T(512)S(1)} %reduce_sum.186, f32[512]{0:T(512)S(1)} %get-tuple-element.46), channel_id=1, replica_groups=mesh['dp'=8,'mp'=4] {'dp','mp'}, use_global_device_ids=true, to_apply=%region_15.0 | all-reduce | flops 1860 | bytes 14880 | tf_op jit(solution)/shard_map/psum | solution.py:172
  439.7 89.4 %all-reduce.5.cloned.1.call-done = f32[324,324]{1,0:T(8,128)} async-done(((f32[324,324]{1,0:T(8,128)}), f32[324,324]{1,0:T(8,128)}) %all-reduce.5.cloned.1.call-update) | async-done | bytes 419920 | tf_op jit(solution)/shard_map/psum | solution.py:172
  529.1 1.8 copy.38
  (77 shorter events, 1.2 us)
Async XLA Ops:
  7.2 8.1 %copy-start.10 = (f32[64,384]{1,0:T(8,128)S(1)}, f32[64,384]{1,0:T(8,128)}, u32[]{:S(2)}) copy-start(f32[64,384]{1,0:T(8,128)} %param.19) | copy-start | bytes 294916
  7.2 41.2 %copy-start.11 = (f32[64,384]{1,0:T(8,128)S(1)}, f32[64,384]{1,0:T(8,128)}, u32[]{:S(2)}) copy-start(f32[64,384]{1,0:T(8,128)} %param.20) | copy-start | bytes 294916
  7.2 72.5 %copy-start.19 = (s32[16]{0:T(128)S(1)}, s32[16]{0:T(128)}, u32[]{:S(2)}) copy-start(s32[16]{0:T(128)} %param.16) | copy-start | bytes 196
  7.2 72.7 %copy-start.12 = (f32[384,64]{0,1:T(8,128)S(1)}, f32[384,64]{0,1:T(8,128)}, u32[]{:S(2)}) copy-start(f32[384,64]{0,1:T(8,128)} %param.27) | copy-start | bytes 294916
  7.2 103.7 %copy-start.16 = (f32[384]{0:T(512)S(1)}, f32[384]{0:T(512)}, u32[]{:S(2)}) copy-start(f32[384]{0:T(512)} %param.22) | copy-start | bytes 4612
  7.2 103.7 %copy-start.17 = (f32[384]{0:T(512)S(1)}, f32[384]{0:T(512)}, u32[]{:S(2)}) copy-start(f32[384]{0:T(512)} %param.21) | copy-start | bytes 4612
  7.2 103.8 %all-gather.3.cloned.1.call-start = ((), (), s32[]{:S(2)}) async-start(), calls=%async_computation.4 | async-start | bytes 6635520 | tf_op jit(solution)/shard_map/all_gather | solution.py:67
  9.0 2.0 copy-start.6
  10.9 0.6 copy-start.8
  14.5 176.2 %all-gather.5.cloned.1.call-start = ((), (), s32[]{:S(2)}) async-start(), calls=%async_computation.6 | async-start | bytes 6635520 | tf_op jit(solution)/shard_map/all_gather | solution.py:103
  15.3 353.4 %reduce-scatter.5.cloned.1.call-start = ((), (), s32[]{:S(2)}) async-start(), calls=%async_computation.7 | async-start | bytes 6635520 | tf_op jit(solution)/shard_map/reduce_scatter | solution.py:141
  117.3 19.7 %copy-start = (f32[5184,768]{1,0:T(8,128)}, f32[5184,768]{1,0:T(8,128)S(1)}, u32[]{:S(2)}) copy-start(f32[5184,768]{1,0:T(8,128)S(1)} %convolution_add_fusion) | copy-start | bytes 47775748
  137.0 26.5 %copy-start.13 = (f32[384]{0:T(512)S(1)}, f32[384]{0:T(512)}, u32[]{:S(2)}) copy-start(f32[384]{0:T(512)} %param.23) | copy-start | bytes 4612
  137.0 26.5 %copy-start.18 = (f32[384]{0:T(512)S(1)}, f32[384]{0:T(512)}, u32[]{:S(2)}) copy-start(f32[384]{0:T(512)} %param.24) | copy-start | bytes 4612
  172.3 4.9 copy-start.20
  172.3 4.9 copy-start.21
  190.7 24.7 %copy-start.2 = (f32[5184,384]{1,0:T(8,128)S(1)}, f32[5184,384]{1,0:T(8,128)}, u32[]{:S(2)}) copy-start(f32[5184,384]{1,0:T(8,128)} %reshape.157) | copy-start | bytes 23887876
  268.5 14.9 %copy-start.22 = (bf16[5184,384]{1,0:T(8,128)(2,1)S(1)}, bf16[5184,384]{1,0:T(8,128)(2,1)}, u32[]{:S(2)}) copy-start(bf16[5184,384]{1,0:T(8,128)(2,1)} %get-tuple-element.35) | copy-start | bytes 11943940
  281.4 2.0 copy-start.4
  289.7 106.3 %reduce-scatter.3.cloned.1.call-start = ((), (), s32[]{:S(2)}) async-start(), calls=%async_computation.5 | async-start | bytes 6635520 | tf_op jit(solution)/shard_map/reduce_scatter | solution.py:95
  305.1 16.5 %all-to-all-start.1 = ((bf16[8,384,64]{1,2,0:T(8,128)(2,1)}), bf16[8,384,64]{1,2,0:T(8,128)(2,1)S(1)}, u32[]{:S(2)}, u32[]{:S(2)}) async-start(bf16[8,384,64]{1,2,0:T(8,128)(2,1)} %bitcast.7), calls=%async_computation.3 | async-start | bytes 786432 | tf_op jit(solution)/shard_map/all_to_all | solution.py:20
  321.6 10.3 %copy-start.5 = (bf16[8,384,64]{1,2,0:T(8,128)(2,1)}, bf16[8,384,64]{1,2,0:T(8,128)(2,1)S(1)}, u32[]{:S(2)}) copy-start(bf16[8,384,64]{1,2,0:T(8,128)(2,1)S(1)} %all-to-all-done.1) | copy-start | bytes 1179652
  321.6 46.2 %all-to-all-start = ((bf16[8,64,768]{2,1,0:T(8,128)(2,1)}), bf16[8,64,768]{2,1,0:T(8,128)(2,1)S(1)}, u32[]{:S(2)}, u32[]{:S(2)}) async-start(bf16[8,64,768]{2,1,0:T(8,128)(2,1)} %bitcast.4), calls=%async_computation.2 | async-start | bytes 1572864 | tf_op jit(solution)/shard_map/all_to_all | solution.py:20
  327.0 202.2 %all-reduce.5.cloned.1.call-start = ((), (), s32[]{:S(2)}) async-start(), calls=%async_computation.8 | async-start | bytes 1007616 | tf_op jit(solution)/shard_map/psum | solution.py:172
  336.9 31.7 %copy-start.1 = (bf16[1296,512]{1,0:T(8,128)(2,1)S(1)}, bf16[1296,512]{1,0:T(8,128)(2,1)}, u32[]{:S(2)}) copy-start(bf16[1296,512]{1,0:T(8,128)(2,1)} %param.15) | copy-start | bytes 3981316
  336.9 31.7 %copy-start.7 = (f32[1296]{0:T(1024)S(1)}, f32[1296]{0:T(1024)}, u32[]{:S(2)}) copy-start(f32[1296]{0:T(1024)} %copy-done.6) | copy-start | bytes 15556
  336.9 31.7 %copy-start.9 = (f32[1296]{0:T(1024)S(1)}, f32[1296]{0:T(1024)}, u32[]{:S(2)}) copy-start(f32[1296]{0:T(1024)} %copy-done.8) | copy-start | bytes 15556
  336.9 31.7 %copy-start.14 = (f32[512]{0:T(512)S(1)}, f32[512]{0:T(512)}, u32[]{:S(2)}) copy-start(f32[512]{0:T(512)} %param.17) | copy-start | bytes 6148
  336.9 59.0 %copy-start.3 = (bf16[1296,512]{1,0:T(8,128)(2,1)S(1)}, bf16[1296,512]{1,0:T(8,128)(2,1)}, u32[]{:S(2)}) copy-start(bf16[1296,512]{1,0:T(8,128)(2,1)} %param.29) | copy-start | bytes 3981316
  336.9 59.0 %copy-start.15 = (f32[512]{0:T(512)S(1)}, f32[512]{0:T(512)}, u32[]{:S(2)}) copy-start(f32[512]{0:T(512)} %param.28) | copy-start | bytes 6148
Sparse Core Ops, SparseCore 0:
  14.6 43.4 all-gather.2
  59.7 40.7 all-gather.4
  289.8 51.6 reduce-scatter.4
  344.1 51.8 reduce-scatter.2
  401.7 127.3 all-reduce.4
where the time goes:
time: 548 us; the launch traced here: 538 us
  blocking collectives  190 us (35%)
  waiting for transfers between devices  115 us (21%)
  other arithmetic  86.5 us (16%)
  matrix products  80.2 us (15%)
  local copies, waits for them, and re-layouts  40.2 us (7%)
  between operations  14.6 us (3%)
  starting transfers between devices  11.1 us (2%)
    psum x1, waiting for transfers between devices, body(): lax.psum((grad_spatial, grad_spatial_bias, grad_gain_part, grad_shift_par...  89.4 us
    psum x1, blocking collectives, body(): lax.psum((grad_spatial, grad_spatial_bias, grad_gain_part, grad_shift_par...  39.5 us
    all_gather x1, blocking collectives, body(): lax.all_gather(w_value.astype(jnp.bfloat16), 'dp', axis=0, tiled=True)  33 us
    all_gather x1, blocking collectives, body(): lax.all_gather(w_gate.astype(jnp.bfloat16), 'dp', axis=0, tiled=True)  31.3 us
    all_gather x1, blocking collectives, body(): lax.all_gather(w_out.astype(jnp.bfloat16), 'dp', axis=1, tiled=True)  31 us
    dot_general x1, matrix products, body(): lax.dot_general(tangent_all, out_w, (((1,), (1,)), ((), ())), preferred_e...  24.7 us
    reduce_scatter x1, waiting for transfers between devices, body(): lax.psum_scatter(jnp.dot(slab_rows, out_w, preferred_element_type=jnp.flo...  24.5 us
    psum x1, blocking collectives, body(): lax.psum((grad_bias_value, grad_bias_gate, grad_gate_gain, grad_gate_shif...  22.6 us
  transfers between devices with their start and end apart: 7, of which 3 were waited for; matrix products, arithmetic and copies ran while one was open for 20% of the time, Pallas kernels for 0%

commit v1 on v0

v1 whole, which is shorter than its diff:
```python
import jax, jax.numpy as jnp
from jax import lax
from jax.experimental import pallas as pl
from jax.experimental.pallas import tpu as pltpu
EPS=1e-5
BF=jnp.bfloat16; F32=jnp.float32
MAXP=324
WIN=336; STEP=320; CH=16
GELU_C=(7.97882133e-01,3.63449931e-02,-4.51808700e-05,-5.02619616e-05,3.08533547e-06,-6.58149666e-08)
LOG2E_HALF=-0.7213475204444817
INV_SQRT_2PI=0.3989422804014327

def gelu_both(x):
    u=x*x
    um=jnp.minimum(u,30.0)
    p=GELU_C[5]
    for c in GELU_C[4::-1]:
        p=p*um+c
    cdf=0.5+0.5*jnp.tanh(x*p)
    slope=cdf+(x*INV_SQRT_2PI)*jnp.exp2(u*LOG2E_HALF)
    return x*cdf, slope

def dot(a,b): return jnp.dot(a,b,preferred_element_type=F32)
def dot_tn(a,b): return lax.dot_general(a,b,(((0,),(0,)),((),())),preferred_element_type=F32)
def dot_nt(a,b): return lax.dot_general(a,b,(((1,),(1,)),((),())),preferred_element_type=F32)

def norm_kernel(x_ref,g_ref,gain_ref,shift_ref,n_ref,gs_ref):
    x=x_ref[...].astype(F32)
    cen=x-jnp.mean(x,-1,keepdims=True)
    inv=lax.rsqrt(jnp.mean(cen*cen,-1,keepdims=True)+EPS)
    n_ref[...]=(cen*inv*gain_ref[...]+shift_ref[...]).astype(BF)
    @pl.when(pl.program_id(0)==0)
    def _(): gs_ref[...]=jnp.zeros_like(gs_ref)
    gs_ref[...]+=jnp.sum(g_ref[...].astype(F32),0,keepdims=True)

def norm_call(x,g,gain,shift):
    rows,d=x.shape; t=rows//3
    row=pl.BlockSpec((t,d),lambda i:(i,0)); one=pl.BlockSpec((1,d),lambda i:(0,0))
    return pl.pallas_call(norm_kernel,grid=(3,),in_specs=[row,row,one,one],out_specs=[row,one],
        out_shape=[jax.ShapeDtypeStruct((rows,d),BF),jax.ShapeDtypeStruct((1,d),F32)],name="input_norm")(x,g,gain[None],shift[None])

def gate_kernel(n_ref,w_ref,b_ref,gain_ref,shift_ref,s_ref,sb_ref,rows_ref,hat_ref,slope_ref,inv_ref,shifted_ref,pre):
    width=w_ref.shape[1]
    pre[...]=dot(n_ref[...],w_ref[...])
    for r in range(0,WIN,CH):
        act,slope=gelu_both(pre[r:r+CH,:]+b_ref[...])
        slope_ref[0,r:r+CH,:]=slope.astype(BF)
        cen=act-jnp.sum(act,-1,keepdims=True)*(1.0/width)
        inv=lax.rsqrt(jnp.sum(cen*cen,-1,keepdims=True)*(1.0/width)+EPS)
        hat=cen*inv
        inv_ref[0,r:r+CH,:]=inv
        hat_ref[0,r:r+CH,:]=hat.astype(BF)
        rows_ref[0,r:r+CH,:]=(hat*gain_ref[...]+shift_ref[...]).astype(BF)
    shifted_ref[0]=(dot(s_ref[0],rows_ref[0])+sb_ref[0]).astype(BF)

def win_spec(d): return pl.BlockSpec((pl.Element(WIN),pl.Element(d)),lambda b:(b*STEP,0))
def img(*s): return pl.BlockSpec((1,)+s,lambda b:(b,)+(0,)*len(s))
def const(*s): return pl.BlockSpec(s,lambda b:(0,)*len(s))
def params(mb=56): return pltpu.CompilerParams(vmem_limit_bytes=mb*2**20)

def gate_call(normed,w,b,gain,shift,sm,sbias):
    n=sm.shape[0]; d=normed.shape[1]; c=w.shape[1]
    big=jax.ShapeDtypeStruct((n,WIN,c),BF)
    return pl.pallas_call(gate_kernel,grid=(n,),
        in_specs=[win_spec(d),const(d,c),const(1,c),const(1,c),const(1,c),img(WIN,WIN),img(WIN,1)],
        out_specs=[img(WIN,c)]*3+[img(WIN,1),img(WIN,c)],
        out_shape=[big,big,big,jax.ShapeDtypeStruct((n,WIN,1),F32),big],
        scratch_shapes=[pltpu.VMEM((WIN,c),F32)],compiler_params=params(),name="gate_forward")(normed,w,b[None],gain[None],shift[None],sm,sbias)

def value_kernel(n_ref,g_ref,wv_ref,wo_ref,b_ref,shifted_ref,prod_ref,dshift_ref,dpre_ref,ssum_ref,gwv_ref,gwo_ref,gb_ref,pre,dprod):
    @pl.when(pl.program_id(0)==0)
    def _():
        gwv_ref[...]=jnp.zeros_like(gwv_ref); gwo_ref[...]=jnp.zeros_like(gwo_ref); gb_ref[...]=jnp.zeros_like(gb_ref)
    pre[...]=dot(n_ref[...],wv_ref[...])
    dprod[...]=dot(g_ref[...],wo_ref[...])
    for r in range(0,WIN,CH):
        act,slope=gelu_both(pre[r:r+CH,:]+b_ref[...])
        sh=shifted_ref[0,r:r+CH,:].astype(F32)
        dp=dprod[r:r+CH,:]
        prod_ref[0,r:r+CH,:]=(act*sh).astype(BF)
        ds=dp*act
        dshift_ref[0,r:r+CH,:]=ds.astype(BF)
        ssum_ref[0,r:r+CH,:]=jnp.sum(ds,-1,keepdims=True)
        dv=dp*sh*slope
        dpre_ref[0,r:r+CH,:]=dv.astype(BF)
        gb_ref[...]+=dv[0:8]+dv[8:16]
    gwv_ref[...]+=dot_tn(n_ref[...],dpre_ref[0])
    gwo_ref[...]+=dot_tn(g_ref[...],prod_ref[0])

def value_call(normed,g,wv,wo,b,shifted):
    n=shifted.shape[0]; d=normed.shape[1]; c=wv.shape[1]
    big=jax.ShapeDtypeStruct((n,WIN,c),BF)
    gw=jax.ShapeDtypeStruct((d,c),F32)
    return pl.pallas_call(value_kernel,grid=(n,),
        in_specs=[win_spec(d),win_spec(d),const(d,c),const(d,c),const(1,c),img(WIN,c)],
        out_specs=[img(WIN,c)]*3+[img(WIN,1),const(d,c),const(d,c),const(8,c)],
        out_shape=[big,big,big,jax.ShapeDtypeStruct((n,WIN,1),F32),gw,gw,jax.ShapeDtypeStruct((8,c),F32)],
        scratch_shapes=[pltpu.VMEM((WIN,c),F32)]*2,compiler_params=params(),name="value_and_backward")(normed,g,wv,wo,b[None],shifted)

def back_kernel(n_ref,dshift_ref,rows_ref,hat_ref,slope_ref,inv_ref,st_ref,gain_ref,dpre_ref,gsp_ref,gwg_ref,gb_ref,gg_ref,gsh_ref,dgr):
    @pl.when(pl.program_id(0)==0)
    def _():
        for r in (gwg_ref,gb_ref,gg_ref,gsh_ref): r[...]=jnp.zeros_like(r)
    width=gain_ref.shape[1]
    dgr[...]=dot(st_ref[0],dshift_ref[0])
    gsp_ref[0]=dot_nt(dshift_ref[0],rows_ref[0])
    for r in range(0,WIN,CH):
        d=dgr[r:r+CH,:]
        hat=hat_ref[0,r:r+CH,:].astype(F32)
        dh=d*hat
        gg_ref[...]+=dh[0:8]+dh[8:16]
        gsh_ref[...]+=d[0:8]+d[8:16]
        dg=d*gain_ref[...]
        m1=jnp.sum(dg,-1,keepdims=True)*(1.0/width)
        m2=jnp.sum(dg*hat,-1,keepdims=True)*(1.0/width)
        dpg=(dg-m1-hat*m2)*inv_ref[0,r:r+CH,:]*slope_ref[0,r:r+CH,:].astype(F32)
        dpre_ref[0,r:r+CH,:]=dpg.astype(BF)
        gb_ref[...]+=dpg[0:8]+dpg[8:16]
    gwg_ref[...]+=dot_tn(n_ref[...],dpre_ref[0])

def back_call(normed,dshift,rows,hat,slope,inv,st,gain):
    n=dshift.shape[0]; d=normed.shape[1]; c=dshift.shape[2]
    v8=jax.ShapeDtypeStruct((8,c),F32)
    return pl.pallas_call(back_kernel,grid=(n,),
        in_specs=[win_spec(d)]+[img(WIN,c)]*4+[img(WIN,1),img(WIN,WIN),const(1,c)],
        out_specs=[img(WIN,c),img(WIN,WIN),const(d,c)]+[const(8,c)]*3,
        out_shape=[jax.ShapeDtypeStruct((n,WIN,c),BF),jax.ShapeDtypeStruct((n,WIN,WIN),F32),jax.ShapeDtypeStruct((d,c),F32),v8,v8,v8],
        scratch_shapes=[pltpu.VMEM((WIN,c),F32)],compiler_params=params(),name="gate_backward")(normed,dshift,rows,hat,slope,inv,st,gain[None])

def out_kernel(x_ref,g_ref,prod_ref,dpv_ref,dpg_ref,wv_ref,wg_ref,wo_ref,gain_ref,bias_ref,res_ref,ing_ref,gg_ref,gs_ref,carry_a,carry_b):
    i=pl.program_id(0)
    @pl.when(i==0)
    def _():
        carry_a[...]=jnp.zeros_like(carry_a); carry_b[...]=jnp.zeros_like(carry_b)
        gg_ref[...]=jnp.zeros_like(gg_ref); gs_ref[...]=jnp.zeros_like(gs_ref)
    start=pl.multiple_of(i*STEP,16)
    br=dot_nt(prod_ref[0],wo_ref[...])
    dn=dot_nt(dpv_ref[0],wv_ref[...])+dot_nt(dpg_ref[0],wg_ref[...])
    br=jnp.concatenate([br[:16]+carry_a[...],br[16:]],0)
    carry_a[...]=br[STEP:]
    dn=jnp.concatenate([dn[:16]+carry_b[...],dn[16:]],0)
    carry_b[...]=dn[STEP:]
    last=i==pl.num_programs(0)-1
    x=x_ref[...].astype(F32)
    res_ref[pl.ds(start,WIN),:]=(x+br+bias_ref[...]).astype(BF)
    cen=x-jnp.mean(x,-1,keepdims=True)
    inv=lax.rsqrt(jnp.mean(cen*cen,-1,keepdims=True)+EPS)
    hat=cen*inv
    keep=jnp.where(jnp.logical_or(last,lax.broadcasted_iota(jnp.int32,(WIN,1),0)<STEP),1.0,0.0)
    dk=dn*keep
    gg_ref[...]+=jnp.sum(dk*hat,0,keepdims=True)
    gs_ref[...]+=jnp.sum(dk,0,keepdims=True)
    dx=dn*gain_ref[...]
    m1=jnp.mean(dx,-1,keepdims=True); m2=jnp.mean(dx*hat,-1,keepdims=True)
    ing_ref[pl.ds(start,WIN),:]=g_ref[...].astype(F32)+inv*(dx-m1-hat*m2)

def out_call(x,g,prod,dpv,dpg,wv,wg,wo,gain,bias):
    n=prod.shape[0]; rows,d=x.shape; c=wv.shape[1]
    return pl.pallas_call(out_kernel,grid=(n,),
        in_specs=[win_spec(d),win_spec(d)]+[img(WIN,c)]*3+[const(d,c)]*3+[const(1,d)]*2,
        out_specs=[const(rows,d),const(rows,d),const(1,d),const(1,d)],
        out_shape=[jax.ShapeDtypeStruct((rows,d),BF),jax.ShapeDtypeStruct((rows,d),F32)]+[jax.ShapeDtypeStruct((1,d),F32)]*2,
        scratch_shapes=[pltpu.VMEM((16,d),F32)]*2,compiler_params=params(),name="outputs")(x,g,prod,dpv,dpg,wv,wg,wo,gain[None],bias[None])

def spatial_windows(spatial,sbias,counts):
    n=counts.shape[0]; p=spatial.shape[0]
    live=(jnp.arange(p,dtype=jnp.int32)[None]<counts[:,None])
    s=spatial.astype(BF)
    mats=[];cols=[]
    for b in range(n):
        off=b*p-b*STEP
        m=jnp.where(live[b][:,None]&live[b][None,:],s,0)
        mats.append(jnp.pad(m,((off,WIN-p-off),)*2))
        cols.append(jnp.pad(jnp.where(live[b],sbias,0.0),(off,WIN-p-off)))
    return jnp.stack(mats),jnp.stack(cols)[:,:,None]

from jax.sharding import PartitionSpec as P
ORDER=(0,2,1,3)

def swap(x,k):
    n=lax.axis_size("mp")
    return lax.ppermute(x,"mp",[(i,i^k) for i in range(n)])

def gather_dp(x):
    n=lax.axis_size("dp")
    return lax.all_to_all(jnp.broadcast_to(x[None],(n,)+x.shape),"dp",0,0,tiled=True)

def gather_weight(shard):
    t=gather_dp(shard); t=t.reshape(-1,shard.shape[1])
    own=jnp.concatenate([t,swap(t,2)],1)
    return own,swap(own,1)

def scatter_sum(own,other):
    n=lax.axis_size("dp"); c=own.shape[1]//2
    a=own.astype(F32)+swap(other,1).astype(F32)
    s=a[:,:c]+swap(a[:,c:].astype(BF),2).astype(F32)
    s=s.astype(BF).reshape(n,-1,c)
    return lax.all_to_all(s,"dp",0,0,tiled=True).astype(F32).sum(0)

def body(inputs,counts,input_norm_gain,shift_in,w_value,w_gate,bias_value,bias_gate,gate_gain,gate_shift,spatial,spatial_bias,w_out,out_bias,cotangent):
    me=lax.axis_index("mp"); n_mp=lax.axis_size("mp"); ndp=lax.axis_size("dp")
    c=w_value.shape[1]; d=inputs.shape[1]; p=spatial.shape[0]
    n=counts.shape[0]//n_mp
    counts=lax.dynamic_slice(counts,(me*n,),(n,))
    order=jnp.bitwise_xor(jnp.array(ORDER,jnp.int32),me)
    vecs=lax.all_gather(jnp.stack([bias_value,bias_gate,gate_gain,gate_shift]),"mp")
    vecs=jnp.take(vecs,order,axis=0)
    bv,bg,gg,gs=[vecs[:,k].reshape(-1) for k in range(4)]
    g_own,g_oth=gather_weight(w_gate.astype(BF))
    wg=jnp.concatenate([g_own,g_oth],1)
    vo=jnp.concatenate([w_value,w_out.T],1).astype(BF)
    t=gather_dp(vo).reshape(d,2*c)
    y=swap(t,2)
    own=jnp.concatenate([t[:,:c],y[:,:c],t[:,c:],y[:,c:]],1)
    oth=swap(own,1)
    wv=jnp.concatenate([own[:,:2*c],oth[:,:2*c]],1)
    wo=jnp.concatenate([own[:,2*c:],oth[:,2*c:]],1)

    sm,sb=spatial_windows(spatial,spatial_bias,counts)
    normed,gsum=norm_call(inputs,cotangent,input_norm_gain,shift_in)
    rows,hat,slope,inv,shifted=gate_call(normed,wg,bg,gg,gs,sm,sb)
    prod,dshift,dpv,ssum,gwv,gwo,gbv=value_call(normed,cotangent,wv,wo,bv,shifted)
    gwv=gwv.astype(BF); gwo=gwo.astype(BF)
    w=2*c
    def inter(a,b): return jnp.concatenate([a[:,:c],b[:,:c],a[:,c:],b[:,c:]],1)
    vo_sum=scatter_sum(inter(gwv[:,:w],gwo[:,:w]),inter(gwv[:,w:],gwo[:,w:]))
    dpg,gsp,gwg,gbg,ggain,gshift=back_call(normed,dshift,rows,hat,slope,inv,jnp.swapaxes(sm,1,2),gg)
    gwg=gwg.astype(BF)
    live=(jnp.arange(p,dtype=jnp.int32)[None]<counts[:,None]).astype(F32)
    gspat=0; gsb=0
    for b in range(n):
        off=b*p-b*STEP
        gspat+=gsp[b,off:off+p,off:off+p]*live[b][:,None]*live[b][None]
        gsb+=ssum[b,off:off+p,0]*live[b]
    e=-(-p*p//(d*n_mp*8))*8
    sp=jnp.pad(gspat.reshape(-1).astype(BF),(0,d*n_mp*e-p*p)).reshape(n_mp,d,e)
    sp=jnp.take(sp,order,axis=0)
    own=jnp.concatenate([gwg[:,:c],sp[0],gwg[:,c:w],sp[1]],1)
    oth=jnp.concatenate([gwg[:,w:w+c],sp[2],gwg[:,w+c:],sp[3]],1)
    gs_sum=scatter_sum(own,oth)
    res,ing,gin,sin=out_call(inputs,cotangent,prod,dpv,dpg,wv,wg,wo,input_norm_gain,out_bias)
    sums=jnp.concatenate([gbv.sum(0),gbg.sum(0),ggain.sum(0),gshift.sum(0)]).reshape(4,n_mp,c)
    sums=jnp.take(sums,jnp.argsort(order),axis=1).reshape(-1)
    sums=jnp.concatenate([sums,gsb,gin[0],sin[0],gsum[0]])
    part=gs_sum[:,c:].reshape(-1)
    m=sums.shape[0]
    both=gather_dp(jnp.concatenate([sums,part]))
    sums=both[:,:m].sum(0); part=both[:,m:].reshape(1,d,e)
    r=swap(jnp.concatenate([sums,part.reshape(-1)]),2)
    sums=sums+r[:m]; part=jnp.concatenate([part,r[m:].reshape(1,d,e)],0)
    r=swap(jnp.concatenate([sums,part.reshape(-1)]),1)
    sums=sums+r[:m]; part=jnp.concatenate([part,r[m:].reshape(2,d,e)],0)
    part=jnp.take(part,jnp.argsort(order),axis=0).reshape(-1)[:p*p].reshape(p,p)
    four=lax.dynamic_index_in_dim(sums[:4*n_mp*c].reshape(4,n_mp,c),me,1,keepdims=False)
    k=4*n_mp*c
    return (res,ing,sums[k+p:k+p+d],sums[k+p+d:k+p+2*d],vo_sum[:,:c],gs_sum[:,:c],four[0],four[1],four[2],four[3],part,sums[k:k+p],vo_sum[:,c:].T,sums[k+p+2*d:])

def solution(mesh):
    row=P(("dp","mp"),None); wi=P("dp","mp"); mp=P("mp"); al=P()
    return jax.shard_map(body,mesh=mesh,
        in_specs=(row,P("dp"),al,al,wi,wi,mp,mp,mp,mp,al,al,P("mp","dp"),al,row),
        out_specs=(row,row,al,al,wi,wi,mp,mp,mp,mp,al,al,P("mp","dp"),al),check_vma=False)
```

time: 548 us -> 262 us (0.48); the launches traced: 538 us -> 261 us
  blocking collectives: 190 us -> 5.37 us
  matrix products: 80.2 us -> 0 us
  Pallas kernels: 0 us -> 70.6 us
  other arithmetic: 86.5 us -> 27.7 us
  waiting for transfers between devices: 115 us -> 66.8 us
  starting transfers between devices: 11.1 us -> 37 us
  between operations: 14.6 us -> 1.54 us
  local copies, waits for them, and re-layouts: 40.2 us -> 52 us
    psum x5 -> x0, blocking collectives: 94.6 us -> none  [the longest x1 39.5 us: body(): lax.psum((grad_spatial, grad_spatial_bias, grad_gain_part, grad_shift_par...]
    all_gather x3 -> x1, blocking collectives: 95.3 us -> 5.37 us  [body(): lax.all_gather(jnp.stack([bias_value, bias_gate, gate_gain, gate_shift]),...]
    psum x1 -> x0, waiting for transfers between devices: 89.4 us -> none  [body(): lax.psum((grad_spatial, grad_spatial_bias, grad_gain_part, grad_shift_par...]
    dot_general x9 -> x0, matrix products: 80.2 us -> none  [the longest x1 24.7 us: body(): lax.dot_general(tangent_all, out_w, (((1,), (1,)), ((), ())), preferred_e...]
    reduce_sum x13 -> x7, other arithmetic: 74.4 us -> 0.33 us  [the longest x2 0.18 us: scatter_sum(): return lax.all_to_all(s, 'dp', 0, 0, tiled=True).astype(F32).sum(0)]
    pallas_call x0 -> x5, Pallas kernels: none -> 70.6 us  [the longest x1 22.4 us: value_call(): pl.pallas_call(value_kernel, grid=(n,), in_specs=[win_spec(d), win_spec(d...]
    all_to_all x2 -> x5, waiting for transfers between devices: 0.67 us -> 40.7 us  [the longest x3 33.1 us: gather_dp(): lax.all_to_all(jnp.broadcast_to(x[None], (n,) + x.shape), 'dp', 0, 0, til...]
    ppermute x0 -> x10, waiting for transfers between devices: none -> 26.1 us  [swap(): return lax.ppermute(x, 'mp', [(i, i ^ k) for i in range(n)])]
  transfers between devices with their start and end apart: 7 -> 15, of which waited for: 3 -> 8; matrix products, arithmetic and copies ran while one was open for 20% -> 20% of each run, Pallas kernels for 0% -> 13%
where the time goes in v1:
time: 262 us; the launch traced here: 261 us
  Pallas kernels  70.6 us (27%)
  waiting for transfers between devices  66.8 us (25%)
  local copies, waits for them, and re-layouts  52 us (20%)
  starting transfers between devices  37 us (14%)
  other arithmetic  27.7 us (11%)
  blocking collectives  5.37 us (2%)
    all_to_all x3, waiting for transfers between devices, gather_dp(): lax.all_to_all(jnp.broadcast_to(x[None], (n,) + x.shape), 'dp', 0, 0, til...  33.1 us
    ppermute x10, waiting for transfers between devices, swap(): return lax.ppermute(x, 'mp', [(i, i ^ k) for i in range(n)])  26.1 us
    pallas_call x1, Pallas kernels, value_call(): pl.pallas_call(value_kernel, grid=(n,), in_specs=[win_spec(d), win_spec(d...  22.4 us
    all_to_all x3, starting transfers between devices, gather_dp(): lax.all_to_all(jnp.broadcast_to(x[None], (n,) + x.shape), 'dp', 0, 0, til...  16.8 us
    pallas_call x1, Pallas kernels, gate_call(): pl.pallas_call(gate_kernel, grid=(n,), in_specs=[win_spec(d), const(d, c)...  16 us
    pallas_call x1, Pallas kernels, back_call(): pl.pallas_call(back_kernel, grid=(n,), in_specs=[win_spec(d)] + [img(WIN,...  14.4 us
    pallas_call x1, Pallas kernels, out_call(): pl.pallas_call(out_kernel, grid=(n,), in_specs=[win_spec(d), win_spec(d)]...  13.8 us
    all_to_all x2, starting transfers between devices, scatter_sum(): return lax.all_to_all(s, 'dp', 0, 0, tiled=True).astype(F32).sum(0)  11.7 us
  transfers between devices with their start and end apart: 15, of which 8 were waited for; matrix products, arithmetic and copies ran while one was open for 20% of the time, Pallas kernels for 13%

profile of v1, /device:TPU:0, one launch (start us, length us, event | category | flops | bytes accessed | tf_op | source)
XLA Modules:
  0.0 260.9 jit_solution(17671189775543505430)
XLA Ops:
  3.5 7.3 %all-to-all-start = ((bf16[8,64,768]{2,1,0:T(8,128)(2,1)}), bf16[8,64,768]{2,1,0:T(8,128)(2,1)S(1)}, u32[]{:S(2)}, u32[]{:S(2)}) async-start(bf16[8,64,768]{2,1,0:T(8,128)(2,1)} %broadcast_in_dim.93), calls=%async_computation | async-start | bytes 1572864 | tf_op jit(solution)/shard_map/all_to_all | solution.py:186
  11.2 19.8 %all-to-all-done = bf16[8,64,768]{2,1,0:T(8,128)(2,1)S(1)} async-done(((bf16[8,64,768]{2,1,0:T(8,128)(2,1)}), bf16[8,64,768]{2,1,0:T(8,128)(2,1)S(1)}, u32[]{:S(2)}, u32[]{:S(2)}) %all-to-all-start) | async-done | bytes 786464 | tf_op jit(solution)/shard_map/all_to_all | solution.py:186
  31.7 3.6 %all-to-all-start.1 = ((bf16[8,64,384]{2,1,0:T(8,128)(2,1)}), bf16[8,64,384]{2,1,0:T(8,128)(2,1)S(1)}, u32[]{:S(2)}, u32[]{:S(2)}) async-start(bf16[8,64,384]{2,1,0:T(8,128)(2,1)} %broadcast_in_dim.97), calls=%async_computation.1 | async-start | bytes 786432 | tf_op jit(solution)/shard_map/all_to_all | solution.py:186
  35.3 1.6 collective-permute-start
  38.4 8.8 %all-to-all-done.1 = bf16[8,64,384]{2,1,0:T(8,128)(2,1)S(1)} async-done(((bf16[8,64,384]{2,1,0:T(8,128)(2,1)}), bf16[8,64,384]{2,1,0:T(8,128)(2,1)S(1)}, u32[]{:S(2)}, u32[]{:S(2)}) %all-to-all-start.1) | async-done | bytes 393248 | tf_op jit(solution)/shard_map/all_to_all | solution.py:186
  47.1 1.5 collective-permute-start.2
  48.7 7.2 %collective-permute-done = bf16[512,768]{1,0:T(8,128)(2,1)} collective-permute-done((bf16[512,768]{1,0:T(8,128)(2,1)S(1)}, bf16[512,768]{1,0:T(8,128)(2,1)}, u32[]{:S(2)}, u32[]{:S(2)}) %collective-permute-start) | collective-permute-done | bytes 786464 | tf_op jit(solution)/shard_map/ppermute | solution.py:182
  57.1 1.3 pad_maximum_fusion
  58.4 1.3 fusion.3
  59.7 1.4 copy.53.s_ref
  63.8 1.2 mul.115
  65.1 1.2 mul.118
  66.4 1.2 mul.121
  67.7 1.2 mul.124
  70.3 1.2 mul.130
  71.5 5.4 %all-gather.1 = f32[4,4,384]{2,1,0:T(4,128)S(1)} all-gather(f32[1,4,384]{2,1,0:T(4,128)S(1)} %maximum_bitcast_fusion), channel_id=2, replica_groups=mesh['dp'=8,'mp'=4] {'mp'}, dimensions={0}, use_global_device_ids=true | all-gather | bytes 30720 | tf_op jit(solution)/shard_map/all_gather | solution.py:206
  76.9 2.0 pad_maximum_fusion.8
  79.8 3.9 %input_norm.1 = (bf16[1296,512]{1,0:T(8,128)(2,1)}, f32[1,512]{1,0:T(1,128)}) custom-call(bf16[1296,512]{1,0:T(8,128)(2,1)} %x_ref.3, bf16[1296,512]{1,0:T(8,128)(2,1)} %g_ref.5, f32[1,512]{1,0:T(1,128)} %bitcast.58, f32[1,512]{1,0:T(1,128)} %bitcast.63), custom_call_target="tpu_custom_call" | custom-call | tf_op jit(solution)/shard_map/input_norm/pallas_call | solution.py:39
  84.4 2.5 pad_maximum_fusion.4.w_ref.wg_ref
  86.9 16.0 %gate_forward.1 = (bf16[4,336,1536]{2,1,0:T(8,128)(2,1)}, bf16[4,336,1536]{2,1,0:T(8,128)(2,1)}, bf16[4,336,1536]{2,1,0:T(8,128)(2,1)}, f32[4,336,1]{2,1,0:T(8,128)}, bf16[4,336,1536]{2,1,0:T(8,128)(2,1)}) custom-call(bf16[1296,512]{1,0:T(8,128)(2,1)} %get-tuple-element.39.n_ref, bf16[512,1536]{1,0:T(8,128)(2,1)} %pad_maximum_fusion.4.w_ref.wg_ref, ...), custom_call_target="tpu_custom_call" | custom-call | tf_op jit(solution)/shard_map/gate_forward/pallas_call | solution.py:64
  102.9 1.5 fusion.8
  104.4 1.9 pad_maximum_fusion.1
  106.3 22.4 %value_and_backward.1 = (bf16[4,336,1536]{2,1,0:T(8,128)(2,1)}, bf16[4,336,1536]{2,1,0:T(8,128)(2,1)}, bf16[4,336,1536]{2,1,0:T(8,128)(2,1)}, f32[4,336,1]{2,1,0...) custom-call(bf16[1296,512]{1,0:T(8,128)(2,1)} %get-tuple-element.39.n_ref, ...), custom_call_target="tpu_custom_call" | custom-call | tf_op jit(solution)/shard_map/value_and_backward/pallas_call | solution.py:94
  128.7 14.4 %gate_backward.1 = (bf16[4,336,1536]{2,1,0:T(8,128)(2,1)}, f32[4,336,336]{2,1,0:T(8,128)}, f32[512,1536]{1,0:T(8,128)}, f32[8,1536]{1,0:T(8,128)}, f32[8,1536]{1,0:T(8,128)}, /*index=5*/f32[8,1536]{1,0:T(8,128)}) custom-call(bf16[1296,512]{1,0:T(8,128)(2,1)} %get-tuple-element.39.n_ref, bf16[4,336,1536]{2,1,0:T(8,128)(2,1)} %get-tuple-element.43.dshift_ref, ...), custom_call_target="tpu_custom_call" | custom-call | tf_op jit(solution)/shard_map/gate_backward/pallas_call | solution.py:124
  143.1 2.0 fusion.4
  149.3 2.0 add_convert_fusion
  151.3 1.6 reshape.143
  152.9 2.4 gather_fusion.2
  157.9 1.3 copy.56
  160.2 2.2 convert_element_type.91
  165.1 1.5 copy.57
  167.4 1.6 collective-permute-start.5
  169.0 1.3 pad_maximum_fusion.5
  170.5 11.1 %collective-permute-done.5 = bf16[512,440]{1,0:T(8,128)(2,1)S(1)} collective-permute-done((bf16[512,440]{1,0:T(8,128)(2,1)S(1)}, bf16[512,440]{1,0:T(8,128)(2,1)S(1)}, u32[]{:S(2)}, u32[]{:S(2)}) %collective-permute-start.5) | collective-permute-done | bytes 450592 | tf_op jit(solution)/shard_map/ppermute | solution.py:182
  182.5 6.0 %all-to-all-start.2 = ((bf16[8,64,440]{2,1,0:T(8,128)(2,1)}), bf16[8,64,440]{2,1,0:T(8,128)(2,1)S(1)}, u32[]{:S(2)}, u32[]{:S(2)}) async-start(bf16[8,64,440]{2,1,0:T(8,128)(2,1)} %bitcast.25), calls=%async_computation.2 | async-start | bytes 1048576 | tf_op jit(solution)/shard_map/all_to_all | solution.py:198
  189.5 13.8 %outputs.1 = (bf16[1296,512]{1,0:T(8,128)(2,1)}, f32[1296,512]{1,0:T(8,128)}, f32[1,512]{1,0:T(1,128)}, f32[1,512]{1,0:T(1,128)}) custom-call(bf16[1296,512]{1,0:T(8,128)(2,1)} %x_ref.3, bf16[1296,512]{1,0:T(8,128)(2,1)} %g_ref.5, bf16[4,336,1536]{2,1,0:T(8,128)(2,1)} %get-tuple-element.41.prod_ref, bf16[4,336,1536]{2,1,0:T(8,128)(2,1)} %get-tuple-element.42.dpv_ref, ...), custom_call_target="tpu_custom_call" | custom-call | tf_op jit(solution)/shard_map/outputs/pallas_call | solution.py:159
  205.6 6.0 %all-to-all-start.3 = ((f32[8,1,11588]{2,1,0:T(1,128)}), f32[8,1,11588]{2,1,0:T(1,128)}, u32[]{:S(2)}, u32[]{:S(2)}) async-start(f32[8,1,11588]{2,1,0:T(1,128)} %broadcast_in_dim.106), calls=%async_computation.3 | async-start | bytes 745472 | tf_op jit(solution)/shard_map/all_to_all | solution.py:186
  212.7 2.2 convert_add_fusion
  215.9 1.6 collective-permute-start.9
  217.4 4.6 %all-to-all-done.3 = f32[8,1,11588]{2,1,0:T(1,128)} async-done(((f32[8,1,11588]{2,1,0:T(1,128)}), f32[8,1,11588]{2,1,0:T(1,128)}, u32[]{:S(2)}, u32[]{:S(2)}) %all-to-all-start.3) | async-done | bytes 370848 | tf_op jit(solution)/shard_map/all_to_all | solution.py:186
  223.8 1.5 reshape_reshape.3
  225.4 1.7 pad_maximum_fusion.12
  227.0 1.6 collective-permute-start.6
  228.7 7.2 %collective-permute-done.9 = bf16[512,768]{1,0:T(8,128)(2,1)} collective-permute-done((bf16[512,768]{1,0:T(8,128)(2,1)}, bf16[512,768]{1,0:T(8,128)(2,1)}, u32[]{:S(2)}, u32[]{:S(2)}) %collective-permute-start.9) | collective-permute-done | bytes 786464 | tf_op jit(solution)/shard_map/ppermute | solution.py:182
  235.9 2.3 fusion
  238.2 5.7 %all-to-all-start.4 = ((bf16[8,64,768]{2,1,0:T(8,128)(2,1)}), bf16[8,64,768]{2,1,0:T(8,128)(2,1)S(1)}, u32[]{:S(2)}, u32[]{:S(2)}) async-start(bf16[8,64,768]{2,1,0:T(8,128)(2,1)} %bitcast.50), calls=%async_computation.4 | async-start | bytes 1572864 | tf_op jit(solution)/shard_map/all_to_all | solution.py:198
  250.0 1.3 reshape.152
  252.6 7.6 %all-to-all-done.4 = bf16[8,64,768]{2,1,0:T(8,128)(2,1)S(1)} async-done(((bf16[8,64,768]{2,1,0:T(8,128)(2,1)}), bf16[8,64,768]{2,1,0:T(8,128)(2,1)S(1)}, u32[]{:S(2)}, u32[]{:S(2)}) %all-to-all-start.4) | async-done | bytes 786464 | tf_op jit(solution)/shard_map/all_to_all | solution.py:198
  (205 shorter events, 39.7 us)
Async XLA Ops:
  0.6 10.1 %copy-start.15 = (f32[324,324]{1,0:T(8,128)S(1)}, f32[324,324]{1,0:T(8,128)}, u32[]{:S(2)}) copy-start(f32[324,324]{1,0:T(8,128)} %param.26) | copy-start | bytes 1259716
  0.7 10.3 %copy-start.18 = (f32[64,384]{1,0:T(8,128)S(1)}, f32[64,384]{1,0:T(8,128)}, u32[]{:S(2)}) copy-start(f32[64,384]{1,0:T(8,128)} %param.21) | copy-start | bytes 294916
  1.6 9.3 %copy-start.33 = (s32[16]{0:T(128)S(1)}, s32[16]{0:T(128)}, u32[]{:S(2)}) copy-start(s32[16]{0:T(128)} %param.17) | copy-start | bytes 196
  3.5 27.4 %all-to-all-start = ((bf16[8,64,768]{2,1,0:T(8,128)(2,1)}), bf16[8,64,768]{2,1,0:T(8,128)(2,1)S(1)}, u32[]{:S(2)}, u32[]{:S(2)}) async-start(bf16[8,64,768]{2,1,0:T(8,128)(2,1)} %broadcast_in_dim.93), calls=%async_computation | async-start | bytes 1572864 | tf_op jit(solution)/shard_map/all_to_all | solution.py:186
  31.7 15.4 %all-to-all-start.1 = ((bf16[8,64,384]{2,1,0:T(8,128)(2,1)}), bf16[8,64,384]{2,1,0:T(8,128)(2,1)S(1)}, u32[]{:S(2)}, u32[]{:S(2)}) async-start(bf16[8,64,384]{2,1,0:T(8,128)(2,1)} %broadcast_in_dim.97), calls=%async_computation.1 | async-start | bytes 786432 | tf_op jit(solution)/shard_map/all_to_all | solution.py:186
  35.3 3.1 %copy-start.31 = (f32[324]{0:T(512)S(1)}, f32[324]{0:T(512)}, u32[]{:S(2)}) copy-start(f32[324]{0:T(512)} %param.27) | copy-start | bytes 3892
  35.3 20.6 %collective-permute-start = (bf16[512,768]{1,0:T(8,128)(2,1)S(1)}, bf16[512,768]{1,0:T(8,128)(2,1)}, u32[]{:S(2)}, u32[]{:S(2)}) collective-permute-start(bf16[512,768]{1,0:T(8,128)(2,1)S(1)} %bitcast.48), channel_id=1, source_target_pairs={{0,2},{1,3},{2,0},{3,1},{4,6},{5,7},{6,4},{7,5},{8,10},{9,11},{10,... | collective-permute-start | bytes 2359304 | tf_op jit(solution)/shard_map/ppermute | solution.py:182
  47.1 29.8 %collective-permute-start.2 = (bf16[512,384]{1,0:T(8,128)(2,1)S(1)}, bf16[512,384]{1,0:T(8,128)(2,1)}, u32[]{:S(2)}, u32[]{:S(2)}) collective-permute-start(bf16[512,384]{1,0:T(8,128)(2,1)S(1)} %bitcast.45), channel_id=1, source_target_pairs={{0,2},{1,3},{2,0},{3,1},{4,6},{5,7},{6,4},{7,5},{8,10},{9,11},{10,... | collective-permute-start | bytes 1179656 | tf_op jit(solution)/shard_map/ppermute | solution.py:182
  57.1 1.3 copy-start.7
  57.1 1.3 copy-start.8
  58.4 44.5 %collective-permute-start.1 = (bf16[512,1536]{1,0:T(8,128)(2,1)}, bf16[512,1536]{1,0:T(8,128)(2,1)}, u32[]{:S(2)}, u32[]{:S(2)}) collective-permute-start(bf16[512,1536]{1,0:T(8,128)(2,1)} %pad_maximum_fusion), channel_id=1, source_target_pairs={{0,1},{1,0},{2,3},{3,2},{4,5},{5,4},{6,7},{7,6},{8,9},{9,8},{10,11... | collective-permute-start | bytes 4718600 | tf_op jit(solution)/shard_map/ppermute | solution.py:182
  59.7 2.8 %copy-start.27 = (f32[384]{0:T(512)S(1)}, f32[384]{0:T(512)}, u32[]{:S(2)}) copy-start(f32[384]{0:T(512)} %param.22) | copy-start | bytes 4612
  59.7 2.8 %copy-start.28 = (f32[384]{0:T(512)S(1)}, f32[384]{0:T(512)}, u32[]{:S(2)}) copy-start(f32[384]{0:T(512)} %param.23) | copy-start | bytes 4612
  59.7 2.8 %copy-start.29 = (f32[384]{0:T(512)S(1)}, f32[384]{0:T(512)}, u32[]{:S(2)}) copy-start(f32[384]{0:T(512)} %param.24) | copy-start | bytes 4612
  59.7 2.8 %copy-start.30 = (f32[384]{0:T(512)S(1)}, f32[384]{0:T(512)}, u32[]{:S(2)}) copy-start(f32[384]{0:T(512)} %param.25) | copy-start | bytes 4612
  69.0 10.2 %copy-start.32 = (s32[4]{0:T(128)S(1)}, s32[4]{0:T(128)}, u32[]{:S(2)}) copy-start(s32[4]{0:T(128)} %constant.72.clone) | copy-start | bytes 52
  78.9 5.6 %collective-permute-start.3 = (bf16[512,768]{1,0:T(8,128)(2,1)}, bf16[512,768]{1,0:T(8,128)(2,1)}, u32[]{:S(2)}, u32[]{:S(2)}) collective-permute-start(bf16[512,768]{1,0:T(8,128)(2,1)} %pad_maximum_fusion.8), channel_id=1, source_target_pairs={{0,1},{1,0},{2,3},{3,2},{4,5},{5,4},{6,7},{7,6},{8,9},{9,8},{10,11... | collective-permute-start | bytes 2359304 | tf_op jit(solution)/shard_map/ppermute | solution.py:182
  145.1 4.1 %copy-start.2 = (f32[104976]{0:T(1024)S(1)}, f32[104976]{0:T(1024)}, u32[]{:S(2)}) copy-start(f32[104976]{0:T(1024)} %mul.115) | copy-start | bytes 1259716
  146.3 2.9 %copy-start.3 = (f32[104976]{0:T(1024)S(1)}, f32[104976]{0:T(1024)}, u32[]{:S(2)}) copy-start(f32[104976]{0:T(1024)} %mul.118) | copy-start | bytes 1259716
  147.5 1.7 copy-start.4
  151.2 6.0 %copy-start.1 = (f32[512,1536]{1,0:T(8,128)S(1)}, f32[512,1536]{1,0:T(8,128)}, u32[]{:S(2)}) copy-start(f32[512,1536]{1,0:T(8,128)} %get-tuple-element.60) | copy-start | bytes 9437188
  159.2 5.9 %collective-permute-start.4 = (bf16[512,880]{0,1:T(8,128)(2,1)}, bf16[512,880]{0,1:T(8,128)(2,1)}, u32[]{:S(2)}, u32[]{:S(2)}) collective-permute-start(bf16[512,880]{0,1:T(8,128)(2,1)} %copy.56), channel_id=1, source_target_pairs={{0,1},{1,0},{2,3},{3,2},{4,5},{5,4},{6,7},{7,6},{8,9},{9,8},{10,11... | collective-permute-start | bytes 2703368 | tf_op jit(solution)/shard_map/ppermute | solution.py:182
  160.2 2.8 %copy-start = (f32[512,1536]{1,0:T(8,128)S(1)}, f32[512,1536]{1,0:T(8,128)}, u32[]{:S(2)}) copy-start(f32[512,1536]{1,0:T(8,128)} %get-tuple-element.63) | copy-start | bytes 9437188
  164.1 2.6 copy-start.13
  164.1 2.6 %copy-start.14 = (bf16[512,56]{1,0:T(8,128)(2,1)S(1)}, bf16[512,56]{1,0:T(8,128)(2,1)}, u32[]{:S(2)}) copy-start(bf16[512,56]{1,0:T(8,128)(2,1)} %get-tuple-element.109) | copy-start | bytes 172036
  166.7 2.3 copy-start.5
  167.3 3.1 %copy-start.34 = (s32[4]{0:T(128)S(1)}, s32[4]{0:T(128)}, u32[]{:S(2)}) copy-start(s32[4]{0:T(128)} %get-tuple-element.51) | copy-start | bytes 52
  167.4 14.2 %collective-permute-start.5 = (bf16[512,440]{1,0:T(8,128)(2,1)S(1)}, bf16[512,440]{1,0:T(8,128)(2,1)S(1)}, u32[]{:S(2)}, u32[]{:S(2)}) collective-permute-start(bf16[512,440]{1,0:T(8,128)(2,1)S(1)} %slice.393), channel_id=1, source_target_pairs={{0,2},{1,3},{2,0},{3,1},{4,6},{5,7},{6,4},{7,5},{8,10},{9,11},{10,... | collective-permute-start | bytes 1351688 | tf_op jit(solution)/shard_map/ppermute | solution.py:182
  170.3 18.2 %copy-start.22 = (f32[8,1536]{1,0:T(8,128)S(1)}, f32[8,1536]{1,0:T(8,128)}, u32[]{:S(2)}) copy-start(f32[8,1536]{1,0:T(8,128)} %get-tuple-element.53) | copy-start | bytes 147460
  170.3 18.2 %copy-start.21 = (f32[8,1536]{1,0:T(8,128)S(1)}, f32[8,1536]{1,0:T(8,128)}, u32[]{:S(2)}) copy-start(f32[8,1536]{1,0:T(8,128)} %get-tuple-element.54) | copy-start | bytes 147460
  170.3 18.3 %copy-start.20 = (f32[8,1536]{1,0:T(8,128)S(1)}, f32[8,1536]{1,0:T(8,128)}, u32[]{:S(2)}) copy-start(f32[8,1536]{1,0:T(8,128)} %get-tuple-element.55) | copy-start | bytes 147460
  170.3 18.3 %copy-start.19 = (f32[8,1536]{1,0:T(8,128)S(1)}, f32[8,1536]{1,0:T(8,128)}, u32[]{:S(2)}) copy-start(f32[8,1536]{1,0:T(8,128)} %get-tuple-element.52) | copy-start | bytes 147460
  170.3 41.2 %collective-permute-start.8 = (bf16[512,1536]{1,0:T(8,128)(2,1)}, bf16[512,1536]{1,0:T(8,128)(2,1)S(1)}, u32[]{:S(2)}, u32[]{:S(2)}) collective-permute-start(bf16[512,1536]{1,0:T(8,128)(2,1)} %pad_maximum_fusion.5), channel_id=1, source_target_pairs={{0,1},{1,0},{2,3},{3,2},{4,5},{5,4},{6,7},{7,6},{8,9},{9,8},{10,11... | collective-permute-start | bytes 4718600 | tf_op jit(solution)/shard_map/ppermute | solution.py:182
  170.4 19.0 %copy-start.24 = (pred[4]{0:T(512)(128)(4,1)}, pred[4]{0:T(512)(128)(4,1)S(1)}, u32[]{:S(2)}) copy-start(pred[4]{0:T(512)(128)(4,1)S(1)} %compare_and_fusion) | copy-start | bytes 16
  182.5 21.1 %all-to-all-start.2 = ((bf16[8,64,440]{2,1,0:T(8,128)(2,1)}), bf16[8,64,440]{2,1,0:T(8,128)(2,1)S(1)}, u32[]{:S(2)}, u32[]{:S(2)}) async-start(bf16[8,64,440]{2,1,0:T(8,128)(2,1)} %bitcast.25), calls=%async_computation.2 | async-start | bytes 1048576 | tf_op jit(solution)/shard_map/all_to_all | solution.py:198
  189.5 13.9 %copy-start.10 = (f32[4,336,1]{2,1,0:T(8,128)S(1)}, f32[4,336,1]{2,1,0:T(8,128)}, u32[]{:S(2)}) copy-start(f32[4,336,1]{2,1,0:T(8,128)} %get-tuple-element.56) | copy-start | bytes 16132
  189.5 14.4 %copy-start.26 = (f32[1,512]{1,0:T(1,128)S(1)}, f32[1,512]{1,0:T(1,128)}, u32[]{:S(2)}) copy-start(f32[1,512]{1,0:T(1,128)} %get-tuple-element.59) | copy-start | bytes 6148
  203.7 7.9 %copy-start.11 = (f32[64,440]{1,0:T(8,128)}, f32[64,440]{1,0:T(8,128)S(1)}, u32[]{:S(2)}) copy-start(f32[64,440]{1,0:T(8,128)S(1)} %convert_reduce_fusion.1) | copy-start | bytes 337924
  205.6 16.4 %all-to-all-start.3 = ((f32[8,1,11588]{2,1,0:T(1,128)}), f32[8,1,11588]{2,1,0:T(1,128)}, u32[]{:S(2)}, u32[]{:S(2)}) async-start(f32[8,1,11588]{2,1,0:T(1,128)} %broadcast_in_dim.106), calls=%async_computation.3 | async-start | bytes 745472 | tf_op jit(solution)/shard_map/all_to_all | solution.py:186
  215.9 20.0 %collective-permute-start.9 = (bf16[512,768]{1,0:T(8,128)(2,1)}, bf16[512,768]{1,0:T(8,128)(2,1)}, u32[]{:S(2)}, u32[]{:S(2)}) collective-permute-start(bf16[512,768]{1,0:T(8,128)(2,1)} %slice.392), channel_id=1, source_target_pairs={{0,2},{1,3},{2,0},{3,1},{4,6},{5,7},{6,4},{7,5},{8,10},{9,11},{10,... | collective-permute-start | bytes 2359304 | tf_op jit(solution)/shard_map/ppermute | solution.py:182
  227.0 16.8 %copy-start.9 = (f32[8,3584]{1,0:T(8,128)S(1)}, f32[8,3584]{1,0:T(8,128)}, u32[]{:S(2)}) copy-start(f32[8,3584]{1,0:T(8,128)} %slice.340) | copy-start | bytes 344068
  227.0 17.0 %collective-permute-start.6 = (f32[36676]{0:T(1024)}, f32[36676]{0:T(1024)S(1)}, u32[]{:S(2)}, u32[]{:S(2)}) collective-permute-start(f32[36676]{0:T(1024)} %pad_maximum_fusion.12), channel_id=1, source_target_pairs={{0,2},{1,3},{2,0},{3,1},{4,6},{5,7},{6,4},{7,5},{8,10},{9,11},{10,... | collective-permute-start | bytes 440120 | tf_op jit(solution)/shard_map/ppermute | solution.py:182
  238.2 22.0 %all-to-all-start.4 = ((bf16[8,64,768]{2,1,0:T(8,128)(2,1)}), bf16[8,64,768]{2,1,0:T(8,128)(2,1)S(1)}, u32[]{:S(2)}, u32[]{:S(2)}) async-start(bf16[8,64,768]{2,1,0:T(8,128)(2,1)} %bitcast.50), calls=%async_computation.4 | async-start | bytes 1572864 | tf_op jit(solution)/shard_map/all_to_all | solution.py:198
  243.9 1.2 copy-start.12
  245.0 1.6 collective-permute-start.7
  246.6 2.1 copy-start.16
  249.1 2.2 slice-start
  249.1 2.8 %copy-start.17 = (f32[8004]{0:T(1024)S(1)}, f32[8004]{0:T(1024)}, u32[]{:S(2)}) copy-start(f32[8004]{0:T(1024)} %copy-done.16) | copy-start | bytes 96052
  (3 other events, 3.1 us)

commit v2 on v0

v2 whole, which is shorter than its diff:
```python
import jax
import jax.numpy as jnp
from jax import lax
from jax.experimental import pallas as pl
from jax.experimental.pallas import tpu as pltpu
from jax.sharding import PartitionSpec as P

EPS = 1e-5
BF = jnp.bfloat16
F32 = jnp.float32
AXES = ("dp", "mp")
WIN = 336
STEP = 320
EXT = 352
CH = 16
PAD = 384
ORDER = (0, 2, 1, 3)
GELU_C = (7.97882133e-01, 3.63449931e-02, -4.51808700e-05, -5.02619616e-05, 3.08533547e-06, -6.58149666e-08)
LOG2E_HALF = -0.7213475204444817
INV_SQRT_2PI = 0.3989422804014327
MB = 2**20


def dot(a, b):
    return jnp.dot(a, b, preferred_element_type=F32)


def dot_tn(a, b):
    return lax.dot_general(a, b, (((0,), (0,)), ((), ())), preferred_element_type=F32)


def dot_nt(a, b):
    return lax.dot_general(a, b, (((1,), (1,)), ((), ())), preferred_element_type=F32)


def gelu_both(x):
    u = x * x
    um = jnp.minimum(u, 30.0)
    p = GELU_C[5]
    for c in GELU_C[4::-1]:
        p = p * um + c
    cdf = 0.5 + 0.5 * jnp.tanh(x * p)
    slope = cdf + (x * INV_SQRT_2PI) * jnp.exp2(u * LOG2E_HALF)
    return x * cdf, slope


def split(v):
    hi = v.astype(BF)
    return hi, (v - hi.astype(F32)).astype(BF)


def fold8(v):
    out = v[0:8]
    for r in range(8, v.shape[0], 8):
        out = out + v[r : r + 8]
    return out


def img(*s):
    return pl.BlockSpec((1,) + s, lambda b, *_: (b,) + (0,) * len(s))


def const(*s):
    return pl.BlockSpec(s, lambda b, *_: (0,) * len(s), pipeline_mode=pl.Buffered(1))


def half(rows, c, h):
    return pl.BlockSpec((1, rows, c), lambda b, *_: (b, 0, h))


def side(d, w, h):
    return pl.BlockSpec((d, w), lambda b, *_: (0, h), pipeline_mode=pl.Buffered(1))


def shape(s, t):
    return jax.ShapeDtypeStruct(s, t)


def fast(s, t):
    return pltpu.VMEM(s, t)


def slow(s, t):
    return pltpu.HBM(s, t)


def in_hbm(*arrays):
    return tuple(pltpu.with_memory_space_constraint(a, pltpu.HBM) for a in arrays)


ANY = pl.BlockSpec(memory_space=pl.ANY)


def call(kernel, info, args, in_specs, outs, out_specs, scratch=(), grid=(1,), name=None, after=(), vmem=8, us=1):
    n_in, n_after = len(args), len(after)

    def ordered(info_ref, *refs):
        kernel(info_ref, *refs[:n_in], *refs[n_in + n_after :])

    return pl.pallas_call(
        ordered,
        grid_spec=pltpu.PrefetchScalarGridSpec(
            num_scalar_prefetch=1, grid=grid, in_specs=list(in_specs) + [ANY] * n_after, out_specs=out_specs, scratch_shapes=list(scratch)
        ),
        out_shape=outs,
        compiler_params=pltpu.CompilerParams(vmem_limit_bytes=vmem * MB),
        cost_estimate=pl.CostEstimate(flops=int(us * 1.1e9), bytes_accessed=int(us * 3.3e6), transcendentals=0),
        name=name,
    )(info, *args, *after)


def whole(a):
    return const(*a.shape)


def simple_call(kernel, info, args, outs, name, scratch=(), after=(), us=1):
    return call(kernel, info, args, [whole(a) for a in args], outs, [whole(o) for o in outs], scratch, name=name, after=after, us=us)


def cast_kernel(info, wg_ref, wv_ref, wo_ref, bv, bg, gg, gs, g_ref, vo_ref, vec_ref):
    c = wg_ref.shape[1]
    g_ref[...] = wg_ref[...].astype(BF)
    vo_ref[:, :c] = wv_ref[...].astype(BF)
    vo_ref[:, c:] = wo_ref[...].astype(BF)
    vec_ref[...] = both(jnp.concatenate([bv[...][None], bg[...][None], gg[...][None], gs[...][None], jnp.zeros((4, bv.shape[0]), F32)], 0))


def run_copies(pairs, sems):
    copies = [pltpu.make_async_copy(src, dst, sems.at[k]) for k, (src, dst) in enumerate(pairs)]
    for c in copies:
        c.start()
    for c in copies:
        c.wait()


def stack_kernel(info, *refs):
    *parts, out, sems = refs
    pairs, at = [], 0
    for ref in parts:
        n = ref.shape[0]
        pairs.append((ref, out.at[at : at + n]))
        at += n
    run_copies(pairs, sems)


def stack_call(info, parts, after, name):
    n = len(parts)
    rows, c = sum(a.shape[0] for a in parts), parts[0].shape[1]
    return call(stack_kernel, info, parts, [ANY] * n, [shape((rows, c), BF)], [ANY], [pltpu.SemaphoreType.DMA((n,))], name=name, after=after)[0]


def assemble_kernel(tensors, extra, info, *refs):
    *pieces, out, sems = refs
    where = ((0, 0), (1, 0), (0, 1), (1, 1))
    d, c = out.shape[0] - extra, out.shape[1] // (2 * tensors)
    n = 4
    r = d // (2 * n)
    pairs = []
    for ref, (xr, slot) in zip(pieces, where):
        for t in range(tensors):
            src, dst = slice(t * c, (t + 1) * c), slice((2 * t + slot) * c, (2 * t + slot + 1) * c)
            for k in range(n):
                row = pl.multiple_of((lax.rem(info[1] + (n - k), n) * 2 + jnp.bitwise_xor(info[2], xr)) * r, r)
                pairs.append((ref.at[k * r : (k + 1) * r, src], out.at[pl.ds(row, r), dst]))
            if xr == 0 and extra:
                pairs.append((ref.at[n * r :, src], out.at[d:, dst]))
    run_copies(pairs, sems)


def assemble_call(info, pieces, tensors, extra, after, name):
    rows, c = pieces[0].shape
    s = (2 * (rows - extra) + extra, 2 * c)
    return call(lambda *a: assemble_kernel(tensors, extra, *a), info, pieces, [ANY] * len(pieces), [shape(s, BF)],
                [const(*s)], [pltpu.SemaphoreType.DMA((18 * tensors,))], name=name, after=after)[0]


def norm_kernel(info, x_ref, g_ref, gain_ref, shift_ref, n_ref, gsum_ref):
    b = pl.program_id(0)

    @pl.when(b == 0)
    def _():
        gsum_ref[...] = jnp.zeros_like(gsum_ref)

    own = jnp.where(b == pl.num_programs(0) - 1, 1.0, 0.0)
    for r in range(0, WIN, 48):
        x = x_ref[r : r + 48, :].astype(F32)
        cen = x - jnp.mean(x, -1, keepdims=True)
        inv = lax.rsqrt(jnp.mean(cen * cen, -1, keepdims=True) + EPS)
        n_ref[0, r : r + 48, :] = (cen * inv * gain_ref[...][None] + shift_ref[...][None]).astype(BF)
    total = fold8(g_ref[STEP:, :].astype(F32)) * own
    for r in range(0, STEP, CH):
        total = total + fold8(g_ref[r : r + CH, :].astype(F32))
    gsum_ref[...] += jnp.sum(total, 0, keepdims=True)


def window_rows(d):
    return pl.BlockSpec((pl.Element(WIN), pl.Element(d)), lambda b, *_: (b * STEP, 0))


def norm_call(info, x, g, gain, shift, n, after):
    d = x.shape[1]
    return call(norm_kernel, info, in_hbm(x, g, gain, shift), [window_rows(d), window_rows(d), const(d), const(d)],
                [slow((n, WIN, d), BF), shape((1, d), F32)], [img(WIN, d), const(1, d)], grid=(n,), name="input_norm", after=after, us=3)


def windows_kernel(info, sp_ref, sb_ref, s_ref, st_ref, sbw_ref, token, pad, tpad, col):
    p = sp_ref.shape[0]
    b = pl.program_id(0)

    @pl.when(b == 0)
    def _():
        pad[...] = jnp.zeros_like(pad)
        pad[0:p, 0:p] = sp_ref[...]
        tpad[...] = pad[...].T
        col[...] = jnp.concatenate([jnp.broadcast_to(sb_ref[...][None], (128, p)), jnp.zeros((128, PAD - p), F32)], 1).T
        token[...] = jnp.zeros_like(token)

    ri = lax.broadcasted_iota(jnp.int32, (WIN, PAD), 0)
    ci = lax.broadcasted_iota(jnp.int32, (WIN, PAD), 1)
    for k in range(4):

        @pl.when(lax.rem(b, 4) == k)
        def _():
            off = k * (p - STEP)
            end = off + count_of(info, b)
            live = (ri >= off) & (ri < end) & (ci >= off) & (ci < end)
            move = lambda v: pltpu.roll(pltpu.roll(v, off, 0), off, 1) if off else v
            s_ref[0] = jnp.where(live, move(pad[...])[:WIN], 0.0).astype(BF)[:, :WIN]
            st_ref[0] = jnp.where(live, move(tpad[...])[:WIN], 0.0).astype(BF)[:, :WIN]
            cb = pltpu.roll(col[...], off, 0) if off else col[...]
            sbw_ref[0] = jnp.where(((ri >= off) & (ri < end))[:, :128], cb[:WIN], 0.0)


def count_of(info, b):
    return info[8 + info[5] + b]


def windows_call(info, spatial, sbias, n, after):
    p = spatial.shape[0]
    win = slow((n, WIN, WIN), BF)
    return call(windows_kernel, info, in_hbm(spatial, sbias), [const(p, p), const(p)], [win, win, slow((n, WIN, 128), F32), shape((8, 128), F32)],
                [img(WIN, WIN), img(WIN, WIN), img(WIN, 128), const(8, 128)], [pltpu.VMEM((PAD, PAD), F32)] * 2 + [pltpu.VMEM((PAD, 128), F32)],
                grid=(n,), name="windows", after=after, us=2)


def gate_kernel(info, wa_ref, wb_ref, n_ref, s_ref, sb_ref, rows_ref, hat_ref, slope_ref, inv_ref, shifted_ref, v_ref, pre):
    w = wa_ref.shape[1]
    d = wa_ref.shape[0] - 16
    width = 2 * w

    @pl.when(pl.program_id(0) == 0)
    def _():
        for k, ref in enumerate((wa_ref, wb_ref)):
            v = ref[d:, :].astype(F32)
            v_ref[:, k * w : (k + 1) * w] = v[:8] + v[8:]

    bias, gain, shift = v_ref[1:2, :], v_ref[2:3, :], v_ref[3:4, :]
    pre[:, :w] = dot(n_ref[0], wa_ref[:d, :])
    pre[:, w:] = dot(n_ref[0], wb_ref[:d, :])
    for r in range(0, WIN, CH):
        act, slope = gelu_both(pre[r : r + CH, :] + bias)
        slope_ref[0, r : r + CH, :] = slope.astype(BF)
        cen = act - jnp.sum(act, -1, keepdims=True) * (1.0 / width)
        inv = lax.rsqrt(jnp.sum(cen * cen, -1, keepdims=True) * (1.0 / width) + EPS)
        hat = cen * inv
        inv_ref[0, r : r + CH, :] = jnp.broadcast_to(inv, (CH, 128))
        hat_ref[0, r : r + CH, :] = hat.astype(BF)
        rows_ref[0, r : r + CH, :] = (hat * gain + shift).astype(BF)
    rows_ref[0, WIN:, :] = jnp.ones((EXT - WIN, width), BF)
    sb = sb_ref[0]
    mixed = dot(s_ref[0], rows_ref[0, :WIN, :])
    for t in range(0, width, 128):
        shifted_ref[0, :, t : t + 128] = (mixed[:, t : t + 128] + sb).astype(BF)


def gate_call(info, halves, normed, s, sb, after):
    n, _, d = normed.shape
    w = 2 * halves[0].shape[1]
    big = slow((n, WIN, w), BF)
    return call(
        gate_kernel, info, (*halves, *in_hbm(normed, s, sb)),
        [whole(a) for a in halves] + [img(WIN, d), img(WIN, WIN), img(WIN, 128)],
        [slow((n, EXT, w), BF), big, big, slow((n, WIN, 128), F32), big, shape((8, w), F32)],
        [img(EXT, w), img(WIN, w), img(WIN, w), img(WIN, 128), img(WIN, w), const(8, w)],
        [pltpu.VMEM((WIN, w), F32)], grid=(n,), name="gate_forward", after=after, us=1, vmem=17,
    )


def value_kernel(info, wv_ref, wo_ref, n_ref, g_ref, v_ref, shifted_ref, rows_ref, gin_ref, prod_ref, dshift_ref, dpre_ref, gw_ref, gb_ref, gsp_ref, small_ref,
                 pre, dprod, prods, dpres, n_all, g_all):
    b = pl.program_id(0)
    n_img = pl.num_programs(0)
    d, _ = wv_ref.shape

    @pl.when(b == 0)
    def _():
        gb_ref[...] = jnp.zeros_like(gb_ref)
        gsp_ref[...] = gin_ref[...]

    pre[...] = dot(n_ref[0], wv_ref[...])
    dprod[...] = dot(g_ref[...], wo_ref[...])
    bias = v_ref[0:1, :]
    for r in range(0, WIN, CH):
        act, slope = gelu_both(pre[r : r + CH, :] + bias)
        sh = shifted_ref[0, r : r + CH, :].astype(F32)
        dp = dprod[r : r + CH, :]
        prod = (act * sh).astype(BF)
        prod_ref[0, r : r + CH, :] = prod
        dshift_ref[0, r : r + CH, :] = (dp * act).astype(BF)
        dv = dp * sh * slope
        dvl = dv.astype(BF)
        dpre_ref[0, r : r + CH, :] = dvl
        gb_ref[...] += fold8(dv)
    row = pl.multiple_of(b * WIN, 16)
    n_all[pl.ds(row, WIN), :] = n_ref[0]
    g_all[pl.ds(row, WIN), :] = g_ref[...]
    prods[pl.ds(row, WIN), :] = prod_ref[0]
    dpres[pl.ds(row, WIN), :] = dpre_ref[0]
    part = dot_nt(dshift_ref[0], rows_ref[0])
    part = jnp.concatenate([jnp.concatenate([part, jnp.zeros((WIN, PAD - EXT), F32)], 1), jnp.zeros((PAD - WIN, PAD), F32)], 0)
    off = b * (MAXP_STEP)
    end = off + count_of(info, b)
    ri = lax.broadcasted_iota(jnp.int32, (PAD, PAD), 0)
    ci = lax.broadcasted_iota(jnp.int32, (PAD, PAD), 1)
    live = (ri >= off) & (ri < end) & (((ci >= off) & (ci < end)) | (ci >= WIN))
    part = jnp.where(live, part, 0.0)
    back = lax.rem(PAD - off, PAD)
    gsp_ref[...] += pltpu.roll(pltpu.roll(part, back, 0), back, 1)

    @pl.when(b == n_img - 1)
    def _():
        gwv = dot_tn(n_all[...], dpres[...])
        gw_ref[:d, :] = gwv.astype(gw_ref.dtype)
        gw_ref[d:, :] = dot_tn(g_all[...], prods[...]).astype(gw_ref.dtype)
        small_ref[...] = jnp.concatenate([row_sums(gwv, wv_ref), back_sum(gb_ref[...], wv_ref), jnp.zeros((6, d), F32)], 0)


def row_sums(gw, w_ref):
    prod = gw * w_ref[...].astype(F32)
    t = prod[:, :128]
    for k in range(128, prod.shape[1], 128):
        t = t + prod[:, k : k + 128]
    return jnp.sum(t.T, 0, keepdims=True)


def back_sum(sums, w_ref):
    hi, lo = split(sums)
    return jnp.sum(dot_nt(hi, w_ref[...]) + dot_nt(lo, w_ref[...]), 0, keepdims=True)


MAXP_STEP = 4


def value_call(info, h, keep, vo, normed, g, vecs, shifted, rows, gsp, after=()):
    n, _, d = normed.shape
    w = vecs.shape[1] // 2
    big, out = shape((n, WIN, w), BF), slow((n, WIN, w), BF)
    return call(
        value_kernel, info, (vo, vo, *in_hbm(normed, g), vecs, *in_hbm(shifted, rows), gsp),
        [side(d, w, 0), side(d, w, 1), img(WIN, d), window_rows(d), pl.BlockSpec((8, w), lambda b, *_: (0, h)), half(WIN, w, h), half(EXT, w, h), const(PAD, PAD)],
        [out, big, out, shape((2 * d, w), F32 if keep else BF), shape((8, w), F32), shape((PAD, PAD), F32), shape((8, d), F32)],
        [img(WIN, w)] * 3 + [const(2 * d, w), const(8, w), const(PAD, PAD), const(8, d)],
        [pltpu.VMEM((WIN, w), F32)] * 2 + [pltpu.VMEM((n * WIN, w), BF)] * 2 + [pltpu.VMEM((n * WIN, d), BF)] * 2,
        grid=(n,), name="value_own" if keep else "value_other", after=after, us=1, vmem=23,
    )


def back_kernel(info, n_ref, dsa_ref, dsb_ref, rows_hat_ref, slope_ref, inv_ref, st_ref, v_ref, wa_ref, wb_ref, gba_ref, gbb_ref, sma_ref, smb_ref, gsum_ref,
                dpre_ref, keep_ref, send_ref, vown_ref, dgr, dpres, n_all, gb, gg, gsh):
    b = pl.program_id(0)
    n_img = pl.num_programs(0)
    d, w = n_ref.shape[2], wa_ref.shape[1]
    width = 2 * w
    wa_ref, wb_ref = wa_ref.at[:d], wb_ref.at[:d]

    @pl.when(b == 0)
    def _():
        for r in (gb, gg, gsh):
            r[...] = jnp.zeros_like(r)

    gain = v_ref[2:3, :]
    dgr[:, :w] = dot(st_ref[0], dsa_ref[0])
    dgr[:, w:] = dot(st_ref[0], dsb_ref[0])
    for r in range(0, WIN, CH):
        dr = dgr[r : r + CH, :]
        hat = rows_hat_ref[0, r : r + CH, :].astype(F32)
        gg[...] += fold8(dr * hat)
        gsh[...] += fold8(dr)
        dg = dr * gain
        m1 = jnp.sum(dg, -1, keepdims=True) * (1.0 / width)
        m2 = jnp.sum(dg * hat, -1, keepdims=True) * (1.0 / width)
        dpg = (dg - m1 - hat * m2) * inv_ref[0, r : r + CH, 0:1] * slope_ref[0, r : r + CH, :].astype(F32)
        dpre_ref[0, r : r + CH, :] = dpg.astype(BF)
        gb[...] += fold8(dpg)
    row = pl.multiple_of(b * WIN, 16)
    dpres[pl.ds(row, WIN), :] = dpre_ref[0]
    n_all[pl.ds(row, WIN), :] = n_ref[0]

    @pl.when(b == n_img - 1)
    def _():
        gw = dot_tn(n_all[...], dpres[...])
        keep_ref[...] = gw[:, :w]
        sums = gb[...]
        send_ref[:d, :] = gw[:, w:].astype(BF)
        t = sma_ref[0:1, :] + smb_ref[0:1, :] + row_sums(gw[:, :w], wa_ref) + row_sums(gw[:, w:], wb_ref)
        s = sma_ref[1:2, :] + smb_ref[1:2, :] + back_sum(sums[:, :w], wa_ref) + back_sum(sums[:, w:], wb_ref)
        one = lambda v: jnp.sum(v, 0, keepdims=True)
        fours = [jnp.concatenate([one(gba_ref[...]), one(gbb_ref[...])], 1), one(gb[...]), one(gg[...]), one(gsh[...])]
        wide = lambda v: jnp.concatenate([v, jnp.zeros((1, w - d), F32)], 1)
        full = jnp.concatenate([wide(t), wide(s), wide(gsum_ref[...]), jnp.zeros((1, w), F32)], 0)
        fours = jnp.concatenate(fours, 0)
        hi, lo = split(jnp.concatenate([fours[:, w:], full], 0))
        send_ref[d:, :] = jnp.concatenate([hi, lo], 0)
        fhi, flo = split(full)
        vown_ref[...] = jnp.concatenate([fours[:, :w], fhi.astype(F32) + flo.astype(F32)], 0)


def back_call(info, normed, ds, hat, slope, inv, st, vecs, wg, gbv, small, gsum, after):
    n, _, d = normed.shape
    width = vecs.shape[1]
    w = width // 2
    return call(
        back_kernel, info, (*in_hbm(normed), *ds, *in_hbm(hat, slope, inv, st), vecs, *wg, *gbv, *small, gsum),
        [img(WIN, d), img(WIN, w), img(WIN, w), img(WIN, width), img(WIN, width), img(WIN, 128), img(WIN, WIN), const(8, width), whole(wg[0]), whole(wg[1]),
         const(8, w), const(8, w), const(8, d), const(8, d), const(1, d)],
        [slow((n, WIN, width), BF), shape((d, w), F32), shape((d + 16, w), BF), shape((8, w), F32)],
        [img(WIN, width), const(d, w), const(d + 16, w), const(8, w)],
        [pltpu.VMEM((WIN, width), F32), pltpu.VMEM((n * WIN, width), BF), pltpu.VMEM((n * WIN, d), BF)] + [pltpu.VMEM((8, width), F32)] * 3,
        grid=(n,), name="gate_backward", after=after, us=1, vmem=23,
    )


def joined(v, carry):
    @pl.when(pl.program_id(0) == 0)
    def _():
        carry[...] = jnp.zeros_like(carry)

    v = jnp.concatenate([v[:16] + carry[...], v[16:]], 0)
    carry[...] = v[STEP:]
    return v


def result_kernel(info, x_ref, pa_ref, pb_ref, woa_ref, wob_ref, bias_ref, res_ref, carry):
    start = pl.multiple_of(pl.program_id(0) * STEP, 16)
    br = joined(dot_nt(pa_ref[0], woa_ref[...]) + dot_nt(pb_ref[0], wob_ref[...]), carry)
    res_ref[pl.ds(start, WIN), :] = (x_ref[pl.ds(start, WIN), :].astype(F32) + br + bias_ref[...][None]).astype(BF)


def grad_kernel(info, x_ref, g_ref, va_ref, vb_ref, dg_ref, wva_ref, wvb_ref, wga_ref, wgb_ref, gain_ref, ing_ref, carry):
    start = pl.multiple_of(pl.program_id(0) * STEP, 16)
    d, w = wva_ref.shape
    dn = dot_nt(va_ref[0], wva_ref[...]) + dot_nt(vb_ref[0], wvb_ref[...])
    dn = joined(dn + dot_nt(dg_ref[0, :, :w], wga_ref[:d, :]) + dot_nt(dg_ref[0, :, w:], wgb_ref[:d, :]), carry)
    x = x_ref[pl.ds(start, WIN), :].astype(F32)
    cen = x - jnp.mean(x, -1, keepdims=True)
    inv = lax.rsqrt(jnp.mean(cen * cen, -1, keepdims=True) + EPS)
    hat = cen * inv
    dx = dn * gain_ref[...][None]
    m1 = jnp.mean(dx, -1, keepdims=True)
    m2 = jnp.mean(dx * hat, -1, keepdims=True)
    ing_ref[pl.ds(start, WIN), :] = g_ref[...].astype(F32) + inv * (dx - m1 - hat * m2)


def result_call(info, x, prod, vo, bias, after):
    n, _, w = prod[0].shape
    rows, d = x.shape
    return call(
        result_kernel, info, (*in_hbm(x, *prod), *vo, *in_hbm(bias)), [const(rows, d), img(WIN, w), img(WIN, w), side(d, w, 1), side(d, w, 1), const(d)],
        [shape((rows, d), BF)], [const(rows, d)], [pltpu.VMEM((16, d), F32)], grid=(n,), name="result", after=after, us=1, vmem=10,
    )[0]


def grad_call(info, x, g, dpv, dpg, vo, wg, gain, after):
    n, _, w = dpv[0].shape
    rows, d = x.shape
    return call(
        grad_kernel, info, (*in_hbm(x, g, *dpv, dpg), *vo, *wg, *in_hbm(gain)),
        [const(rows, d), window_rows(d), img(WIN, w), img(WIN, w), img(WIN, 2 * w)] + [side(d, w, 0)] * 2 + [whole(wg[0]), whole(wg[1]), const(d)],
        [shape((rows, d), F32)], [const(rows, d)], [pltpu.VMEM((16, d), F32)], grid=(n,), name="input_grad", after=after, us=1, vmem=16,
    )[0]


VROWS = 32


def quarter_kernel(tensors, extra, info, *refs):
    if extra == "spatial":
        keep, recv, gsp, *outs = refs
    else:
        keep, recv, vown, *outs = refs
    x, y, core = info[2], info[3], info[4]
    d = keep.shape[0] // tensors
    c = keep.shape[1] // 2
    nz = 4
    r = d // (2 * nz)
    for a, out in enumerate(outs):
        for b in range(2):
            xr, yr = jnp.where(core == 0, b, a), jnp.where(core == 0, a, b)
            cols = pl.ds(pl.multiple_of(yr * c, c), c)
            for t in range(tensors):
                for z in range(nz):
                    row = pl.multiple_of(t * d + (2 * z + jnp.bitwise_xor(x, xr)) * r, r)
                    dst = t * nz * r + z * r
                    out[b, dst : dst + r, :] = (keep[pl.ds(row, r), cols] + recv[pl.ds(row, r), cols].astype(F32)).astype(out.dtype)
            at = tensors * nz * r
            if extra == "spatial":
                q = PAD // 4
                row = pl.multiple_of((2 * jnp.bitwise_xor(x, xr) + jnp.bitwise_xor(y, yr)) * q, q)
                out[b, at:, :] = gsp[pl.ds(row, q), :].astype(BF).astype(out.dtype)
            else:
                got = recv[d:, :].astype(F32)
                v = vown[...] + (got[:8] + got[8:])
                four = jnp.where(yr == 0, v[0:4, :c], v[0:4, c:])
                v = jnp.concatenate([four, v[4:7, :c], jnp.concatenate([v[4:7, c : c + 128], jnp.zeros((3, c - 128), F32)], 1), jnp.zeros((6, c), F32)], 0)
                out[b, at:, :] = both(v).astype(out.dtype)


def both(v):
    hi, lo = split(v)
    return jnp.concatenate([hi, lo], 0)


def rounded(v):
    return both(v[:16] + v[16:]) if v.shape[0] == VROWS else v.astype(BF)


def plane_kernel(extra, info, parts, recv, keep, send):
    m = keep.shape[0] - extra
    for b, out in enumerate((keep, send)):
        out[:m, :] = (parts[b, :m, :] + recv[b, :m, :].astype(F32)).astype(out.dtype)
        out[m:, :] = rounded(parts[b, m:, :] + recv[b, m:, :].astype(F32)).astype(out.dtype)


def line_kernel(tensors, chunks, extra, info, part, recv, keep, send):
    m = part.shape[0] - extra
    r = m // (tensors * chunks)
    h = chunks // 2
    bit = lax.rem(lax.div(info[1], h), 2)
    for out, which in ((keep, bit), (send, 1 - bit)):
        for t in range(tensors):
            rows = pl.ds(pl.multiple_of((t * chunks + which * h) * r, r), h * r)
            out[t * h * r : (t + 1) * h * r, :] = (part[rows, :] + recv[rows, :].astype(F32)).astype(out.dtype)
        out[tensors * h * r :, :] = rounded(part[m:, :] + recv[m:, :].astype(F32)).astype(out.dtype)


def finish_vo_kernel(info, part, recv, gwv, gwo, sp):
    r = gwv.shape[0]
    v = part[...] + recv[...].astype(F32)
    gwv[...] = v[:r]
    gwo[...] = v[r : 2 * r]
    sp[...] = v[2 * r :].astype(BF)


def finish_g_kernel(info, part, recv, gain, shift, gwg, gbv, gbg, ggain, gshift, rows):
    r = gwg.shape[0]
    v = part[...] + recv[...].astype(F32)
    gwg[...] = v[:r]
    v = v[r : r + 16] + v[r + 16 :]
    for k, out in enumerate((gbv, gbg, ggain, gshift)):
        out[...] = v[k]
    full = jnp.concatenate([v[4:7, :], v[7:10, :128]], 1)
    gin = (full[0:1, :] - shift[...][None] * full[1:2, :]) / gain[...][None]
    rows[...] = jnp.concatenate([gin, full[1:], jnp.zeros((5, full.shape[1]), F32)], 0)


def pair_kernel(info, a, b, out):
    out[...] = (a[...].astype(F32) + b[...].astype(F32)).astype(BF)


def spatial_kernel(info, a, rx, ry, rxy, mine, other, out, bias, gin, sin, gout, full):
    q = a.shape[0]
    for ref, k in ((a, 0), (ry, 1), (rx, 2), (rxy, 3)):
        full[pl.ds(pl.multiple_of(jnp.bitwise_xor(2 * info[2] + info[3], k) * q, q), q), :] = ref[...].astype(F32)
    p = out.shape[0]
    out[...] = full[:p, :p]
    bias[...] = full[:, 256:].T[WIN - 256, :p]
    v = jnp.where(info[4] == 0, mine[...], other[...])
    gin[...] = v[0]
    sin[...] = v[1]
    gout[...] = v[2]


def permute(x, to):
    n_dp, n_mp = lax.axis_size("dp"), lax.axis_size("mp")
    pairs = []
    for i in range(n_dp * n_mp):
        dp, mp = to(i // n_mp, i % n_mp)
        pairs.append((i, dp * n_mp + mp))
    return lax.ppermute(x, AXES, pairs)


def core_swap(x):
    return permute(x, lambda dp, mp: (dp, mp ^ 1))


def plane_swaps(a, b, c):
    return (
        permute(a, lambda dp, mp: (dp ^ 1, mp)),
        permute(b, lambda dp, mp: (dp, mp ^ 2)),
        permute(c, lambda dp, mp: (dp ^ 1, mp ^ 2)),
    )


def first_swap(x):
    return permute(x, lambda dp, mp: (dp, mp ^ 2) if mp % 2 == 0 else (dp ^ 1, mp))


def second_swap(x):
    return permute(x, lambda dp, mp: (dp ^ 1, mp) if mp % 2 == 0 else (dp, mp ^ 2))


def z_swap(x, bit):
    return permute(x, lambda dp, mp: (dp ^ (2 * bit), mp))


def line_swaps(arrays):
    n_dp = lax.axis_size("dp")
    return [permute(a, lambda dp, mp, k=k: ((dp + 2 * (k + 1)) % n_dp, mp)) for k, a in enumerate(arrays)]


def gather_dp(copies):
    t = lax.all_to_all(copies, "dp", 0, 0, tiled=True)
    return t.reshape(-1, t.shape[2])


def after(x, y):
    return lax.optimization_barrier((x, y))


def y_swap(x):
    return permute(x, lambda dp, mp: (dp, mp ^ 2))


def scatter_any(keep, recv):
    n = lax.axis_size("dp")
    c = keep.shape[1] // 2
    a = keep + recv.astype(F32)
    s = a[:, :c] + permute(a[:, c:].astype(BF), lambda dp, mp: (dp, mp ^ 2)).astype(F32)
    return lax.all_to_all(s.astype(BF).reshape(n, -1, c), "dp", 0, 0, tiled=True).astype(F32).sum(0)


def body(inputs, counts, input_norm_gain, shift_in, w_value, w_gate, bias_value, bias_gate, gate_gain, gate_shift, spatial, spatial_bias, w_out, out_bias, cotangent):
    n_dp, n_mp = lax.axis_size("dp"), lax.axis_size("mp")
    me, dp = lax.axis_index("mp"), lax.axis_index("dp")
    r, c = w_value.shape
    d = inputs.shape[1]
    p = spatial.shape[0]
    n = counts.shape[0] // n_mp
    quick = n_dp == 8 and r % 16 == 0
    head = jnp.stack([me, dp // 2, dp % 2, me // 2, me % 2, me * n, 0, 0]).astype(jnp.int32)
    info = jnp.concatenate([head, counts])

    args = in_hbm(w_gate, w_value, w_out.T, bias_value, bias_gate, gate_gain, gate_shift)
    pg, vo1, vec = simple_call(cast_kernel, info, args, [shape((r, c), BF), shape((r, 2 * c), BF), shape((16, c), BF)], "casts")
    if quick:
        zg, zvo = line_swaps([pg] * 3), line_swaps([vo1] * 3)
        zg = stack_call(info, (pg, *zg, vec), (), "line_gate")
        pieces = (zg, *plane_swaps(zg, zg, zg))
    else:
        copies = lambda a: gather_dp(jnp.broadcast_to(a[None], (n_dp,) + a.shape))
        g0 = jnp.concatenate([copies(pg), vec])
        zg = wga = jnp.concatenate([g0, y_swap(g0)], 1)
        vo0 = copies(vo1)
        vo2 = y_swap(vo0)
        zvo = ()
        voa = jnp.concatenate([vo0[:, :c], vo2[:, :c], vo0[:, c:], vo2[:, c:]], 1)
    normed, gsum = norm_call(info, inputs, cotangent, input_norm_gain, shift_in, n, (zg,))
    s, st, sb, token = windows_call(info, spatial, spatial_bias, n, (gsum, *zvo))
    if quick:
        wga = assemble_call(info, pieces, 1, 16, (token,), "assemble_gate")
        zvo = stack_call(info, (vo1, *zvo), (wga,), "line_value_out")
        pieces = (zvo, *plane_swaps(zvo, zvo, zvo))
    wgb = core_swap(wga)
    rows, hat, slope, inv, shifted, vec = gate_call(info, (wga, wgb), normed, s, sb, (zvo,) if quick else ())
    if quick:
        voa = assemble_call(info, pieces, 2, 0, (vec,), "assemble_value_out")
    vob = core_swap(voa)
    zero = jnp.zeros((PAD, PAD), F32)
    prod_b, ds_b, dpv_b, gw_b, gb_b, gsp, small_b = value_call(info, 1, False, vob, normed, cotangent, vec, shifted, rows, zero)
    recv_vo = core_swap(gw_b)
    prod_a, ds_a, dpv_a, gw_a, gb_a, gsp, small_a = value_call(info, 0, True, voa, normed, cotangent, vec, shifted, rows, gsp)
    q = PAD // 4
    def quarters(tensors, extra, args, rows, name, after):
        return simple_call(lambda *a: quarter_kernel(tensors, extra, *a), info, args, [shape((2, rows, c), F32), shape((2, rows, c), BF)], name, after=after)

    def plane(parts, recv, extra, name, after):
        s = parts.shape[1:]
        return simple_call(lambda *a: plane_kernel(extra, *a), info, (parts, recv), [shape(s, F32), shape(s, BF)], name, after=after)

    def line(part, recv, tensors, chunks, extra, name, after):
        s = ((part.shape[0] - extra) // 2 + extra, c)
        return simple_call(lambda *a: line_kernel(tensors, chunks, extra, *a), info, (part, recv), [shape(s, F32), shape(s, BF)], name, after=after)

    if quick:
        kvo, snd = quarters(2, "spatial", (gw_a, recv_vo, gsp), 8 * r + q, "quarters_vo", ())
        got_vo = first_swap(snd)
    dpg, keep_g, send_g, vown = back_call(info, normed, (ds_a, ds_b), hat, slope, inv, st, vec, (wga, wgb), (gb_a, gb_b), (small_a, small_b), gsum, (snd,) if quick else ())
    recv_g = core_swap(send_g)
    if quick:
        kvo, snd = plane(kvo, got_vo, q, "plane_vo", (vown,))
        got_vo = second_swap(snd)
    res = result_call(info, inputs, (prod_a, prod_b), (voa, vob), out_bias, (snd if quick else vown,))
    if quick:
        kg, snd = quarters(1, "vectors", (keep_g, recv_g, vown), 4 * r + VROWS, "quarters_g", (res,))
        got_g = first_swap(snd)
        kvo, snd = line(kvo, got_vo, 2, 4, q, "line_vo", (snd,))
        got_vo = z_swap(snd, 2)
        kg, snd = plane(kg, got_g, VROWS, "plane_g", (snd,))
        got_g = second_swap(snd)
        ing = grad_call(info, inputs, cotangent, (dpv_a, dpv_b), dpg, (voa, vob), (wga, wgb), input_norm_gain, (snd,))
        kg, snd = line(kg, got_g, 1, 4, VROWS, "line_g", (ing,))
        got_g = z_swap(snd, 2)
        kvo, snd = line(kvo, got_vo, 2, 2, q, "pair_vo", (snd,))
        got_vo = z_swap(snd, 1)
        kg, snd = line(kg, got_g, 1, 2, VROWS, "pair_g", (snd,))
        got_g = z_swap(snd, 1)
        gwv, gwo, sp = simple_call(finish_vo_kernel, info, (kvo, got_vo), [shape((r, c), F32), shape((r, c), F32), shape((q, c), BF)], "finish_vo", after=(snd,))
        (sp,) = simple_call(pair_kernel, info, (sp, core_swap(sp)), [shape((q, c), BF)], "spatial_pair")
        sps = plane_swaps(sp, sp, sp)
        one = shape((c,), F32)
        gwg, gbv, gbg, ggain, gshift, full = simple_call(
            finish_g_kernel, info, (kg, got_g, *in_hbm(input_norm_gain, shift_in)),
            [shape((r, c), F32)] + [one] * 4 + [shape((8, d), F32)], "finish_g", after=(sp,))
        gspat, gsb, gin, sin, gob = simple_call(spatial_kernel, info, (sp, *sps, full, core_swap(full)), [shape((p, p), F32), shape((p,), F32)] + [shape((d,), F32)] * 3, "spatial_sum", [pltpu.VMEM((PAD, PAD), F32)], after=(gwg,))
    else:
        ing = grad_call(info, inputs, cotangent, (dpv_a, dpv_b), dpg, (voa, vob), (wga, wgb), input_norm_gain, ())
        gwv = scatter_any(gw_a[:d], recv_vo[:d])
        gwo = scatter_any(gw_a[d:], recv_vo[d:])
        gwg = scatter_any(keep_g, recv_g[:d])
        gsp = lax.psum(gsp, AXES)
        gspat, gsb = gsp[:p, :p], gsp[:p, WIN]
        other = send_g[d:].astype(F32)
        other = other[:8] + other[8:]
        back = jnp.argsort(jnp.bitwise_xor(jnp.array(ORDER, jnp.int32), me))
        four = jnp.concatenate([vown[:4], other[:4]], 1).reshape(4, n_mp, c)
        four = lax.psum(jnp.take(four, back, axis=1), AXES)
        gbv, gbg, ggain, gshift = lax.dynamic_index_in_dim(four, me, 1, keepdims=False)
        t, sin, gob = lax.psum(vown[4:7, :d], AXES)
        gin = (t - shift_in * sin) / input_norm_gain
    return (res, ing, gin, sin, gwv, gwg, gbv, gbg, ggain, gshift, gspat, gsb, gwo.T, gob)


def solution(mesh):
    row, wi, mp, al = P(("dp", "mp"), None), P("dp", "mp"), P("mp"), P()
    return jax.shard_map(
        body, mesh=mesh,
        in_specs=(row, P("dp"), al, al, wi, wi, mp, mp, mp, mp, al, al, P("mp", "dp"), al, row),
        out_specs=(row, row, al, al, wi, wi, mp, mp, mp, mp, al, al, P("mp", "dp"), al),
        check_vma=False,
    )
```

time: 548 us -> 162 us (0.30); the launches traced: 538 us -> 161 us
  blocking collectives: 190 us -> 0 us
  Pallas kernels: 0 us -> 102 us
  waiting for transfers between devices: 115 us -> 21.4 us
  other arithmetic: 86.5 us -> 0 us
  matrix products: 80.2 us -> 0 us
  local copies, waits for them, and re-layouts: 40.2 us -> 4.74 us
  starting transfers between devices: 11.1 us -> 31.9 us
  between operations: 14.6 us -> 0.86 us
    pallas_call x0 -> x25, Pallas kernels: none -> 102 us  [call(): pl.pallas_call(ordered, grid_spec=pltpu.PrefetchScalarGridSpec(num_scalar...]
    all_gather x3 -> x0, blocking collectives: 95.3 us -> none  [the longest x1 33 us: body(): lax.all_gather(w_value.astype(jnp.bfloat16), 'dp', axis=0, tiled=True)]
    psum x5 -> x0, blocking collectives: 94.6 us -> none  [the longest x1 39.5 us: body(): lax.psum((grad_spatial, grad_spatial_bias, grad_gain_part, grad_shift_par...]
    psum x1 -> x0, waiting for transfers between devices: 89.4 us -> none  [body(): lax.psum((grad_spatial, grad_spatial_bias, grad_gain_part, grad_shift_par...]
    dot_general x9 -> x0, matrix products: 80.2 us -> none  [the longest x1 24.7 us: body(): lax.dot_general(tangent_all, out_w, (((1,), (1,)), ((), ())), preferred_e...]
    reduce_sum x13 -> x0, other arithmetic: 74.4 us -> none  [the longest x1 19.7 us: body(): gate_sum_total = lax.psum(jnp.sum(gate_act, -1, keepdims=True), 'mp')]
    ppermute x0 -> x29, starting transfers between devices: none -> 31.9 us  [permute(): return lax.ppermute(x, AXES, pairs)]
    reduce_scatter x2 -> x0, waiting for transfers between devices: 24.5 us -> none  [the longest x1 24.5 us: body(): lax.psum_scatter(jnp.dot(slab_rows, out_w, preferred_element_type=jnp.flo...]
  transfers between devices with their start and end apart: 7 -> 29, of which waited for: 3 -> 11; matrix products, arithmetic and copies ran while one was open for 20% -> 0% of each run, Pallas kernels for 0% -> 50%
where the time goes in v2:
time: 162 us; the launch traced here: 161 us
  Pallas kernels  102 us (63%)
  starting transfers between devices  31.9 us (20%)
  waiting for transfers between devices  21.4 us (13%)
  local copies, waits for them, and re-layouts  4.74 us (3%)
    pallas_call x25, Pallas kernels, call(): pl.pallas_call(ordered, grid_spec=pltpu.PrefetchScalarGridSpec(num_scalar...  102 us
    ppermute x29, starting transfers between devices, permute(): return lax.ppermute(x, AXES, pairs)  31.9 us
    ppermute x29, waiting for transfers between devices, permute(): return lax.ppermute(x, AXES, pairs)  21.4 us
    unnamed x6, local copies, waits for them, and re-layouts  3.96 us
  transfers between devices with their start and end apart: 29, of which 11 were waited for; matrix products, arithmetic and copies ran while one was open for 0% of the time, Pallas kernels for 50%

profile of v2, /device:TPU:0, one launch (start us, length us, event | category | flops | bytes accessed | tf_op | source)
XLA Modules:
  0.0 161.0 jit_solution(5310554527937344712)
XLA Ops:
  0.7 0.7 concatenate.3.info_ref
  1.4 1.6 casts.1
  3.0 5.1 %collective-permute-start.5 = (bf16[64,384]{1,0:T(8,128)(2,1)S(1)}, bf16[64,384]{1,0:T(8,128)(2,1)S(1)}, u32[]{:S(2)}, u32[]{:S(2)}) collective-permute-start(bf16[64,384]{1,0:T(8,128)(2,1)S(1)} %get-tuple-element.78.refs_0_), channel_id=1, source_target_pairs={{0,24},{1,25},{2,26},{3,27},{4,28},{5,29},{6,30},{7,31},{8,0},{9,1... | collective-permute-start | bytes 147464 | tf_op jit(solution)/shard_map/ppermute | solution.py:589
  8.1 1.0 collective-permute-start.3
  9.1 2.8 %collective-permute-start.2 = (bf16[64,768]{1,0:T(8,128)(2,1)S(1)}, bf16[64,768]{1,0:T(8,128)(2,1)S(1)}, u32[]{:S(2)}, u32[]{:S(2)}) collective-permute-start(bf16[64,768]{1,0:T(8,128)(2,1)S(1)} %get-tuple-element.77.refs_0_), channel_id=1, source_target_pairs={{0,24},{1,25},{2,26},{3,27},{4,28},{5,29},{6,30},{7,31},{8,0},{9,1... | collective-permute-start | bytes 294920 | tf_op jit(solution)/shard_map/ppermute | solution.py:589
  12.0 1.1 collective-permute-start.1
  13.7 1.0 collective-permute-done.3.refs_1_
  14.7 0.9 line_gate.1.refs_4_.refs_0_
  15.6 2.5 %collective-permute-start.8 = (bf16[272,384]{1,0:T(8,128)(2,1)S(1)}, bf16[272,384]{1,0:T(8,128)(2,1)S(1)}, u32[]{:S(2)}, u32[]{:S(2)}) collective-permute-start(bf16[272,384]{1,0:T(8,128)(2,1)S(1)} %line_gate.1.refs_4_.refs_0_), channel_id=1, source_target_pairs={{0,6},{1,7},{2,4},{3,5},{4,2},{5,3},{6,0},{7,1},{8,14},{9,15},{10,... | collective-permute-start | bytes 626696 | tf_op jit(solution)/shard_map/ppermute | solution.py:589
  19.1 4.8 %input_norm.1 = (bf16[4,336,512]{2,1,0:T(8,128)(2,1)}, f32[1,512]{1,0:T(1,128)S(1)}) custom-call(s32[24]{0:T(128)S(1)} %concatenate.3.info_ref, bf16[1296,512]{1,0:T(8,128)(2,1)} %refs_0_.9, bf16[1296,512]{1,0:T(8,128)(2,1)} %refs_1_.7, f32[512]{0:T(512)} %refs_2_.3, f32[512]{0:T(512)} %refs_3_.9, bf16[272,384]{1,0:T(8,128)(2,1)S(1)} %line_gate.1.refs_4_.refs_0_), custom_call_target="tpu_custom_call" | custom-call | flops 3300000000 | bytes 9900000 | tf_op jit(solution)/shard_map/input_norm/pallas_call | solution.py:100
  24.0 4.6 %windows.1 = (bf16[4,336,336]{2,1,0:T(8,128)(2,1)}, bf16[4,336,336]{2,1,0:T(8,128)(2,1)}, f32[4,336,128]{2,1,0:T(8,128)}, f32[8,128]{1,0:T(8,128)S(1)}) custom-call(s32[24]{0:T(128)S(1)} %concatenate.3.info_ref, f32[324,324]{1,0:T(8,128)} %refs_0_.7, f32[324]{0:T(512)} %refs_1_.6, f32[1,512]{1,0:T(1,128)S(1)} %get-tuple-element.80.refs_2_.refs_14_, ...), custom_call_target="tpu_custom_call" | custom-call | flops 2200000000 | bytes 6600000 | tf_op jit(solution)/shard_map/windows/pallas_call | solution.py:100
  28.6 0.9 assemble_gate.1.refs_4_.refs_0_.refs_8_.refs_7_
  29.6 1.1 line_value_out.1.refs_5_.refs_0_
  30.7 2.5 %collective-permute-start.11 = (bf16[256,768]{1,0:T(8,128)(2,1)S(1)}, bf16[256,768]{1,0:T(8,128)(2,1)S(1)}, u32[]{:S(2)}, u32[]{:S(2)}) collective-permute-start(bf16[256,768]{1,0:T(8,128)(2,1)S(1)} %line_value_out.1.refs_5_.refs_0_), channel_id=1, source_target_pairs={{0,6},{1,7},{2,4},{3,5},{4,2},{5,3},{6,0},{7,1},{8,14},{9,15},{10,... | collective-permute-start | bytes 1179656 | tf_op jit(solution)/shard_map/ppermute | solution.py:589
  34.3 15.9 %gate_forward.1 = (bf16[4,352,1536]{2,1,0:T(8,128)(2,1)}, bf16[4,336,1536]{2,1,0:T(8,128)(2,1)}, bf16[4,336,1536]{2,1,0:T(8,128)(2,1)}, f32[4,336,128]{2,1,0:T(8...) custom-call(s32[24]{0:T(128)S(1)} %concatenate.3.info_ref, ...), custom_call_target="tpu_custom_call" | custom-call | flops 1100000000 | bytes 3300000 | tf_op jit(solution)/shard_map/gate_forward/pallas_call | solution.py:100
  50.2 1.4 collective-permute-done.10.refs_2_
  51.7 1.2 assemble_value_out.1.refs_0_.refs_1_.refs_3_.refs_5_
  53.0 3.4 %collective-permute-done.13.refs_0_.refs_1_.refs_4_.refs_6_ = bf16[512,1536]{1,0:T(8,128)(2,1)S(1)} collective-permute-done((bf16[512,1536]{1,0:T(8,128)(2,1)S(1)}, bf16[512,1536]{1,0:T(8,128)(2,1)S(1)}, u32[]{:S(2)}, u32[]{:S(2)}) %collective-permute-start.13) | collective-permute-done | bytes 1572896 | tf_op jit(solution)/shard_map/ppermute | solution.py:589
  56.4 14.2 %value_other.1 = (bf16[4,336,768]{2,1,0:T(8,128)(2,1)}, bf16[4,336,768]{2,1,0:T(8,128)(2,1)S(1)}, bf16[4,336,768]{2,1,0:T(8,128)(2,1)}, bf16[1024,768]{1,0:T(8,1...) custom-call(s32[24]{0:T(128)S(1)} %concatenate.3.info_ref, ...), custom_call_target="tpu_custom_call" | custom-call | flops 1100000000 | bytes 3300000 | tf_op jit(solution)/shard_map/value_other/pallas_call | solution.py:100
  70.7 14.4 %value_own.1 = (bf16[4,336,768]{2,1,0:T(8,128)(2,1)}, bf16[4,336,768]{2,1,0:T(8,128)(2,1)S(1)}, bf16[4,336,768]{2,1,0:T(8,128)(2,1)}, f32[1024,768]{1,0:T(8,128)...) custom-call(s32[24]{0:T(128)S(1)} %concatenate.3.info_ref, ...), custom_call_target="tpu_custom_call" | custom-call | flops 1100000000 | bytes 3300000 | tf_op jit(solution)/shard_map/value_own/pallas_call | solution.py:100
  85.1 0.9 quarters_vo.1
  86.0 1.5 collective-permute-start.15
  87.4 13.8 %gate_backward.1 = (bf16[4,336,1536]{2,1,0:T(8,128)(2,1)}, f32[512,768]{1,0:T(8,128)S(1)}, bf16[528,768]{1,0:T(8,128)(2,1)S(1)}, f32[8,768]{1,0:T(8,128)S(1)}) custom-call(s32[24]{0:T(128)S(1)} %concatenate.3.info_ref, bf16[4,336,512]{2,1,0:T(8,128)(2,1)} %get-tuple-element.82.refs_2_.refs_0_, bf16[4,336,768]{2,1,0:T(8,128)(2,1)S(1)} %get-tuple-element.96.refs_1_, ...), custom_call_target="tpu_custom_call" | custom-call | flops 1100000000 | bytes 3300000 | tf_op jit(solution)/shard_map/gate_backward/pallas_call | solution.py:100
  101.3 0.7 plane_vo.1
  102.0 0.7 collective-permute-start.18
  102.8 7.0 %result.1.refs_3_ = bf16[1296,512]{1,0:T(8,128)(2,1)} custom-call(s32[24]{0:T(128)S(1)} %concatenate.3.info_ref, bf16[1296,512]{1,0:T(8,128)(2,1)} %refs_0_.9, bf16[4,336,768]{2,1,0:T(8,128)(2,1)} %get-tuple-element.89.refs_1_, bf16[4,336,768]{2,1,0:T(8,128)(2,1)} %get-tuple-element.90.refs_2_, ...), custom_call_target="tpu_custom_call" | custom-call | flops 1100000000 | bytes 3300000 | tf_op jit(solution)/shard_map/result/pallas_call | solution.py:100
  109.8 1.3 copy-done.1
  111.1 0.7 quarters_g.1
  111.9 1.4 collective-permute-start.17
  113.3 0.7 line_vo.1
  113.9 6.3 %collective-permute-done.17.refs_1_ = bf16[2,288,384]{2,1,0:T(8,128)(2,1)S(1)} collective-permute-done((bf16[2,288,384]{2,1,0:T(8,128)(2,1)S(1)}, bf16[2,288,384]{2,1,0:T(8,128)(2,1)S(1)}, u32[]{:S(2)}, u32[]{:S(2)}) %collective-permute-start.17) | collective-permute-done | bytes 442400 | tf_op jit(solution)/shard_map/ppermute | solution.py:589
  120.2 0.6 plane_g.1
  120.9 1.4 collective-permute-start.20
  122.3 4.5 %collective-permute-start.19 = (bf16[352,384]{1,0:T(8,128)(2,1)S(1)}, bf16[352,384]{1,0:T(8,128)(2,1)S(1)}, u32[]{:S(2)}, u32[]{:S(2)}) collective-permute-start(bf16[352,384]{1,0:T(8,128)(2,1)S(1)} %get-tuple-element.116.refs_2_), channel_id=1, source_target_pairs={{0,16},{1,17},{2,18},{3,19},{4,20},{5,21},{6,22},{7,23},{8,24},{9,... | collective-permute-start | bytes 811016 | tf_op jit(solution)/shard_map/ppermute | solution.py:589
  126.8 11.2 %input_grad.1.refs_2_ = f32[1296,512]{1,0:T(8,128)} custom-call(s32[24]{0:T(128)S(1)} %concatenate.3.info_ref, bf16[1296,512]{1,0:T(8,128)(2,1)} %refs_0_.9, bf16[1296,512]{1,0:T(8,128)(2,1)} %refs_1_.7, bf16[4,336,768]{2,1,0:T(8,128)(2,1)} %get-tuple-element.108.refs_2_, bf16[4,336,768]{2,1,0:T(8,128)(2,1)} %get-tuple-element.109.refs_3_, ...), custom_call_target="tpu_custom_call" | custom-call | flops 1100000000 | bytes 3300000 | tf_op jit(solution)/shard_map/input_grad/pallas_call | solution.py:100
  138.1 1.7 %copy-done = f32[1296,512]{1,0:T(8,128)S(1)} copy-done((f32[1296,512]{1,0:T(8,128)S(1)}, f32[1296,512]{1,0:T(8,128)}, u32[]{:S(2)}) %copy-start) | copy-done | bytes 2654232
  141.1 1.2 collective-permute-start.21
  142.3 4.4 %collective-permute-done.22.refs_1_ = bf16[160,384]{1,0:T(8,128)(2,1)S(1)} collective-permute-done((bf16[160,384]{1,0:T(8,128)(2,1)S(1)}, bf16[160,384]{1,0:T(8,128)(2,1)S(1)}, u32[]{:S(2)}, u32[]{:S(2)}) %collective-permute-start.22) | collective-permute-done | bytes 122912 | tf_op jit(solution)/shard_map/ppermute | solution.py:589
  147.2 1.5 collective-permute-done.21.refs_1_
  148.7 1.2 finish_vo.1
  150.0 1.3 collective-permute-done.23.refs_1_
  151.8 1.6 collective-permute-start.26
  153.4 0.7 collective-permute-start.25
  154.2 1.2 collective-permute-start.24
  155.4 1.9 %finish_g.1 = (f32[64,384]{1,0:T(8,128)}, f32[384]{0:T(512)}, f32[384]{0:T(512)}, f32[384]{0:T(512)}, f32[384]{0:T(512)}, /*index=5*/f32[8,512]{1,0:T(8,128)S(1)}) custom-call(s32[24]{0:T(128)S(1)} %concatenate.3.info_ref, f32[96,384]{1,0:T(8,128)S(1)} %get-tuple-element.126.refs_0_, bf16[96,384]{1,0:T(8,128)(2,1)S(1)} %collective-permute-done.27.refs_1_, ...), custom_call_target="tpu_custom_call" | custom-call | flops 1100000000 | bytes 3300000 | tf_op jit(solution)/shard_map/finish_g/pallas_call | solution.py:100
  157.3 1.2 collective-permute-done.28.refs_5_
  158.7 0.9 copy-done.2
  159.6 1.4 spatial_sum.1
  (44 shorter events, 5.9 us)
Async XLA Ops:
  3.0 10.1 %collective-permute-start.5 = (bf16[64,384]{1,0:T(8,128)(2,1)S(1)}, bf16[64,384]{1,0:T(8,128)(2,1)S(1)}, u32[]{:S(2)}, u32[]{:S(2)}) collective-permute-start(bf16[64,384]{1,0:T(8,128)(2,1)S(1)} %get-tuple-element.78.refs_0_), channel_id=1, source_target_pairs={{0,24},{1,25},{2,26},{3,27},{4,28},{5,29},{6,30},{7,31},{8,0},{9,1... | collective-permute-start | bytes 147464 | tf_op jit(solution)/shard_map/ppermute | solution.py:589
  8.1 5.6 %collective-permute-start.4 = (bf16[64,384]{1,0:T(8,128)(2,1)S(1)}, bf16[64,384]{1,0:T(8,128)(2,1)S(1)}, u32[]{:S(2)}, u32[]{:S(2)}) collective-permute-start(bf16[64,384]{1,0:T(8,128)(2,1)S(1)} %get-tuple-element.78.refs_0_), channel_id=1, source_target_pairs={{0,16},{1,17},{2,18},{3,19},{4,20},{5,21},{6,22},{7,23},{8,24},{9,... | collective-permute-start | bytes 147464 | tf_op jit(solution)/shard_map/ppermute | solution.py:589
  8.1 6.6 %collective-permute-start.3 = (bf16[64,384]{1,0:T(8,128)(2,1)S(1)}, bf16[64,384]{1,0:T(8,128)(2,1)S(1)}, u32[]{:S(2)}, u32[]{:S(2)}) collective-permute-start(bf16[64,384]{1,0:T(8,128)(2,1)S(1)} %get-tuple-element.78.refs_0_), channel_id=1, source_target_pairs={{0,8},{1,9},{2,10},{3,11},{4,12},{5,13},{6,14},{7,15},{8,16},{9,17... | collective-permute-start | bytes 147464 | tf_op jit(solution)/shard_map/ppermute | solution.py:589
  9.1 9.4 %collective-permute-start.2 = (bf16[64,768]{1,0:T(8,128)(2,1)S(1)}, bf16[64,768]{1,0:T(8,128)(2,1)S(1)}, u32[]{:S(2)}, u32[]{:S(2)}) collective-permute-start(bf16[64,768]{1,0:T(8,128)(2,1)S(1)} %get-tuple-element.77.refs_0_), channel_id=1, source_target_pairs={{0,24},{1,25},{2,26},{3,27},{4,28},{5,29},{6,30},{7,31},{8,0},{9,1... | collective-permute-start | bytes 294920 | tf_op jit(solution)/shard_map/ppermute | solution.py:589
  12.0 12.0 %collective-permute-start.1 = (bf16[64,768]{1,0:T(8,128)(2,1)S(1)}, bf16[64,768]{1,0:T(8,128)(2,1)S(1)}, u32[]{:S(2)}, u32[]{:S(2)}) collective-permute-start(bf16[64,768]{1,0:T(8,128)(2,1)S(1)} %get-tuple-element.77.refs_0_), channel_id=1, source_target_pairs={{0,16},{1,17},{2,18},{3,19},{4,20},{5,21},{6,22},{7,23},{8,24},{9,... | collective-permute-start | bytes 294920 | tf_op jit(solution)/shard_map/ppermute | solution.py:589
  13.1 10.9 %collective-permute-start = (bf16[64,768]{1,0:T(8,128)(2,1)S(1)}, bf16[64,768]{1,0:T(8,128)(2,1)S(1)}, u32[]{:S(2)}, u32[]{:S(2)}) collective-permute-start(bf16[64,768]{1,0:T(8,128)(2,1)S(1)} %get-tuple-element.77.refs_0_), channel_id=1, source_target_pairs={{0,8},{1,9},{2,10},{3,11},{4,12},{5,13},{6,14},{7,15},{8,16},{9,17... | collective-permute-start | bytes 294920 | tf_op jit(solution)/shard_map/ppermute | solution.py:589
  15.6 13.1 %collective-permute-start.8 = (bf16[272,384]{1,0:T(8,128)(2,1)S(1)}, bf16[272,384]{1,0:T(8,128)(2,1)S(1)}, u32[]{:S(2)}, u32[]{:S(2)}) collective-permute-start(bf16[272,384]{1,0:T(8,128)(2,1)S(1)} %line_gate.1.refs_4_.refs_0_), channel_id=1, source_target_pairs={{0,6},{1,7},{2,4},{3,5},{4,2},{5,3},{6,0},{7,1},{8,14},{9,15},{10,... | collective-permute-start | bytes 626696 | tf_op jit(solution)/shard_map/ppermute | solution.py:589
  18.1 10.5 %collective-permute-start.7 = (bf16[272,384]{1,0:T(8,128)(2,1)S(1)}, bf16[272,384]{1,0:T(8,128)(2,1)S(1)}, u32[]{:S(2)}, u32[]{:S(2)}) collective-permute-start(bf16[272,384]{1,0:T(8,128)(2,1)S(1)} %line_gate.1.refs_4_.refs_0_), channel_id=1, source_target_pairs={{0,2},{1,3},{2,0},{3,1},{4,6},{5,7},{6,4},{7,5},{8,10},{9,11},{10,... | collective-permute-start | bytes 626696 | tf_op jit(solution)/shard_map/ppermute | solution.py:589
  18.6 10.0 %collective-permute-start.6 = (bf16[272,384]{1,0:T(8,128)(2,1)S(1)}, bf16[272,384]{1,0:T(8,128)(2,1)S(1)}, u32[]{:S(2)}, u32[]{:S(2)}) collective-permute-start(bf16[272,384]{1,0:T(8,128)(2,1)S(1)} %line_gate.1.refs_4_.refs_0_), channel_id=1, source_target_pairs={{0,4},{1,5},{2,6},{3,7},{4,0},{5,1},{6,2},{7,3},{8,12},{9,13},{10,... | collective-permute-start | bytes 626696 | tf_op jit(solution)/shard_map/ppermute | solution.py:589
  29.5 4.7 %collective-permute-start.12 = (bf16[528,768]{1,0:T(8,128)(2,1)S(1)}, bf16[528,768]{1,0:T(8,128)(2,1)S(1)}, u32[]{:S(2)}, u32[]{:S(2)}) collective-permute-start(bf16[528,768]{1,0:T(8,128)(2,1)S(1)} %assemble_gate.1.refs_4_.refs_0_.refs_8_.refs_7_), channel_id=1, source_target_pairs={{0,1},{1,0},{2,3},{3,2},{4,5},{5,4},{6,7},{7,6},{8,9},{9,8},{10,11... | collective-permute-start | bytes 2433032 | tf_op jit(solution)/shard_map/ppermute | solution.py:589
  30.7 19.5 %collective-permute-start.11 = (bf16[256,768]{1,0:T(8,128)(2,1)S(1)}, bf16[256,768]{1,0:T(8,128)(2,1)S(1)}, u32[]{:S(2)}, u32[]{:S(2)}) collective-permute-start(bf16[256,768]{1,0:T(8,128)(2,1)S(1)} %line_value_out.1.refs_5_.refs_0_), channel_id=1, source_target_pairs={{0,6},{1,7},{2,4},{3,5},{4,2},{5,3},{6,0},{7,1},{8,14},{9,15},{10,... | collective-permute-start | bytes 1179656 | tf_op jit(solution)/shard_map/ppermute | solution.py:589
  33.2 18.4 %collective-permute-start.10 = (bf16[256,768]{1,0:T(8,128)(2,1)S(1)}, bf16[256,768]{1,0:T(8,128)(2,1)S(1)}, u32[]{:S(2)}, u32[]{:S(2)}) collective-permute-start(bf16[256,768]{1,0:T(8,128)(2,1)S(1)} %line_value_out.1.refs_5_.refs_0_), channel_id=1, source_target_pairs={{0,2},{1,3},{2,0},{3,1},{4,6},{5,7},{6,4},{7,5},{8,10},{9,11},{10,... | collective-permute-start | bytes 1179656 | tf_op jit(solution)/shard_map/ppermute | solution.py:589
  33.7 18.0 %collective-permute-start.9 = (bf16[256,768]{1,0:T(8,128)(2,1)S(1)}, bf16[256,768]{1,0:T(8,128)(2,1)S(1)}, u32[]{:S(2)}, u32[]{:S(2)}) collective-permute-start(bf16[256,768]{1,0:T(8,128)(2,1)S(1)} %line_value_out.1.refs_5_.refs_0_), channel_id=1, source_target_pairs={{0,4},{1,5},{2,6},{3,7},{4,0},{5,1},{6,2},{7,3},{8,12},{9,13},{10,... | collective-permute-start | bytes 1179656 | tf_op jit(solution)/shard_map/ppermute | solution.py:589
  52.9 3.5 %collective-permute-start.13 = (bf16[512,1536]{1,0:T(8,128)(2,1)S(1)}, bf16[512,1536]{1,0:T(8,128)(2,1)S(1)}, u32[]{:S(2)}, u32[]{:S(2)}) collective-permute-start(bf16[512,1536]{1,0:T(8,128)(2,1)S(1)} %assemble_value_out.1.refs_0_.refs_1_.refs_3_.refs_5_), channel_id=1, source_target_pairs={{0,1},{1,0},{2,3},{3,2},{4,5},{5,4},{6,7},{7,6},{8,9},{9,8},{10,11... | collective-permute-start | bytes 4718600 | tf_op jit(solution)/shard_map/ppermute | solution.py:589
  70.6 14.5 %collective-permute-start.14 = (bf16[1024,768]{1,0:T(8,128)(2,1)S(1)}, bf16[1024,768]{1,0:T(8,128)(2,1)S(1)}, u32[]{:S(2)}, u32[]{:S(2)}) collective-permute-start(bf16[1024,768]{1,0:T(8,128)(2,1)S(1)} %get-tuple-element.92), channel_id=1, source_target_pairs={{0,1},{1,0},{2,3},{3,2},{4,5},{5,4},{6,7},{7,6},{8,9},{9,8},{10,11... | collective-permute-start | bytes 4718600 | tf_op jit(solution)/shard_map/ppermute | solution.py:589
  86.0 15.4 %collective-permute-start.15 = (bf16[2,608,384]{2,1,0:T(8,128)(2,1)S(1)}, bf16[2,608,384]{2,1,0:T(8,128)(2,1)S(1)}, u32[]{:S(2)}, u32[]{:S(2)}) collective-permute-start(bf16[2,608,384]{2,1,0:T(8,128)(2,1)S(1)} %get-tuple-element.95.refs_15_), channel_id=1, source_target_pairs={{0,2},{1,5},{2,0},{3,7},{4,6},{5,1},{6,4},{7,3},{8,10},{9,13},{10,... | collective-permute-start | bytes 2801672 | tf_op jit(solution)/shard_map/ppermute | solution.py:589
  101.2 8.6 %collective-permute-start.16 = (bf16[528,768]{1,0:T(8,128)(2,1)S(1)}, bf16[528,768]{1,0:T(8,128)(2,1)S(1)}, u32[]{:S(2)}, u32[]{:S(2)}) collective-permute-start(bf16[528,768]{1,0:T(8,128)(2,1)S(1)} %get-tuple-element.112), channel_id=1, source_target_pairs={{0,1},{1,0},{2,3},{3,2},{4,5},{5,4},{6,7},{7,6},{8,9},{9,8},{10,11... | collective-permute-start | bytes 2433032 | tf_op jit(solution)/shard_map/ppermute | solution.py:589
  102.0 11.2 %collective-permute-start.18 = (bf16[608,384]{1,0:T(8,128)(2,1)S(1)}, bf16[608,384]{1,0:T(8,128)(2,1)S(1)}, u32[]{:S(2)}, u32[]{:S(2)}) collective-permute-start(bf16[608,384]{1,0:T(8,128)(2,1)S(1)} %get-tuple-element.107.refs_6_), channel_id=1, source_target_pairs={{0,4},{1,3},{2,6},{3,1},{4,0},{5,7},{6,2},{7,5},{8,12},{9,11},{10,... | collective-permute-start | bytes 1400840 | tf_op jit(solution)/shard_map/ppermute | solution.py:589
  109.8 1.3 copy-start.1
  111.9 8.4 %collective-permute-start.17 = (bf16[2,288,384]{2,1,0:T(8,128)(2,1)S(1)}, bf16[2,288,384]{2,1,0:T(8,128)(2,1)S(1)}, u32[]{:S(2)}, u32[]{:S(2)}) collective-permute-start(bf16[2,288,384]{2,1,0:T(8,128)(2,1)S(1)} %get-tuple-element.114.refs_2_), channel_id=1, source_target_pairs={{0,2},{1,5},{2,0},{3,7},{4,6},{5,1},{6,4},{7,3},{8,10},{9,13},{10,... | collective-permute-start | bytes 1327112 | tf_op jit(solution)/shard_map/ppermute | solution.py:589
  120.9 17.2 %collective-permute-start.20 = (bf16[288,384]{1,0:T(8,128)(2,1)S(1)}, bf16[288,384]{1,0:T(8,128)(2,1)S(1)}, u32[]{:S(2)}, u32[]{:S(2)}) collective-permute-start(bf16[288,384]{1,0:T(8,128)(2,1)S(1)} %get-tuple-element.117.refs_10_), channel_id=1, source_target_pairs={{0,4},{1,3},{2,6},{3,1},{4,0},{5,7},{6,2},{7,5},{8,12},{9,11},{10,... | collective-permute-start | bytes 663560 | tf_op jit(solution)/shard_map/ppermute | solution.py:589
  122.3 18.2 %collective-permute-start.19 = (bf16[352,384]{1,0:T(8,128)(2,1)S(1)}, bf16[352,384]{1,0:T(8,128)(2,1)S(1)}, u32[]{:S(2)}, u32[]{:S(2)}) collective-permute-start(bf16[352,384]{1,0:T(8,128)(2,1)S(1)} %get-tuple-element.116.refs_2_), channel_id=1, source_target_pairs={{0,16},{1,17},{2,18},{3,19},{4,20},{5,21},{6,22},{7,23},{8,24},{9,... | collective-permute-start | bytes 811016 | tf_op jit(solution)/shard_map/ppermute | solution.py:589
  138.0 1.8 %copy-start = (f32[1296,512]{1,0:T(8,128)S(1)}, f32[1296,512]{1,0:T(8,128)}, u32[]{:S(2)}) copy-start(f32[1296,512]{1,0:T(8,128)} %input_grad.1.refs_2_) | copy-start | bytes 7962628
  140.4 6.3 %collective-permute-start.22 = (bf16[160,384]{1,0:T(8,128)(2,1)S(1)}, bf16[160,384]{1,0:T(8,128)(2,1)S(1)}, u32[]{:S(2)}, u32[]{:S(2)}) collective-permute-start(bf16[160,384]{1,0:T(8,128)(2,1)S(1)} %get-tuple-element.120.refs_2_), channel_id=1, source_target_pairs={{0,16},{1,17},{2,18},{3,19},{4,20},{5,21},{6,22},{7,23},{8,24},{9,... | collective-permute-start | bytes 368648 | tf_op jit(solution)/shard_map/ppermute | solution.py:589
  141.1 7.6 %collective-permute-start.21 = (bf16[224,384]{1,0:T(8,128)(2,1)S(1)}, bf16[224,384]{1,0:T(8,128)(2,1)S(1)}, u32[]{:S(2)}, u32[]{:S(2)}) collective-permute-start(bf16[224,384]{1,0:T(8,128)(2,1)S(1)} %get-tuple-element.122.refs_2_), channel_id=1, source_target_pairs={{0,8},{1,9},{2,10},{3,11},{4,12},{5,13},{6,14},{7,15},{8,0},{9,1},... | collective-permute-start | bytes 516104 | tf_op jit(solution)/shard_map/ppermute | solution.py:589
  150.0 1.3 collective-permute-start.23
  150.0 5.4 %collective-permute-start.27 = (bf16[96,384]{1,0:T(8,128)(2,1)S(1)}, bf16[96,384]{1,0:T(8,128)(2,1)S(1)}, u32[]{:S(2)}, u32[]{:S(2)}) collective-permute-start(bf16[96,384]{1,0:T(8,128)(2,1)S(1)} %get-tuple-element.124.refs_2_), channel_id=1, source_target_pairs={{0,8},{1,9},{2,10},{3,11},{4,12},{5,13},{6,14},{7,15},{8,0},{9,1},... | collective-permute-start | bytes 221192 | tf_op jit(solution)/shard_map/ppermute | solution.py:589
  151.8 6.6 %collective-permute-start.26 = (bf16[96,384]{1,0:T(8,128)(2,1)S(1)}, bf16[96,384]{1,0:T(8,128)(2,1)S(1)}, u32[]{:S(2)}, u32[]{:S(2)}) collective-permute-start(bf16[96,384]{1,0:T(8,128)(2,1)S(1)} %spatial_pair.1.refs_4_.refs_0_), channel_id=1, source_target_pairs={{0,6},{1,7},{2,4},{3,5},{4,2},{5,3},{6,0},{7,1},{8,14},{9,15},{10,... | collective-permute-start | bytes 221192 | tf_op jit(solution)/shard_map/ppermute | solution.py:589
  153.4 5.3 %collective-permute-start.25 = (bf16[96,384]{1,0:T(8,128)(2,1)S(1)}, bf16[96,384]{1,0:T(8,128)(2,1)S(1)}, u32[]{:S(2)}, u32[]{:S(2)}) collective-permute-start(bf16[96,384]{1,0:T(8,128)(2,1)S(1)} %spatial_pair.1.refs_4_.refs_0_), channel_id=1, source_target_pairs={{0,2},{1,3},{2,0},{3,1},{4,6},{5,7},{6,4},{7,5},{8,10},{9,11},{10,... | collective-permute-start | bytes 221192 | tf_op jit(solution)/shard_map/ppermute | solution.py:589
  154.2 4.5 %collective-permute-start.24 = (bf16[96,384]{1,0:T(8,128)(2,1)S(1)}, bf16[96,384]{1,0:T(8,128)(2,1)S(1)}, u32[]{:S(2)}, u32[]{:S(2)}) collective-permute-start(bf16[96,384]{1,0:T(8,128)(2,1)S(1)} %spatial_pair.1.refs_4_.refs_0_), channel_id=1, source_target_pairs={{0,4},{1,5},{2,6},{3,7},{4,0},{5,1},{6,2},{7,3},{8,12},{9,13},{10,... | collective-permute-start | bytes 221192 | tf_op jit(solution)/shard_map/ppermute | solution.py:589
  157.3 1.2 collective-permute-start.28
  158.7 0.9 copy-start.2

commit v3 on v2

--- a/solution.py
+++ b/solution.py
@@ -15,7 +15,7 @@
 CH = 16
 PAD = 384
 ORDER = (0, 2, 1, 3)
-GELU_C = (7.97882133e-01, 3.63449931e-02, -4.51808700e-05, -5.02619616e-05, 3.08533547e-06, -6.58149666e-08)
+GELU_C = (7.97869712e-01, 3.63922863e-02, -8.78266205e-05, -3.66934307e-05, 1.42500480e-06)
 LOG2E_HALF = -0.7213475204444817
 INV_SQRT_2PI = 0.3989422804014327
 MB = 2**20
@@ -35,10 +35,9 @@
 
 def gelu_both(x):
     u = x * x
-    um = jnp.minimum(u, 30.0)
-    p = GELU_C[5]
-    for c in GELU_C[4::-1]:
-        p = p * um + c
+    p = GELU_C[4]
+    for c in GELU_C[3::-1]:
+        p = p * u + c
     cdf = 0.5 + 0.5 * jnp.tanh(x * p)
     slope = cdf + (x * INV_SQRT_2PI) * jnp.exp2(u * LOG2E_HALF)
     return x * cdf, slope
@@ -84,11 +83,16 @@
     return pltpu.HBM(s, t)
 
 
+def in_vmem(*arrays):
+    return tuple(pltpu.with_memory_space_constraint(a, pltpu.VMEM) for a in arrays)
+
+
 def in_hbm(*arrays):
     return tuple(pltpu.with_memory_space_constraint(a, pltpu.HBM) for a in arrays)
 
 
 ANY = pl.BlockSpec(memory_space=pl.ANY)
+VM = pl.BlockSpec(memory_space=pltpu.VMEM)
 
 
 def call(kernel, info, args, in_specs, outs, out_specs, scratch=(), grid=(1,), name=None, after=(), vmem=8, us=1):
@@ -174,7 +178,11 @@
                 [const(*s)], [pltpu.SemaphoreType.DMA((18 * tensors,))], name=name, after=after)[0]
 
 
-def norm_kernel(info, x_ref, g_ref, gain_ref, shift_ref, n_ref, gsum_ref):
+def shift_of(b):
+    return 4 * b
+
+
+def norm_kernel(info, x_ref, g_ref, gain_ref, shift_ref, n_ref, gw_ref, gsum_ref, rows):
     b = pl.program_id(0)
 
     @pl.when(b == 0)
@@ -182,15 +190,16 @@
         gsum_ref[...] = jnp.zeros_like(gsum_ref)
 
     own = jnp.where(b == pl.num_programs(0) - 1, 1.0, 0.0)
+    up = WIN - shift_of(b)
     for r in range(0, WIN, 48):
         x = x_ref[r : r + 48, :].astype(F32)
         cen = x - jnp.mean(x, -1, keepdims=True)
         inv = lax.rsqrt(jnp.mean(cen * cen, -1, keepdims=True) + EPS)
-        n_ref[0, r : r + 48, :] = (cen * inv * gain_ref[...][None] + shift_ref[...][None]).astype(BF)
-    total = fold8(g_ref[STEP:, :].astype(F32)) * own
-    for r in range(0, STEP, CH):
-        total = total + fold8(g_ref[r : r + CH, :].astype(F32))
-    gsum_ref[...] += jnp.sum(total, 0, keepdims=True)
+        rows[r : r + 48, :] = cen * inv * gain_ref[...][None] + shift_ref[...][None]
+    n_ref[b] = pltpu.roll(rows[...], up, 0).astype(BF)
+    g = g_ref[...].astype(F32)
+    gw_ref[b] = pltpu.roll(g, up, 0).astype(BF)
+    gsum_ref[...] += jnp.sum(fold8(g[:STEP]) + fold8(g[STEP:]) * own, 0, keepdims=True)
 
 
 def window_rows(d):
@@ -200,7 +209,8 @@
 def norm_call(info, x, g, gain, shift, n, after):
     d = x.shape[1]
     return call(norm_kernel, info, in_hbm(x, g, gain, shift), [window_rows(d), window_rows(d), const(d), const(d)],
-                [slow((n, WIN, d), BF), shape((1, d), F32)], [img(WIN, d), const(1, d)], grid=(n,), name="input_norm", after=after, us=3)
+                [fast((n, WIN, d), BF), fast((n, WIN, d), BF), shape((1, d), F32)], [VM, VM, const(1, d)],
+                [pltpu.VMEM((WIN, d), F32)], grid=(n,), name="input_norm", after=after, us=3)
 
 
 def windows_kernel(info, sp_ref, sb_ref, s_ref, st_ref, sbw_ref, token, pad, tpad, col):
@@ -215,20 +225,13 @@
         col[...] = jnp.concatenate([jnp.broadcast_to(sb_ref[...][None], (128, p)), jnp.zeros((128, PAD - p), F32)], 1).T
         token[...] = jnp.zeros_like(token)
 
-    ri = lax.broadcasted_iota(jnp.int32, (WIN, PAD), 0)
-    ci = lax.broadcasted_iota(jnp.int32, (WIN, PAD), 1)
-    for k in range(4):
-
-        @pl.when(lax.rem(b, 4) == k)
-        def _():
-            off = k * (p - STEP)
-            end = off + count_of(info, b)
-            live = (ri >= off) & (ri < end) & (ci >= off) & (ci < end)
-            move = lambda v: pltpu.roll(pltpu.roll(v, off, 0), off, 1) if off else v
-            s_ref[0] = jnp.where(live, move(pad[...])[:WIN], 0.0).astype(BF)[:, :WIN]
-            st_ref[0] = jnp.where(live, move(tpad[...])[:WIN], 0.0).astype(BF)[:, :WIN]
-            cb = pltpu.roll(col[...], off, 0) if off else col[...]
-            sbw_ref[0] = jnp.where(((ri >= off) & (ri < end))[:, :128], cb[:WIN], 0.0)
+    ri = lax.broadcasted_iota(jnp.int32, (WIN, WIN), 0)
+    ci = lax.broadcasted_iota(jnp.int32, (WIN, WIN), 1)
+    end = count_of(info, b)
+    live = (ri < end) & (ci < end)
+    s_ref[b] = jnp.where(live, pad[:WIN, :WIN], 0.0).astype(BF)
+    st_ref[b] = jnp.where(live, tpad[:WIN, :WIN], 0.0).astype(BF)
+    sbw_ref[b] = jnp.where((ri < end)[:, :128], col[:WIN], 0.0)
 
 
 def count_of(info, b):
@@ -237,101 +240,92 @@
 
 def windows_call(info, spatial, sbias, n, after):
     p = spatial.shape[0]
-    win = slow((n, WIN, WIN), BF)
-    return call(windows_kernel, info, in_hbm(spatial, sbias), [const(p, p), const(p)], [win, win, slow((n, WIN, 128), F32), shape((8, 128), F32)],
-                [img(WIN, WIN), img(WIN, WIN), img(WIN, 128), const(8, 128)], [pltpu.VMEM((PAD, PAD), F32)] * 2 + [pltpu.VMEM((PAD, 128), F32)],
+    win = fast((n, WIN, WIN), BF)
+    return call(windows_kernel, info, in_hbm(spatial, sbias), [const(p, p), const(p)], [win, win, fast((n, WIN, 128), F32), shape((8, 128), F32)],
+                [VM, VM, VM, const(8, 128)], [pltpu.VMEM((PAD, PAD), F32)] * 2 + [pltpu.VMEM((PAD, 128), F32)],
                 grid=(n,), name="windows", after=after, us=2)
 
 
 def gate_kernel(info, wa_ref, wb_ref, n_ref, s_ref, sb_ref, rows_ref, hat_ref, slope_ref, inv_ref, shifted_ref, v_ref, pre):
+    b = pl.program_id(0)
     w = wa_ref.shape[1]
     d = wa_ref.shape[0] - 16
     width = 2 * w
 
-    @pl.when(pl.program_id(0) == 0)
+    @pl.when(b == 0)
     def _():
         for k, ref in enumerate((wa_ref, wb_ref)):
             v = ref[d:, :].astype(F32)
             v_ref[:, k * w : (k + 1) * w] = v[:8] + v[8:]
 
     bias, gain, shift = v_ref[1:2, :], v_ref[2:3, :], v_ref[3:4, :]
-    pre[:, :w] = dot(n_ref[0], wa_ref[:d, :])
-    pre[:, w:] = dot(n_ref[0], wb_ref[:d, :])
+    pre[:, :w] = dot(n_ref[b], wa_ref[:d, :])
+    pre[:, w:] = dot(n_ref[b], wb_ref[:d, :])
     for r in range(0, WIN, CH):
         act, slope = gelu_both(pre[r : r + CH, :] + bias)
-        slope_ref[0, r : r + CH, :] = slope.astype(BF)
+        slope_ref[b, r : r + CH, :] = slope.astype(BF)
         cen = act - jnp.sum(act, -1, keepdims=True) * (1.0 / width)
         inv = lax.rsqrt(jnp.sum(cen * cen, -1, keepdims=True) * (1.0 / width) + EPS)
         hat = cen * inv
-        inv_ref[0, r : r + CH, :] = jnp.broadcast_to(inv, (CH, 128))
-        hat_ref[0, r : r + CH, :] = hat.astype(BF)
-        rows_ref[0, r : r + CH, :] = (hat * gain + shift).astype(BF)
-    rows_ref[0, WIN:, :] = jnp.ones((EXT - WIN, width), BF)
-    sb = sb_ref[0]
-    mixed = dot(s_ref[0], rows_ref[0, :WIN, :])
+        inv_ref[b, r : r + CH, :] = jnp.broadcast_to(inv, (CH, 128))
+        hat_ref[b, r : r + CH, :] = hat.astype(BF)
+        rows_ref[b, r : r + CH, :] = (hat * gain + shift).astype(BF)
+    rows_ref[b, WIN:, :] = jnp.ones((EXT - WIN, width), BF)
+    sb = sb_ref[b]
+    mixed = dot(s_ref[b], rows_ref[b, :WIN, :])
     for t in range(0, width, 128):
-        shifted_ref[0, :, t : t + 128] = (mixed[:, t : t + 128] + sb).astype(BF)
+        shifted_ref[b, :, t : t + 128] = (mixed[:, t : t + 128] + sb).astype(BF)
 
 
 def gate_call(info, halves, normed, s, sb, after):
     n, _, d = normed.shape
     w = 2 * halves[0].shape[1]
-    big = slow((n, WIN, w), BF)
+    big = fast((n, WIN, w), BF)
     return call(
-        gate_kernel, info, (*halves, *in_hbm(normed, s, sb)),
-        [whole(a) for a in halves] + [img(WIN, d), img(WIN, WIN), img(WIN, 128)],
-        [slow((n, EXT, w), BF), big, big, slow((n, WIN, 128), F32), big, shape((8, w), F32)],
-        [img(EXT, w), img(WIN, w), img(WIN, w), img(WIN, 128), img(WIN, w), const(8, w)],
-        [pltpu.VMEM((WIN, w), F32)], grid=(n,), name="gate_forward", after=after, us=1, vmem=17,
+        gate_kernel, info, (*halves, *in_vmem(normed, s, sb)), [whole(a) for a in halves] + [VM] * 3,
+        [fast((n, EXT, w), BF), big, big, fast((n, WIN, 128), F32), big, shape((8, w), F32)], [VM] * 5 + [const(8, w)],
+        [pltpu.VMEM((WIN, w), F32)], grid=(n,), name="gate_forward", after=after, us=1, vmem=8,
     )
 
 
-def value_kernel(info, wv_ref, wo_ref, n_ref, g_ref, v_ref, shifted_ref, rows_ref, gin_ref, prod_ref, dshift_ref, dpre_ref, gw_ref, gb_ref, gsp_ref, small_ref,
-                 pre, dprod, prods, dpres, n_all, g_all):
+def value_kernel(h, info, wv_ref, wo_ref, n_ref, g_ref, v_ref, shifted_ref, rows_ref, gin_ref, prod_ref, dshift_ref, dpre_ref, gw_ref, gb_ref, gsp_ref, small_ref,
+                 pre, dprod):
     b = pl.program_id(0)
     n_img = pl.num_programs(0)
-    d, _ = wv_ref.shape
+    d, w = wv_ref.shape
+    cols = slice(h * w, (h + 1) * w)
 
     @pl.when(b == 0)
     def _():
         gb_ref[...] = jnp.zeros_like(gb_ref)
         gsp_ref[...] = gin_ref[...]
 
-    pre[...] = dot(n_ref[0], wv_ref[...])
-    dprod[...] = dot(g_ref[...], wo_ref[...])
+    pre[...] = dot(n_ref[b], wv_ref[...])
+    dprod[...] = dot(g_ref[b], wo_ref[...])
     bias = v_ref[0:1, :]
     for r in range(0, WIN, CH):
         act, slope = gelu_both(pre[r : r + CH, :] + bias)
-        sh = shifted_ref[0, r : r + CH, :].astype(F32)
+        sh = shifted_ref[b, r : r + CH, cols].astype(F32)
         dp = dprod[r : r + CH, :]
         prod = (act * sh).astype(BF)
-        prod_ref[0, r : r + CH, :] = prod
-        dshift_ref[0, r : r + CH, :] = (dp * act).astype(BF)
+        prod_ref[b, r : r + CH, :] = prod
+        dshift_ref[b, r : r + CH, :] = (dp * act).astype(BF)
         dv = dp * sh * slope
         dvl = dv.astype(BF)
-        dpre_ref[0, r : r + CH, :] = dvl
+        dpre_ref[b, r : r + CH, :] = dvl
         gb_ref[...] += fold8(dv)
-    row = pl.multiple_of(b * WIN, 16)
-    n_all[pl.ds(row, WIN), :] = n_ref[0]
-    g_all[pl.ds(row, WIN), :] = g_ref[...]
-    prods[pl.ds(row, WIN), :] = prod_ref[0]
-    dpres[pl.ds(row, WIN), :] = dpre_ref[0]
-    part = dot_nt(dshift_ref[0], rows_ref[0])
-    part = jnp.concatenate([jnp.concatenate([part, jnp.zeros((WIN, PAD - EXT), F32)], 1), jnp.zeros((PAD - WIN, PAD), F32)], 0)
-    off = b * (MAXP_STEP)
-    end = off + count_of(info, b)
-    ri = lax.broadcasted_iota(jnp.int32, (PAD, PAD), 0)
-    ci = lax.broadcasted_iota(jnp.int32, (PAD, PAD), 1)
-    live = (ri >= off) & (ri < end) & (((ci >= off) & (ci < end)) | (ci >= WIN))
-    part = jnp.where(live, part, 0.0)
-    back = lax.rem(PAD - off, PAD)
-    gsp_ref[...] += pltpu.roll(pltpu.roll(part, back, 0), back, 1)
+    part = dot_nt(dshift_ref[b], rows_ref[b, :, cols])
+    end = count_of(info, b)
+    ri = lax.broadcasted_iota(jnp.int32, (WIN, EXT), 0)
+    ci = lax.broadcasted_iota(jnp.int32, (WIN, EXT), 1)
+    live = (ri < end) & ((ci < end) | (ci >= WIN))
+    gsp_ref[:WIN, :EXT] += jnp.where(live, part, 0.0)
 
     @pl.when(b == n_img - 1)
     def _():
-        gwv = dot_tn(n_all[...], dpres[...])
+        gwv = dot_tn(n_ref[...].reshape(-1, d), dpre_ref[...].reshape(-1, w))
         gw_ref[:d, :] = gwv.astype(gw_ref.dtype)
-        gw_ref[d:, :] = dot_tn(g_all[...], prods[...]).astype(gw_ref.dtype)
+        gw_ref[d:, :] = dot_tn(g_ref[...].reshape(-1, d), prod_ref[...].reshape(-1, w)).astype(gw_ref.dtype)
         small_ref[...] = jnp.concatenate([row_sums(gwv, wv_ref), back_sum(gb_ref[...], wv_ref), jnp.zeros((6, d), F32)], 0)
 
 
@@ -348,25 +342,21 @@
     return jnp.sum(dot_nt(hi, w_ref[...]) + dot_nt(lo, w_ref[...]), 0, keepdims=True)
 
 
-MAXP_STEP = 4
-
-
 def value_call(info, h, keep, vo, normed, g, vecs, shifted, rows, gsp, after=()):
     n, _, d = normed.shape
     w = vecs.shape[1] // 2
-    big, out = shape((n, WIN, w), BF), slow((n, WIN, w), BF)
+    big = fast((n, WIN, w), BF)
     return call(
-        value_kernel, info, (vo, vo, *in_hbm(normed, g), vecs, *in_hbm(shifted, rows), gsp),
-        [side(d, w, 0), side(d, w, 1), img(WIN, d), window_rows(d), pl.BlockSpec((8, w), lambda b, *_: (0, h)), half(WIN, w, h), half(EXT, w, h), const(PAD, PAD)],
-        [out, big, out, shape((2 * d, w), F32 if keep else BF), shape((8, w), F32), shape((PAD, PAD), F32), shape((8, d), F32)],
-        [img(WIN, w)] * 3 + [const(2 * d, w), const(8, w), const(PAD, PAD), const(8, d)],
-        [pltpu.VMEM((WIN, w), F32)] * 2 + [pltpu.VMEM((n * WIN, w), BF)] * 2 + [pltpu.VMEM((n * WIN, d), BF)] * 2,
-        grid=(n,), name="value_own" if keep else "value_other", after=after, us=1, vmem=23,
+        lambda *a: value_kernel(h, *a), info, (vo, vo, *in_vmem(normed, g), vecs, *in_vmem(shifted, rows), gsp),
+        [side(d, w, 0), side(d, w, 1), VM, VM, pl.BlockSpec((8, w), lambda b, *_: (0, h)), VM, VM, const(PAD, PAD)],
+        [big, big, big, shape((2 * d, w), BF), shape((8, w), F32), shape((PAD, PAD), F32), shape((8, d), F32)],
+        [VM] * 3 + [const(2 * d, w), const(8, w), const(PAD, PAD), const(8, d)],
+        [pltpu.VMEM((WIN, w), F32)] * 2, grid=(n,), name="value_own" if keep else "value_other", after=after, us=1, vmem=12,
     )
 
 
 def back_kernel(info, n_ref, dsa_ref, dsb_ref, rows_hat_ref, slope_ref, inv_ref, st_ref, v_ref, wa_ref, wb_ref, gba_ref, gbb_ref, sma_ref, smb_ref, gsum_ref,
-                dpre_ref, keep_ref, send_ref, vown_ref, dgr, dpres, n_all, gb, gg, gsh):
+                dpre_ref, keep_ref, send_ref, vown_ref, dgr, gb, gg, gsh):
     b = pl.program_id(0)
     n_img = pl.num_programs(0)
     d, w = n_ref.shape[2], wa_ref.shape[1]
@@ -379,27 +369,24 @@
             r[...] = jnp.zeros_like(r)
 
     gain = v_ref[2:3, :]
-    dgr[:, :w] = dot(st_ref[0], dsa_ref[0])
-    dgr[:, w:] = dot(st_ref[0], dsb_ref[0])
+    dgr[:, :w] = dot(st_ref[b], dsa_ref[b])
+    dgr[:, w:] = dot(st_ref[b], dsb_ref[b])
     for r in range(0, WIN, CH):
         dr = dgr[r : r + CH, :]
-        hat = rows_hat_ref[0, r : r + CH, :].astype(F32)
+        hat = rows_hat_ref[b, r : r + CH, :].astype(F32)
         gg[...] += fold8(dr * hat)
         gsh[...] += fold8(dr)
         dg = dr * gain
         m1 = jnp.sum(dg, -1, keepdims=True) * (1.0 / width)
         m2 = jnp.sum(dg * hat, -1, keepdims=True) * (1.0 / width)
-        dpg = (dg - m1 - hat * m2) * inv_ref[0, r : r + CH, 0:1] * slope_ref[0, r : r + CH, :].astype(F32)
-        dpre_ref[0, r : r + CH, :] = dpg.astype(BF)
+        dpg = (dg - m1 - hat * m2) * inv_ref[b, r : r + CH, 0:1] * slope_ref[b, r : r + CH, :].astype(F32)
+        dpre_ref[b, r : r + CH, :] = dpg.astype(BF)
         gb[...] += fold8(dpg)
-    row = pl.multiple_of(b * WIN, 16)
-    dpres[pl.ds(row, WIN), :] = dpre_ref[0]
-    n_all[pl.ds(row, WIN), :] = n_ref[0]
 
     @pl.when(b == n_img - 1)
     def _():
-        gw = dot_tn(n_all[...], dpres[...])
-        keep_ref[...] = gw[:, :w]
+        gw = dot_tn(n_ref[...].reshape(-1, d), dpre_ref[...].reshape(-1, width))
+        keep_ref[...] = gw[:, :w].astype(BF)
         sums = gb[...]
         send_ref[:d, :] = gw[:, w:].astype(BF)
         t = sma_ref[0:1, :] + smb_ref[0:1, :] + row_sums(gw[:, :w], wa_ref) + row_sums(gw[:, w:], wb_ref)
@@ -420,64 +407,94 @@
     width = vecs.shape[1]
     w = width // 2
     return call(
-        back_kernel, info, (*in_hbm(normed), *ds, *in_hbm(hat, slope, inv, st), vecs, *wg, *gbv, *small, gsum),
-        [img(WIN, d), img(WIN, w), img(WIN, w), img(WIN, width), img(WIN, width), img(WIN, 128), img(WIN, WIN), const(8, width), whole(wg[0]), whole(wg[1]),
-         const(8, w), const(8, w), const(8, d), const(8, d), const(1, d)],
-        [slow((n, WIN, width), BF), shape((d, w), F32), shape((d + 16, w), BF), shape((8, w), F32)],
-        [img(WIN, width), const(d, w), const(d + 16, w), const(8, w)],
-        [pltpu.VMEM((WIN, width), F32), pltpu.VMEM((n * WIN, width), BF), pltpu.VMEM((n * WIN, d), BF)] + [pltpu.VMEM((8, width), F32)] * 3,
-        grid=(n,), name="gate_backward", after=after, us=1, vmem=23,
+        back_kernel, info, (*in_vmem(normed, *ds, hat, slope, inv, st), vecs, *wg, *gbv, *small, gsum),
+        [VM] * 7 + [const(8, width), whole(wg[0]), whole(wg[1]), const(8, w), const(8, w), const(8, d), const(8, d), const(1, d)],
+        [fast((n, WIN, width), BF), shape((d, w), BF), shape((d + 16, w), BF), shape((8, w), F32)],
+        [VM, const(d, w), const(d + 16, w), const(8, w)],
+        [pltpu.VMEM((WIN, width), F32)] + [pltpu.VMEM((8, width), F32)] * 3, grid=(n,), name="gate_backward", after=after, us=1, vmem=14,
     )
 
 
 def joined(v, carry):
-    @pl.when(pl.program_id(0) == 0)
+    b = pl.program_id(0)
+
+    @pl.when(b == 0)
     def _():
         carry[...] = jnp.zeros_like(carry)
 
+    v = pltpu.roll(v, shift_of(b), 0)
     v = jnp.concatenate([v[:16] + carry[...], v[16:]], 0)
     carry[...] = v[STEP:]
     return v
 
 
-def result_kernel(info, x_ref, pa_ref, pb_ref, woa_ref, wob_ref, bias_ref, res_ref, carry):
-    start = pl.multiple_of(pl.program_id(0) * STEP, 16)
-    br = joined(dot_nt(pa_ref[0], woa_ref[...]) + dot_nt(pb_ref[0], wob_ref[...]), carry)
-    res_ref[pl.ds(start, WIN), :] = (x_ref[pl.ds(start, WIN), :].astype(F32) + br + bias_ref[...][None]).astype(BF)
-
-
-def grad_kernel(info, x_ref, g_ref, va_ref, vb_ref, dg_ref, wva_ref, wvb_ref, wga_ref, wgb_ref, gain_ref, ing_ref, carry):
-    start = pl.multiple_of(pl.program_id(0) * STEP, 16)
+def result_kernel(info, x_ref, pa_ref, pb_ref, woa_ref, wob_ref, bias_ref, res_ref, token, carry):
+    b = pl.program_id(0)
+    token[...] = jnp.zeros_like(token)
+    finish = lambda x, br: (x.astype(F32) + br + bias_ref[...][None]).astype(BF)
+
+    @pl.when(b < pl.num_programs(0) - 1)
+    def _():
+        br = joined(dot_nt(pa_ref[b], woa_ref[...]) + dot_nt(pb_ref[b], wob_ref[...]), carry)
+        res_ref[...] = finish(x_ref[:STEP, :], br[:STEP])
+
+    @pl.when(b == pl.num_programs(0) - 1)
+    def _():
+        res_ref[:16, :] = finish(x_ref[STEP:, :], carry[...])
+
+
+def grad_kernel(info, x_ref, g_ref, va_ref, vb_ref, dg_ref, wva_ref, wvb_ref, wga_ref, wgb_ref, gain_ref, ing_ref, token, carry):
+    b = pl.program_id(0)
+    token[...] = jnp.zeros_like(token)
     d, w = wva_ref.shape
-    dn = dot_nt(va_ref[0], wva_ref[...]) + dot_nt(vb_ref[0], wvb_ref[...])
-    dn = joined(dn + dot_nt(dg_ref[0, :, :w], wga_ref[:d, :]) + dot_nt(dg_ref[0, :, w:], wgb_ref[:d, :]), carry)
-    x = x_ref[pl.ds(start, WIN), :].astype(F32)
-    cen = x - jnp.mean(x, -1, keepdims=True)
-    inv = lax.rsqrt(jnp.mean(cen * cen, -1, keepdims=True) + EPS)
-    hat = cen * inv
-    dx = dn * gain_ref[...][None]
-    m1 = jnp.mean(dx, -1, keepdims=True)
-    m2 = jnp.mean(dx * hat, -1, keepdims=True)
-    ing_ref[pl.ds(start, WIN), :] = g_ref[...].astype(F32) + inv * (dx - m1 - hat * m2)
+
+    def finish(x, g, dn):
+        x = x.astype(F32)
+        cen = x - jnp.mean(x, -1, keepdims=True)
+        inv = lax.rsqrt(jnp.mean(cen * cen, -1, keepdims=True) + EPS)
+        hat = cen * inv
+        dx = dn * gain_ref[...][None]
+        m1 = jnp.mean(dx, -1, keepdims=True)
+        m2 = jnp.mean(dx * hat, -1, keepdims=True)
+        return g.astype(F32) + inv * (dx - m1 - hat * m2)
+
+    @pl.when(b < pl.num_programs(0) - 1)
+    def _():
+        dn = dot_nt(va_ref[b], wva_ref[...]) + dot_nt(vb_ref[b], wvb_ref[...])
+        dn = joined(dn + dot_nt(dg_ref[b, :, :w], wga_ref[:d, :]) + dot_nt(dg_ref[b, :, w:], wgb_ref[:d, :]), carry)
+        ing_ref[...] = finish(x_ref[:STEP, :], g_ref[:STEP, :], dn[:STEP])
+
+    @pl.when(b == pl.num_programs(0) - 1)
+    def _():
+        ing_ref[:16, :] = finish(x_ref[STEP:, :], g_ref[STEP:, :], carry[...])
+
+
+def last_rows(n, d):
+    return pl.BlockSpec((pl.Element(WIN), pl.Element(d)), lambda b, *_: (jnp.minimum(b, n - 1) * STEP, 0))
+
+
+def row_block(d):
+    return pl.BlockSpec((STEP, d), lambda b, *_: (b, 0))
 
 
 def result_call(info, x, prod, vo, bias, after):
     n, _, w = prod[0].shape
     rows, d = x.shape
     return call(
-        result_kernel, info, (*in_hbm(x, *prod), *vo, *in_hbm(bias)), [const(rows, d), img(WIN, w), img(WIN, w), side(d, w, 1), side(d, w, 1), const(d)],
-        [shape((rows, d), BF)], [const(rows, d)], [pltpu.VMEM((16, d), F32)], grid=(n,), name="result", after=after, us=1, vmem=10,
-    )[0]
+        result_kernel, info, (*in_hbm(x), *in_vmem(*prod), *vo, *in_hbm(bias)),
+        [last_rows(n, d), VM, VM, side(d, w, 1), side(d, w, 1), const(d)],
+        [slow((rows, d), BF), shape((8, 128), F32)], [row_block(d), const(8, 128)], [pltpu.VMEM((16, d), F32)], grid=(n + 1,), name="result", after=after, us=1, vmem=10,
+    )
 
 
 def grad_call(info, x, g, dpv, dpg, vo, wg, gain, after):
     n, _, w = dpv[0].shape
     rows, d = x.shape
     return call(
-        grad_kernel, info, (*in_hbm(x, g, *dpv, dpg), *vo, *wg, *in_hbm(gain)),
-        [const(rows, d), window_rows(d), img(WIN, w), img(WIN, w), img(WIN, 2 * w)] + [side(d, w, 0)] * 2 + [whole(wg[0]), whole(wg[1]), const(d)],
-        [shape((rows, d), F32)], [const(rows, d)], [pltpu.VMEM((16, d), F32)], grid=(n,), name="input_grad", after=after, us=1, vmem=16,
-    )[0]
+        grad_kernel, info, (*in_hbm(x, g), *in_vmem(*dpv, dpg), *vo, *wg, *in_hbm(gain)),
+        [last_rows(n, d), last_rows(n, d), VM, VM, VM] + [side(d, w, 0)] * 2 + [whole(wg[0]), whole(wg[1]), const(d)],
+        [slow((rows, d), F32), shape((8, 128), F32)], [row_block(d), const(8, 128)], [pltpu.VMEM((16, d), F32)], grid=(n + 1,), name="input_grad", after=after, us=1, vmem=16,
+    )
 
 
 VROWS = 32
@@ -501,7 +518,7 @@
                 for z in range(nz):
                     row = pl.multiple_of(t * d + (2 * z + jnp.bitwise_xor(x, xr)) * r, r)
                     dst = t * nz * r + z * r
-                    out[b, dst : dst + r, :] = (keep[pl.ds(row, r), cols] + recv[pl.ds(row, r), cols].astype(F32)).astype(out.dtype)
+                    out[b, dst : dst + r, :] = (keep[pl.ds(row, r), cols].astype(F32) + recv[pl.ds(row, r), cols].astype(F32)).astype(out.dtype)
             at = tensors * nz * r
             if extra == "spatial":
                 q = PAD // 4
@@ -634,7 +651,7 @@
 def scatter_any(keep, recv):
     n = lax.axis_size("dp")
     c = keep.shape[1] // 2
-    a = keep + recv.astype(F32)
+    a = keep.astype(F32) + recv.astype(F32)
     s = a[:, :c] + permute(a[:, c:].astype(BF), lambda dp, mp: (dp, mp ^ 2)).astype(F32)
     return lax.all_to_all(s.astype(BF).reshape(n, -1, c), "dp", 0, 0, tiled=True).astype(F32).sum(0)
 
@@ -664,7 +681,7 @@
         vo2 = y_swap(vo0)
         zvo = ()
         voa = jnp.concatenate([vo0[:, :c], vo2[:, :c], vo0[:, c:], vo2[:, c:]], 1)
-    normed, gsum = norm_call(info, inputs, cotangent, input_norm_gain, shift_in, n, (zg,))
+    normed, g_win, gsum = norm_call(info, inputs, cotangent, input_norm_gain, shift_in, n, (zg,))
     s, st, sb, token = windows_call(info, spatial, spatial_bias, n, (gsum, *zvo))
     if quick:
         wga = assemble_call(info, pieces, 1, 16, (token,), "assemble_gate")
@@ -676,9 +693,9 @@
         voa = assemble_call(info, pieces, 2, 0, (vec,), "assemble_value_out")
     vob = core_swap(voa)
     zero = jnp.zeros((PAD, PAD), F32)
-    prod_b, ds_b, dpv_b, gw_b, gb_b, gsp, small_b = value_call(info, 1, False, vob, normed, cotangent, vec, shifted, rows, zero)
+    prod_b, ds_b, dpv_b, gw_b, gb_b, gsp, small_b = value_call(info, 1, False, vob, normed, g_win, vec, shifted, rows, zero)
     recv_vo = core_swap(gw_b)
-    prod_a, ds_a, dpv_a, gw_a, gb_a, gsp, small_a = value_call(info, 0, True, voa, normed, cotangent, vec, shifted, rows, gsp)
+    prod_a, ds_a, dpv_a, gw_a, gb_a, gsp, small_a = value_call(info, 0, True, voa, normed, g_win, vec, shifted, rows, gsp)
     q = PAD // 4
     def quarters(tensors, extra, args, rows, name, after):
         return simple_call(lambda *a: quarter_kernel(tensors, extra, *a), info, args, [shape((2, rows, c), F32), shape((2, rows, c), BF)], name, after=after)
@@ -699,16 +716,16 @@
     if quick:
         kvo, snd = plane(kvo, got_vo, q, "plane_vo", (vown,))
         got_vo = second_swap(snd)
-    res = result_call(info, inputs, (prod_a, prod_b), (voa, vob), out_bias, (snd if quick else vown,))
+        kg, snd = quarters(1, "vectors", (keep_g, recv_g, vown), 4 * r + VROWS, "quarters_g", (snd,))
+        got_g = first_swap(snd)
+    res, token = result_call(info, inputs, (prod_a, prod_b), (voa, vob), out_bias, (snd if quick else vown,))
     if quick:
-        kg, snd = quarters(1, "vectors", (keep_g, recv_g, vown), 4 * r + VROWS, "quarters_g", (res,))
-        got_g = first_swap(snd)
-        kvo, snd = line(kvo, got_vo, 2, 4, q, "line_vo", (snd,))
+        kvo, snd = line(kvo, got_vo, 2, 4, q, "line_vo", (token,))
         got_vo = z_swap(snd, 2)
         kg, snd = plane(kg, got_g, VROWS, "plane_g", (snd,))
         got_g = second_swap(snd)
-        ing = grad_call(info, inputs, cotangent, (dpv_a, dpv_b), dpg, (voa, vob), (wga, wgb), input_norm_gain, (snd,))
-        kg, snd = line(kg, got_g, 1, 4, VROWS, "line_g", (ing,))
+        ing, token = grad_call(info, inputs, cotangent, (dpv_a, dpv_b), dpg, (voa, vob), (wga, wgb), input_norm_gain, (snd,))
+        kg, snd = line(kg, got_g, 1, 4, VROWS, "line_g", (token,))
         got_g = z_swap(snd, 2)
         kvo, snd = line(kvo, got_vo, 2, 2, q, "pair_vo", (snd,))
         got_vo = z_swap(snd, 1)
@@ -721,9 +738,9 @@
         gwg, gbv, gbg, ggain, gshift, full = simple_call(
             finish_g_kernel, info, (kg, got_g, *in_hbm(input_norm_gain, shift_in)),
             [shape((r, c), F32)] + [one] * 4 + [shape((8, d), F32)], "finish_g", after=(sp,))
-        gspat, gsb, gin, sin, gob = simple_call(spatial_kernel, info, (sp, *sps, full, core_swap(full)), [shape((p, p), F32), shape((p,), F32)] + [shape((d,), F32)] * 3, "spatial_sum", [pltpu.VMEM((PAD, PAD), F32)], after=(gwg,))
+        gspat, gsb, gin, sin, gob = simple_call(spatial_kernel, info, (sp, *sps, full, core_swap(full)), [shape((p, p), F32), shape((p,), F32)] + [shape((d,), F32)] * 3, "spatial_sum", [pltpu.VMEM((PAD, PAD), F32)])
     else:
-        ing = grad_call(info, inputs, cotangent, (dpv_a, dpv_b), dpg, (voa, vob), (wga, wgb), input_norm_gain, ())
+        ing, _ = grad_call(info, inputs, cotangent, (dpv_a, dpv_b), dpg, (voa, vob), (wga, wgb), input_norm_gain, ())
         gwv = scatter_any(gw_a[:d], recv_vo[:d])
         gwo = scatter_any(gw_a[d:], recv_vo[d:])
         gwg = scatter_any(keep_g, recv_g[:d])

time: 162 us -> 144 us (0.89)
  Pallas kernels: 102 us -> 84.7 us
  local copies, waits for them, and re-layouts: 4.74 us -> 0.78 us
  waiting for transfers between devices: 21.4 us -> 23.9 us
    pallas_call x25, Pallas kernels: 102 us -> 84.7 us  [call(): pl.pallas_call(ordered, grid_spec=pltpu.PrefetchScalarGridSpec(num_scalar...]
    unnamed x6 -> x0, local copies, waits for them, and re-layouts: 3.96 us -> none
    ppermute x29, waiting for transfers between devices: 21.4 us -> 23.9 us  [permute(): return lax.ppermute(x, AXES, pairs)]
  transfers between devices with their start and end apart: 29 -> 29, of which waited for: 11 -> 12; matrix products, arithmetic and copies ran while one was open for 0% -> 0% of each run, Pallas kernels for 50% -> 47%
where the time goes in v3:
time: 144 us; the launch traced here: 143 us
  Pallas kernels  84.7 us (59%)
  starting transfers between devices  33.1 us (23%)
  waiting for transfers between devices  23.9 us (17%)
    pallas_call x25, Pallas kernels, call(): pl.pallas_call(ordered, grid_spec=pltpu.PrefetchScalarGridSpec(num_scalar...  84.7 us
    ppermute x29, starting transfers between devices, permute(): return lax.ppermute(x, AXES, pairs)  33.1 us
    ppermute x29, waiting for transfers between devices, permute(): return lax.ppermute(x, AXES, pairs)  23.9 us
  transfers between devices with their start and end apart: 29, of which 12 were waited for; matrix products, arithmetic and copies ran while one was open for 0% of the time, Pallas kernels for 47%

profile of v3, /device:TPU:0, one launch (start us, length us, event | category | flops | bytes accessed | tf_op | source)
XLA Modules:
  0.0 143.4 jit_solution(6052179725787976858)
XLA Ops:
  0.7 0.7 concatenate.3.info_ref
  1.4 1.6 %casts.1 = (bf16[64,384]{1,0:T(8,128)(2,1)S(1)}, bf16[64,768]{1,0:T(8,128)(2,1)S(1)}, bf16[16,384]{1,0:T(8,128)(2,1)S(1)}) custom-call(s32[24]{0:T(128)S(1)} %concatenate.3.info_ref, f32[64,384]{1,0:T(8,128)} %refs_0_.5, f32[64,384]{1,0:T(8,128)} %refs_1_.4, f32[64,384]{1,0:T(8,128)} %bitcast.8, f32[384]{0:T(512)} %refs_3_.3, f32[384]{0:T(512)} %refs_4_.1, ...), custom_call_target="tpu_custom_call" | custom-call | flops 1100000000 | bytes 3300000 | tf_op jit(solution)/shard_map/casts/pallas_call | solution.py:104
  3.0 5.1 %collective-permute-start.5 = (bf16[64,384]{1,0:T(8,128)(2,1)S(1)}, bf16[64,384]{1,0:T(8,128)(2,1)S(1)}, u32[]{:S(2)}, u32[]{:S(2)}) collective-permute-start(bf16[64,384]{1,0:T(8,128)(2,1)S(1)} %get-tuple-element.83.refs_0_), channel_id=1, source_target_pairs={{0,24},{1,25},{2,26},{3,27},{4,28},{5,29},{6,30},{7,31},{8,0},{9,1... | collective-permute-start | bytes 147464 | tf_op jit(solution)/shard_map/ppermute | solution.py:606
  8.1 1.0 collective-permute-start.3
  9.1 2.8 %collective-permute-start.2 = (bf16[64,768]{1,0:T(8,128)(2,1)S(1)}, bf16[64,768]{1,0:T(8,128)(2,1)S(1)}, u32[]{:S(2)}, u32[]{:S(2)}) collective-permute-start(bf16[64,768]{1,0:T(8,128)(2,1)S(1)} %get-tuple-element.82.refs_0_), channel_id=1, source_target_pairs={{0,24},{1,25},{2,26},{3,27},{4,28},{5,29},{6,30},{7,31},{8,0},{9,1... | collective-permute-start | bytes 294920 | tf_op jit(solution)/shard_map/ppermute | solution.py:606
  12.0 1.1 collective-permute-start.1
  13.1 0.6 collective-permute-done.4.refs_2_
  13.7 1.0 collective-permute-done.3.refs_1_
  14.7 0.9 line_gate.1.refs_4_.refs_0_
  15.6 2.5 %collective-permute-start.8 = (bf16[272,384]{1,0:T(8,128)(2,1)S(1)}, bf16[272,384]{1,0:T(8,128)(2,1)S(1)}, u32[]{:S(2)}, u32[]{:S(2)}) collective-permute-start(bf16[272,384]{1,0:T(8,128)(2,1)S(1)} %line_gate.1.refs_4_.refs_0_), channel_id=1, source_target_pairs={{0,6},{1,7},{2,4},{3,5},{4,2},{5,3},{6,0},{7,1},{8,14},{9,15},{10,... | collective-permute-start | bytes 626696 | tf_op jit(solution)/shard_map/ppermute | solution.py:606
  19.1 5.8 %input_norm.1 = (bf16[4,336,512]{2,1,0:T(8,128)(2,1)S(1)}, bf16[4,336,512]{2,1,0:T(8,128)(2,1)S(1)}, f32[1,512]{1,0:T(1,128)S(1)}) custom-call(s32[24]{0:T(128)S(1)} %concatenate.3.info_ref, bf16[1296,512]{1,0:T(8,128)(2,1)} %refs_0_.9, bf16[1296,512]{1,0:T(8,128)(2,1)} %refs_1_.7, f32[512]{0:T(512)} %refs_2_.3, f32[512]{0:T(512)} %refs_3_.5, ...), custom_call_target="tpu_custom_call" | custom-call | flops 3300000000 | bytes 9900000 | tf_op jit(solution)/shard_map/input_norm/pallas_call | solution.py:104
  24.9 2.6 %windows.1 = (bf16[4,336,336]{2,1,0:T(8,128)(2,1)S(1)}, bf16[4,336,336]{2,1,0:T(8,128)(2,1)S(1)}, f32[4,336,128]{2,1,0:T(8,128)S(1)}, f32[8,128]{1,0:T(8,128)S(1)}) custom-call(s32[24]{0:T(128)S(1)} %concatenate.3.info_ref, f32[324,324]{1,0:T(8,128)} %refs_0_.7, f32[324]{0:T(512)} %refs_1_.6, f32[1,512]{1,0:T(1,128)S(1)} %get-tuple-element.85.refs_2_.refs_14_, ...), custom_call_target="tpu_custom_call" | custom-call | flops 2200000000 | bytes 6600000 | tf_op jit(solution)/shard_map/windows/pallas_call | solution.py:104
  27.6 0.9 assemble_gate.1.refs_4_.refs_0_.refs_8_.refs_7_
  28.5 1.1 line_value_out.1.refs_5_.refs_0_
  29.6 2.5 %collective-permute-start.11 = (bf16[256,768]{1,0:T(8,128)(2,1)S(1)}, bf16[256,768]{1,0:T(8,128)(2,1)S(1)}, u32[]{:S(2)}, u32[]{:S(2)}) collective-permute-start(bf16[256,768]{1,0:T(8,128)(2,1)S(1)} %line_value_out.1.refs_5_.refs_0_), channel_id=1, source_target_pairs={{0,6},{1,7},{2,4},{3,5},{4,2},{5,3},{6,0},{7,1},{8,14},{9,15},{10,... | collective-permute-start | bytes 1179656 | tf_op jit(solution)/shard_map/ppermute | solution.py:606
  33.2 12.2 %gate_forward.1 = (bf16[4,352,1536]{2,1,0:T(8,128)(2,1)S(1)}, bf16[4,336,1536]{2,1,0:T(8,128)(2,1)S(1)}, bf16[4,336,1536]{2,1,0:T(8,128)(2,1)S(1)}, f32[4,336,12...) custom-call(s32[24]{0:T(128)S(1)} %concatenate.3.info_ref, ...), custom_call_target="tpu_custom_call" | custom-call | flops 1100000000 | bytes 3300000 | tf_op jit(solution)/shard_map/gate_forward/pallas_call | solution.py:104
  45.4 5.1 %collective-permute-done.10.refs_2_ = bf16[256,768]{1,0:T(8,128)(2,1)S(1)} collective-permute-done((bf16[256,768]{1,0:T(8,128)(2,1)S(1)}, bf16[256,768]{1,0:T(8,128)(2,1)S(1)}, u32[]{:S(2)}, u32[]{:S(2)}) %collective-permute-start.10) | collective-permute-done | bytes 393248 | tf_op jit(solution)/shard_map/ppermute | solution.py:606
  50.6 1.2 assemble_value_out.1.refs_0_.refs_1_.refs_3_.refs_5_
  51.9 3.4 %collective-permute-done.13.refs_0_.refs_1_.refs_4_.refs_6_ = bf16[512,1536]{1,0:T(8,128)(2,1)S(1)} collective-permute-done((bf16[512,1536]{1,0:T(8,128)(2,1)S(1)}, bf16[512,1536]{1,0:T(8,128)(2,1)S(1)}, u32[]{:S(2)}, u32[]{:S(2)}) %collective-permute-start.13) | collective-permute-done | bytes 1572896 | tf_op jit(solution)/shard_map/ppermute | solution.py:606
  55.3 9.9 %value_other.1 = (bf16[4,336,768]{2,1,0:T(8,128)(2,1)S(1)}, bf16[4,336,768]{2,1,0:T(8,128)(2,1)S(1)}, bf16[4,336,768]{2,1,0:T(8,128)(2,1)S(1)}, bf16[1024,768]{1...) custom-call(s32[24]{0:T(128)S(1)} %concatenate.3.info_ref, ...), custom_call_target="tpu_custom_call" | custom-call | flops 1100000000 | bytes 3300000 | tf_op jit(solution)/shard_map/value_other/pallas_call | solution.py:104
  65.4 10.1 %value_own.1 = (bf16[4,336,768]{2,1,0:T(8,128)(2,1)S(1)}, bf16[4,336,768]{2,1,0:T(8,128)(2,1)S(1)}, bf16[4,336,768]{2,1,0:T(8,128)(2,1)S(1)}, bf16[1024,768]{1,0...) custom-call(s32[24]{0:T(128)S(1)} %concatenate.3.info_ref, ...), custom_call_target="tpu_custom_call" | custom-call | flops 1100000000 | bytes 3300000 | tf_op jit(solution)/shard_map/value_own/pallas_call | solution.py:104
  75.5 0.9 quarters_vo.1
  76.5 1.5 %collective-permute-start.16 = (bf16[2,608,384]{2,1,0:T(8,128)(2,1)S(1)}, bf16[2,608,384]{2,1,0:T(8,128)(2,1)S(1)}, u32[]{:S(2)}, u32[]{:S(2)}) collective-permute-start(bf16[2,608,384]{2,1,0:T(8,128)(2,1)S(1)} %get-tuple-element.110.refs_15_), channel_id=1, source_target_pairs={{0,2},{1,5},{2,0},{3,7},{4,6},{5,1},{6,4},{7,3},{8,10},{9,13},{10,... | collective-permute-start | bytes 2801672 | tf_op jit(solution)/shard_map/ppermute | solution.py:606
  78.0 10.5 %gate_backward.1 = (bf16[4,336,1536]{2,1,0:T(8,128)(2,1)S(1)}, bf16[512,768]{1,0:T(8,128)(2,1)S(1)}, bf16[528,768]{1,0:T(8,128)(2,1)S(1)}, f32[8,768]{1,0:T(8,128)S(1)}) custom-call(s32[24]{0:T(128)S(1)} %concatenate.3.info_ref, bf16[4,336,512]{2,1,0:T(8,128)(2,1)S(1)} %get-tuple-element.87.refs_2_.refs_0_, ...), custom_call_target="tpu_custom_call" | custom-call | flops 1100000000 | bytes 3300000 | tf_op jit(solution)/shard_map/gate_backward/pallas_call | solution.py:104
  88.8 1.3 collective-permute-done.16.refs_1_
  90.1 0.8 plane_vo.1
  90.9 1.5 %collective-permute-start.18 = (bf16[608,384]{1,0:T(8,128)(2,1)S(1)}, bf16[608,384]{1,0:T(8,128)(2,1)S(1)}, u32[]{:S(2)}, u32[]{:S(2)}) collective-permute-start(bf16[608,384]{1,0:T(8,128)(2,1)S(1)} %get-tuple-element.115.refs_3_), channel_id=1, source_target_pairs={{0,4},{1,3},{2,6},{3,1},{4,0},{5,7},{6,2},{7,5},{8,12},{9,11},{10,... | collective-permute-start | bytes 1400840 | tf_op jit(solution)/shard_map/ppermute | solution.py:606
  92.4 0.8 quarters_g.1
  93.2 0.8 collective-permute-start.17
  94.0 6.6 %result.1 = (bf16[1296,512]{1,0:T(8,128)(2,1)}, f32[8,128]{1,0:T(8,128)S(1)}) custom-call(s32[24]{0:T(128)S(1)} %concatenate.3.info_ref, bf16[1296,512]{1,0:T(8,128)(2,1)} %refs_0_.9, bf16[4,336,768]{2,1,0:T(8,128)(2,1)S(1)} %get-tuple-element.95.refs_1_, bf16[4,336,768]{2,1,0:T(8,128)(2,1)S(1)} %get-tuple-element.96.refs_2_, ...), custom_call_target="tpu_custom_call" | custom-call | flops 1100000000 | bytes 3300000 | tf_op jit(solution)/shard_map/result/pallas_call | solution.py:104
  100.5 3.5 %collective-permute-done.18.refs_1_ = bf16[608,384]{1,0:T(8,128)(2,1)S(1)} collective-permute-done((bf16[608,384]{1,0:T(8,128)(2,1)S(1)}, bf16[608,384]{1,0:T(8,128)(2,1)S(1)}, u32[]{:S(2)}, u32[]{:S(2)}) %collective-permute-start.18) | collective-permute-done | bytes 466976 | tf_op jit(solution)/shard_map/ppermute | solution.py:606
  104.1 0.7 line_vo.1
  104.7 0.6 plane_g.1
  105.4 1.5 %collective-permute-start.20 = (bf16[288,384]{1,0:T(8,128)(2,1)S(1)}, bf16[288,384]{1,0:T(8,128)(2,1)S(1)}, u32[]{:S(2)}, u32[]{:S(2)}) collective-permute-start(bf16[288,384]{1,0:T(8,128)(2,1)S(1)} %get-tuple-element.125.refs_10_), channel_id=1, source_target_pairs={{0,4},{1,3},{2,6},{3,1},{4,0},{5,7},{6,2},{7,5},{8,12},{9,11},{10,... | collective-permute-start | bytes 663560 | tf_op jit(solution)/shard_map/ppermute | solution.py:606
  106.9 4.5 %collective-permute-start.19 = (bf16[352,384]{1,0:T(8,128)(2,1)S(1)}, bf16[352,384]{1,0:T(8,128)(2,1)S(1)}, u32[]{:S(2)}, u32[]{:S(2)}) collective-permute-start(bf16[352,384]{1,0:T(8,128)(2,1)S(1)} %get-tuple-element.124.refs_2_), channel_id=1, source_target_pairs={{0,16},{1,17},{2,18},{3,19},{4,20},{5,21},{6,22},{7,23},{8,24},{9,... | collective-permute-start | bytes 811016 | tf_op jit(solution)/shard_map/ppermute | solution.py:606
  111.4 10.7 %input_grad.1 = (f32[1296,512]{1,0:T(8,128)}, f32[8,128]{1,0:T(8,128)S(1)}) custom-call(s32[24]{0:T(128)S(1)} %concatenate.3.info_ref, bf16[1296,512]{1,0:T(8,128)(2,1)} %refs_0_.9, bf16[1296,512]{1,0:T(8,128)(2,1)} %refs_1_.7, bf16[4,336,768]{2,1,0:T(8,128)(2,1)S(1)} %get-tuple-element.118.refs_2_, bf16[4,336,768]{2,1,0:T(8,128)(2,1)S(1)} %get-tuple-element.119.refs_3_, ...), custom_call_target="tpu_custom_call" | custom-call | flops 1100000000 | bytes 3300000 | tf_op jit(solution)/shard_map/input_grad/pallas_call | solution.py:104
  122.8 0.6 pair_vo.1
  123.5 1.1 collective-permute-start.21
  124.5 4.2 %collective-permute-done.22.refs_1_ = bf16[160,384]{1,0:T(8,128)(2,1)S(1)} collective-permute-done((bf16[160,384]{1,0:T(8,128)(2,1)S(1)}, bf16[160,384]{1,0:T(8,128)(2,1)S(1)}, u32[]{:S(2)}, u32[]{:S(2)}) %collective-permute-start.22) | collective-permute-done | bytes 122912 | tf_op jit(solution)/shard_map/ppermute | solution.py:606
  129.3 1.3 collective-permute-done.21.refs_1_
  130.6 1.2 finish_vo.1
  132.3 0.8 collective-permute-done.23.refs_1_
  133.7 1.9 %collective-permute-start.26 = (bf16[96,384]{1,0:T(8,128)(2,1)S(1)}, bf16[96,384]{1,0:T(8,128)(2,1)S(1)}, u32[]{:S(2)}, u32[]{:S(2)}) collective-permute-start(bf16[96,384]{1,0:T(8,128)(2,1)S(1)} %spatial_pair.1.refs_4_.refs_0_), channel_id=1, source_target_pairs={{0,6},{1,7},{2,4},{3,5},{4,2},{5,3},{6,0},{7,1},{8,14},{9,15},{10,... | collective-permute-start | bytes 221192 | tf_op jit(solution)/shard_map/ppermute | solution.py:606
  135.6 1.9 %collective-permute-start.25 = (bf16[96,384]{1,0:T(8,128)(2,1)S(1)}, bf16[96,384]{1,0:T(8,128)(2,1)S(1)}, u32[]{:S(2)}, u32[]{:S(2)}) collective-permute-start(bf16[96,384]{1,0:T(8,128)(2,1)S(1)} %spatial_pair.1.refs_4_.refs_0_), channel_id=1, source_target_pairs={{0,2},{1,3},{2,0},{3,1},{4,6},{5,7},{6,4},{7,5},{8,10},{9,11},{10,... | collective-permute-start | bytes 221192 | tf_op jit(solution)/shard_map/ppermute | solution.py:606
  137.6 1.9 %finish_g.1 = (f32[64,384]{1,0:T(8,128)}, f32[384]{0:T(512)}, f32[384]{0:T(512)}, f32[384]{0:T(512)}, f32[384]{0:T(512)}, /*index=5*/f32[8,512]{1,0:T(8,128)S(1)}) custom-call(s32[24]{0:T(128)S(1)} %concatenate.3.info_ref, f32[96,384]{1,0:T(8,128)S(1)} %get-tuple-element.136.refs_0_, bf16[96,384]{1,0:T(8,128)(2,1)S(1)} %collective-permute-done.27.refs_1_, ...), custom_call_target="tpu_custom_call" | custom-call | flops 1100000000 | bytes 3300000 | tf_op jit(solution)/shard_map/finish_g/pallas_call | solution.py:104
  139.5 1.2 collective-permute-done.28.refs_5_
  140.7 1.3 collective-permute-done.24.refs_1_
  141.9 1.4 %spatial_sum.1 = (f32[324,324]{1,0:T(8,128)}, f32[324]{0:T(512)}, f32[512]{0:T(512)}, f32[512]{0:T(512)}, f32[512]{0:T(512)}) custom-call(s32[24]{0:T(128)S(1)} %concatenate.3.info_ref, bf16[96,384]{1,0:T(8,128)(2,1)S(1)} %spatial_pair.1.refs_4_.refs_0_, bf16[96,384]{1,0:T(8,128)(2,1)S(1)} %collective-permute-done.24.refs_1_, ...), custom_call_target="tpu_custom_call" | custom-call | flops 1100000000 | bytes 3300000 | tf_op jit(solution)/shard_map/spatial_sum/pallas_call | solution.py:104
  (38 shorter events, 5.1 us)
Async XLA Ops:
  3.0 10.1 %collective-permute-start.5 = (bf16[64,384]{1,0:T(8,128)(2,1)S(1)}, bf16[64,384]{1,0:T(8,128)(2,1)S(1)}, u32[]{:S(2)}, u32[]{:S(2)}) collective-permute-start(bf16[64,384]{1,0:T(8,128)(2,1)S(1)} %get-tuple-element.83.refs_0_), channel_id=1, source_target_pairs={{0,24},{1,25},{2,26},{3,27},{4,28},{5,29},{6,30},{7,31},{8,0},{9,1... | collective-permute-start | bytes 147464 | tf_op jit(solution)/shard_map/ppermute | solution.py:606
  8.1 5.6 %collective-permute-start.4 = (bf16[64,384]{1,0:T(8,128)(2,1)S(1)}, bf16[64,384]{1,0:T(8,128)(2,1)S(1)}, u32[]{:S(2)}, u32[]{:S(2)}) collective-permute-start(bf16[64,384]{1,0:T(8,128)(2,1)S(1)} %get-tuple-element.83.refs_0_), channel_id=1, source_target_pairs={{0,16},{1,17},{2,18},{3,19},{4,20},{5,21},{6,22},{7,23},{8,24},{9,... | collective-permute-start | bytes 147464 | tf_op jit(solution)/shard_map/ppermute | solution.py:606
  8.1 6.6 %collective-permute-start.3 = (bf16[64,384]{1,0:T(8,128)(2,1)S(1)}, bf16[64,384]{1,0:T(8,128)(2,1)S(1)}, u32[]{:S(2)}, u32[]{:S(2)}) collective-permute-start(bf16[64,384]{1,0:T(8,128)(2,1)S(1)} %get-tuple-element.83.refs_0_), channel_id=1, source_target_pairs={{0,8},{1,9},{2,10},{3,11},{4,12},{5,13},{6,14},{7,15},{8,16},{9,17... | collective-permute-start | bytes 147464 | tf_op jit(solution)/shard_map/ppermute | solution.py:606
  9.1 9.4 %collective-permute-start.2 = (bf16[64,768]{1,0:T(8,128)(2,1)S(1)}, bf16[64,768]{1,0:T(8,128)(2,1)S(1)}, u32[]{:S(2)}, u32[]{:S(2)}) collective-permute-start(bf16[64,768]{1,0:T(8,128)(2,1)S(1)} %get-tuple-element.82.refs_0_), channel_id=1, source_target_pairs={{0,24},{1,25},{2,26},{3,27},{4,28},{5,29},{6,30},{7,31},{8,0},{9,1... | collective-permute-start | bytes 294920 | tf_op jit(solution)/shard_map/ppermute | solution.py:606
  12.0 12.9 %collective-permute-start.1 = (bf16[64,768]{1,0:T(8,128)(2,1)S(1)}, bf16[64,768]{1,0:T(8,128)(2,1)S(1)}, u32[]{:S(2)}, u32[]{:S(2)}) collective-permute-start(bf16[64,768]{1,0:T(8,128)(2,1)S(1)} %get-tuple-element.82.refs_0_), channel_id=1, source_target_pairs={{0,16},{1,17},{2,18},{3,19},{4,20},{5,21},{6,22},{7,23},{8,24},{9,... | collective-permute-start | bytes 294920 | tf_op jit(solution)/shard_map/ppermute | solution.py:606
  13.1 11.8 %collective-permute-start = (bf16[64,768]{1,0:T(8,128)(2,1)S(1)}, bf16[64,768]{1,0:T(8,128)(2,1)S(1)}, u32[]{:S(2)}, u32[]{:S(2)}) collective-permute-start(bf16[64,768]{1,0:T(8,128)(2,1)S(1)} %get-tuple-element.82.refs_0_), channel_id=1, source_target_pairs={{0,8},{1,9},{2,10},{3,11},{4,12},{5,13},{6,14},{7,15},{8,16},{9,17... | collective-permute-start | bytes 294920 | tf_op jit(solution)/shard_map/ppermute | solution.py:606
  15.6 12.0 %collective-permute-start.8 = (bf16[272,384]{1,0:T(8,128)(2,1)S(1)}, bf16[272,384]{1,0:T(8,128)(2,1)S(1)}, u32[]{:S(2)}, u32[]{:S(2)}) collective-permute-start(bf16[272,384]{1,0:T(8,128)(2,1)S(1)} %line_gate.1.refs_4_.refs_0_), channel_id=1, source_target_pairs={{0,6},{1,7},{2,4},{3,5},{4,2},{5,3},{6,0},{7,1},{8,14},{9,15},{10,... | collective-permute-start | bytes 626696 | tf_op jit(solution)/shard_map/ppermute | solution.py:606
  18.1 9.5 %collective-permute-start.7 = (bf16[272,384]{1,0:T(8,128)(2,1)S(1)}, bf16[272,384]{1,0:T(8,128)(2,1)S(1)}, u32[]{:S(2)}, u32[]{:S(2)}) collective-permute-start(bf16[272,384]{1,0:T(8,128)(2,1)S(1)} %line_gate.1.refs_4_.refs_0_), channel_id=1, source_target_pairs={{0,2},{1,3},{2,0},{3,1},{4,6},{5,7},{6,4},{7,5},{8,10},{9,11},{10,... | collective-permute-start | bytes 626696 | tf_op jit(solution)/shard_map/ppermute | solution.py:606
  18.6 9.0 %collective-permute-start.6 = (bf16[272,384]{1,0:T(8,128)(2,1)S(1)}, bf16[272,384]{1,0:T(8,128)(2,1)S(1)}, u32[]{:S(2)}, u32[]{:S(2)}) collective-permute-start(bf16[272,384]{1,0:T(8,128)(2,1)S(1)} %line_gate.1.refs_4_.refs_0_), channel_id=1, source_target_pairs={{0,4},{1,5},{2,6},{3,7},{4,0},{5,1},{6,2},{7,3},{8,12},{9,13},{10,... | collective-permute-start | bytes 626696 | tf_op jit(solution)/shard_map/ppermute | solution.py:606
  28.5 4.7 %collective-permute-start.12 = (bf16[528,768]{1,0:T(8,128)(2,1)S(1)}, bf16[528,768]{1,0:T(8,128)(2,1)S(1)}, u32[]{:S(2)}, u32[]{:S(2)}) collective-permute-start(bf16[528,768]{1,0:T(8,128)(2,1)S(1)} %assemble_gate.1.refs_4_.refs_0_.refs_8_.refs_7_), channel_id=1, source_target_pairs={{0,1},{1,0},{2,3},{3,2},{4,5},{5,4},{6,7},{7,6},{8,9},{9,8},{10,11... | collective-permute-start | bytes 2433032 | tf_op jit(solution)/shard_map/ppermute | solution.py:606
  29.6 15.8 %collective-permute-start.11 = (bf16[256,768]{1,0:T(8,128)(2,1)S(1)}, bf16[256,768]{1,0:T(8,128)(2,1)S(1)}, u32[]{:S(2)}, u32[]{:S(2)}) collective-permute-start(bf16[256,768]{1,0:T(8,128)(2,1)S(1)} %line_value_out.1.refs_5_.refs_0_), channel_id=1, source_target_pairs={{0,6},{1,7},{2,4},{3,5},{4,2},{5,3},{6,0},{7,1},{8,14},{9,15},{10,... | collective-permute-start | bytes 1179656 | tf_op jit(solution)/shard_map/ppermute | solution.py:606
  32.1 18.4 %collective-permute-start.10 = (bf16[256,768]{1,0:T(8,128)(2,1)S(1)}, bf16[256,768]{1,0:T(8,128)(2,1)S(1)}, u32[]{:S(2)}, u32[]{:S(2)}) collective-permute-start(bf16[256,768]{1,0:T(8,128)(2,1)S(1)} %line_value_out.1.refs_5_.refs_0_), channel_id=1, source_target_pairs={{0,2},{1,3},{2,0},{3,1},{4,6},{5,7},{6,4},{7,5},{8,10},{9,11},{10,... | collective-permute-start | bytes 1179656 | tf_op jit(solution)/shard_map/ppermute | solution.py:606
  32.7 18.0 %collective-permute-start.9 = (bf16[256,768]{1,0:T(8,128)(2,1)S(1)}, bf16[256,768]{1,0:T(8,128)(2,1)S(1)}, u32[]{:S(2)}, u32[]{:S(2)}) collective-permute-start(bf16[256,768]{1,0:T(8,128)(2,1)S(1)} %line_value_out.1.refs_5_.refs_0_), channel_id=1, source_target_pairs={{0,4},{1,5},{2,6},{3,7},{4,0},{5,1},{6,2},{7,3},{8,12},{9,13},{10,... | collective-permute-start | bytes 1179656 | tf_op jit(solution)/shard_map/ppermute | solution.py:606
  51.8 3.5 %collective-permute-start.13 = (bf16[512,1536]{1,0:T(8,128)(2,1)S(1)}, bf16[512,1536]{1,0:T(8,128)(2,1)S(1)}, u32[]{:S(2)}, u32[]{:S(2)}) collective-permute-start(bf16[512,1536]{1,0:T(8,128)(2,1)S(1)} %assemble_value_out.1.refs_0_.refs_1_.refs_3_.refs_5_), channel_id=1, source_target_pairs={{0,1},{1,0},{2,3},{3,2},{4,5},{5,4},{6,7},{7,6},{8,9},{9,8},{10,11... | collective-permute-start | bytes 4718600 | tf_op jit(solution)/shard_map/ppermute | solution.py:606
  65.2 10.3 %collective-permute-start.14 = (bf16[1024,768]{1,0:T(8,128)(2,1)S(1)}, bf16[1024,768]{1,0:T(8,128)(2,1)S(1)}, u32[]{:S(2)}, u32[]{:S(2)}) collective-permute-start(bf16[1024,768]{1,0:T(8,128)(2,1)S(1)} %get-tuple-element.108), channel_id=1, source_target_pairs={{0,1},{1,0},{2,3},{3,2},{4,5},{5,4},{6,7},{7,6},{8,9},{9,8},{10,11... | collective-permute-start | bytes 4718600 | tf_op jit(solution)/shard_map/ppermute | solution.py:606
  76.5 13.6 %collective-permute-start.16 = (bf16[2,608,384]{2,1,0:T(8,128)(2,1)S(1)}, bf16[2,608,384]{2,1,0:T(8,128)(2,1)S(1)}, u32[]{:S(2)}, u32[]{:S(2)}) collective-permute-start(bf16[2,608,384]{2,1,0:T(8,128)(2,1)S(1)} %get-tuple-element.110.refs_15_), channel_id=1, source_target_pairs={{0,2},{1,5},{2,0},{3,7},{4,6},{5,1},{6,4},{7,3},{8,10},{9,13},{10,... | collective-permute-start | bytes 2801672 | tf_op jit(solution)/shard_map/ppermute | solution.py:606
  88.5 3.9 %collective-permute-start.15 = (bf16[528,768]{1,0:T(8,128)(2,1)S(1)}, bf16[528,768]{1,0:T(8,128)(2,1)S(1)}, u32[]{:S(2)}, u32[]{:S(2)}) collective-permute-start(bf16[528,768]{1,0:T(8,128)(2,1)S(1)} %get-tuple-element.112), channel_id=1, source_target_pairs={{0,1},{1,0},{2,3},{3,2},{4,5},{5,4},{6,7},{7,6},{8,9},{9,8},{10,11... | collective-permute-start | bytes 2433032 | tf_op jit(solution)/shard_map/ppermute | solution.py:606
  90.9 13.2 %collective-permute-start.18 = (bf16[608,384]{1,0:T(8,128)(2,1)S(1)}, bf16[608,384]{1,0:T(8,128)(2,1)S(1)}, u32[]{:S(2)}, u32[]{:S(2)}) collective-permute-start(bf16[608,384]{1,0:T(8,128)(2,1)S(1)} %get-tuple-element.115.refs_3_), channel_id=1, source_target_pairs={{0,4},{1,3},{2,6},{3,1},{4,0},{5,7},{6,2},{7,5},{8,12},{9,11},{10,... | collective-permute-start | bytes 1400840 | tf_op jit(solution)/shard_map/ppermute | solution.py:606
  93.2 11.6 %collective-permute-start.17 = (bf16[2,288,384]{2,1,0:T(8,128)(2,1)S(1)}, bf16[2,288,384]{2,1,0:T(8,128)(2,1)S(1)}, u32[]{:S(2)}, u32[]{:S(2)}) collective-permute-start(bf16[2,288,384]{2,1,0:T(8,128)(2,1)S(1)} %get-tuple-element.116.refs_6_), channel_id=1, source_target_pairs={{0,2},{1,5},{2,0},{3,7},{4,6},{5,1},{6,4},{7,3},{8,10},{9,13},{10,... | collective-permute-start | bytes 1327112 | tf_op jit(solution)/shard_map/ppermute | solution.py:606
  105.4 16.8 %collective-permute-start.20 = (bf16[288,384]{1,0:T(8,128)(2,1)S(1)}, bf16[288,384]{1,0:T(8,128)(2,1)S(1)}, u32[]{:S(2)}, u32[]{:S(2)}) collective-permute-start(bf16[288,384]{1,0:T(8,128)(2,1)S(1)} %get-tuple-element.125.refs_10_), channel_id=1, source_target_pairs={{0,4},{1,3},{2,6},{3,1},{4,0},{5,7},{6,2},{7,5},{8,12},{9,11},{10,... | collective-permute-start | bytes 663560 | tf_op jit(solution)/shard_map/ppermute | solution.py:606
  106.9 15.9 %collective-permute-start.19 = (bf16[352,384]{1,0:T(8,128)(2,1)S(1)}, bf16[352,384]{1,0:T(8,128)(2,1)S(1)}, u32[]{:S(2)}, u32[]{:S(2)}) collective-permute-start(bf16[352,384]{1,0:T(8,128)(2,1)S(1)} %get-tuple-element.124.refs_2_), channel_id=1, source_target_pairs={{0,16},{1,17},{2,18},{3,19},{4,20},{5,21},{6,22},{7,23},{8,24},{9,... | collective-permute-start | bytes 811016 | tf_op jit(solution)/shard_map/ppermute | solution.py:606
  122.7 6.0 %collective-permute-start.22 = (bf16[160,384]{1,0:T(8,128)(2,1)S(1)}, bf16[160,384]{1,0:T(8,128)(2,1)S(1)}, u32[]{:S(2)}, u32[]{:S(2)}) collective-permute-start(bf16[160,384]{1,0:T(8,128)(2,1)S(1)} %get-tuple-element.130.refs_2_), channel_id=1, source_target_pairs={{0,16},{1,17},{2,18},{3,19},{4,20},{5,21},{6,22},{7,23},{8,24},{9,... | collective-permute-start | bytes 368648 | tf_op jit(solution)/shard_map/ppermute | solution.py:606
  123.5 7.2 %collective-permute-start.21 = (bf16[224,384]{1,0:T(8,128)(2,1)S(1)}, bf16[224,384]{1,0:T(8,128)(2,1)S(1)}, u32[]{:S(2)}, u32[]{:S(2)}) collective-permute-start(bf16[224,384]{1,0:T(8,128)(2,1)S(1)} %get-tuple-element.132.refs_2_), channel_id=1, source_target_pairs={{0,8},{1,9},{2,10},{3,11},{4,12},{5,13},{6,14},{7,15},{8,0},{9,1},... | collective-permute-start | bytes 516104 | tf_op jit(solution)/shard_map/ppermute | solution.py:606
  131.9 1.3 collective-permute-start.23
  131.9 5.7 %collective-permute-start.27 = (bf16[96,384]{1,0:T(8,128)(2,1)S(1)}, bf16[96,384]{1,0:T(8,128)(2,1)S(1)}, u32[]{:S(2)}, u32[]{:S(2)}) collective-permute-start(bf16[96,384]{1,0:T(8,128)(2,1)S(1)} %get-tuple-element.134.refs_2_), channel_id=1, source_target_pairs={{0,8},{1,9},{2,10},{3,11},{4,12},{5,13},{6,14},{7,15},{8,0},{9,1},... | collective-permute-start | bytes 221192 | tf_op jit(solution)/shard_map/ppermute | solution.py:606
  133.7 6.9 %collective-permute-start.26 = (bf16[96,384]{1,0:T(8,128)(2,1)S(1)}, bf16[96,384]{1,0:T(8,128)(2,1)S(1)}, u32[]{:S(2)}, u32[]{:S(2)}) collective-permute-start(bf16[96,384]{1,0:T(8,128)(2,1)S(1)} %spatial_pair.1.refs_4_.refs_0_), channel_id=1, source_target_pairs={{0,6},{1,7},{2,4},{3,5},{4,2},{5,3},{6,0},{7,1},{8,14},{9,15},{10,... | collective-permute-start | bytes 221192 | tf_op jit(solution)/shard_map/ppermute | solution.py:606
  135.6 5.0 %collective-permute-start.25 = (bf16[96,384]{1,0:T(8,128)(2,1)S(1)}, bf16[96,384]{1,0:T(8,128)(2,1)S(1)}, u32[]{:S(2)}, u32[]{:S(2)}) collective-permute-start(bf16[96,384]{1,0:T(8,128)(2,1)S(1)} %spatial_pair.1.refs_4_.refs_0_), channel_id=1, source_target_pairs={{0,2},{1,3},{2,0},{3,1},{4,6},{5,7},{6,4},{7,5},{8,10},{9,11},{10,... | collective-permute-start | bytes 221192 | tf_op jit(solution)/shard_map/ppermute | solution.py:606
  137.6 4.4 %collective-permute-start.24 = (bf16[96,384]{1,0:T(8,128)(2,1)S(1)}, bf16[96,384]{1,0:T(8,128)(2,1)S(1)}, u32[]{:S(2)}, u32[]{:S(2)}) collective-permute-start(bf16[96,384]{1,0:T(8,128)(2,1)S(1)} %spatial_pair.1.refs_4_.refs_0_), channel_id=1, source_target_pairs={{0,4},{1,5},{2,6},{3,7},{4,0},{5,1},{6,2},{7,3},{8,12},{9,13},{10,... | collective-permute-start | bytes 221192 | tf_op jit(solution)/shard_map/ppermute | solution.py:606
  139.5 1.2 collective-permute-start.28
